TPU v7x, 256 devices: a whole 4x4x8 slice. The times are simulated.
256 devices in a mesh: dp: 16 (over z, core), row: 4 (over y), col: 4 (over x).
Axes of the slice: x: 4, y: 4, z: 8, core: 2. Of those that a mesh axis runs over, the one named last changes fastest.
Arguments:
- flat_iterate: bfloat16 [256, 270336], P(('dp', 'row', 'col')), as said below
- lengths: int32 [16, 16], replicated, may hold values from 1 to 270336, 2883584 in all within a row
Outputs:
- new_flat: bfloat16 [256, 270336], P(('dp', 'row', 'col'))
Inputs may be any that keep to these rules, and one draw needn't show every extreme that they name: Every row of lengths sums to 2883584, and its largest entry is 270336. `flat_iterate`: slots at or past a shard's length belong to no group.
All inputs are finite; a program needn't handle non-finite values.
Results may differ from a plain program's by a relative error of at most 0.02.
Values may be sent and summed in bfloat16 or wider, within the bound.
A program may use at most 64 MiB of HBM per device.

v0:
```python
import math

import jax
import jax.numpy as jnp
from jax import lax
from jax.sharding import PartitionSpec as P

COLS = 8192
ROWS = 5632


LINEAR_COEF = 3.4445
CUBIC_COEF = -4.775
QUINTIC_COEF = 2.0315


def reduce_whole(partial_value):
    return lax.psum(partial_value.astype(jnp.bfloat16), "dp").astype(jnp.float32)


def local(flat_iterate, lengths):
    dp_count = lax.axis_size("dp")
    row_count = lax.axis_size("row")
    col_count = lax.axis_size("col")
    groups = row_count * col_count
    dp_index = lax.axis_index("dp")
    group_index = lax.axis_index("row") * col_count + lax.axis_index("col")
    capacity = flat_iterate.shape[1]
    span_rows = (capacity + COLS - 1) // COLS + 1
    group_rows = ROWS // groups
    slab_width = COLS // dp_count
    share_width = ROWS // dp_count
    shard_ends = jnp.cumsum(lengths, axis=1)
    starts = shard_ends - lengths
    own_starts = lax.dynamic_index_in_dim(starts, group_index, 0, keepdims=False)
    own_lengths = lax.dynamic_index_in_dim(lengths, group_index, 0, keepdims=False)
    first_rows = own_starts // COLS
    my_start = lax.dynamic_index_in_dim(own_starts, dp_index, 0, keepdims=False)
    my_length = lax.dynamic_index_in_dim(own_lengths, dp_index, 0, keepdims=False)
    lead_cols = my_start - my_start // COLS * COLS
    places = jnp.arange(capacity, dtype=jnp.int32)
    segment = jnp.where(places < my_length, flat_iterate[0], jnp.zeros((), jnp.bfloat16))
    canvas = lax.dynamic_update_slice(
        jnp.zeros((span_rows * COLS,), jnp.bfloat16), segment, (lead_cols,)
    )
    canvas = canvas.reshape(span_rows, COLS)
    arrived = lax.all_to_all(canvas, "dp", split_axis=1, concat_axis=0, tiled=True)
    targets = (first_rows[:, None] + jnp.arange(span_rows, dtype=jnp.int32)[None, :]).reshape(-1)
    landing = jnp.zeros((group_rows + span_rows, slab_width), jnp.float32)
    landing = landing.at[targets].add(arrived.astype(jnp.float32))
    own_block = landing[:group_rows].astype(jnp.bfloat16)
    slab_all = lax.all_gather(own_block, ("row", "col"), axis=0, tiled=True)
    partial_value = lax.dot_general(
        own_block, slab_all, (((1,), (1,)), ((), ())), preferred_element_type=jnp.float32
    )
    gram_rows = reduce_whole(partial_value).astype(jnp.bfloat16)
    gram_share = lax.dynamic_slice_in_dim(gram_rows, dp_index * share_width, share_width, 1)
    square_part = lax.dot_general(
        gram_share,
        lax.all_gather(gram_share, ("row", "col"), axis=0, tiled=True),
        (((1,), (1,)), ((), ())),
        preferred_element_type=jnp.float32,
    )
    square_rows = reduce_whole(square_part)
    poly_rows = (CUBIC_COEF * gram_rows.astype(jnp.float32) + QUINTIC_COEF * square_rows).astype(
        jnp.bfloat16
    )
    product = jnp.dot(poly_rows, slab_all, preferred_element_type=jnp.float32)
    scale_factor = 0.2 * math.sqrt(max(ROWS, COLS))
    update = (scale_factor * (LINEAR_COEF * own_block.astype(jnp.float32) + product)).astype(
        jnp.bfloat16
    )
    padded = jnp.concatenate([update, jnp.zeros((span_rows, slab_width), jnp.bfloat16)], axis=0)
    outgoing = jnp.take(padded, targets, axis=0)
    returned = lax.all_to_all(outgoing, "dp", split_axis=0, concat_axis=1, tiled=True)
    flat_back = lax.dynamic_slice_in_dim(returned.reshape(-1), lead_cols, capacity)
    flat_back = jnp.where(places < my_length, flat_back, jnp.zeros((), jnp.bfloat16))
    return flat_back[None, :]


def solution(mesh):
    return jax.shard_map(
        local,
        mesh=mesh,
        in_specs=(P(("dp", "row", "col"), None), P()),
        out_specs=P(("dp", "row", "col"), None),
        check_vma=False,
    )
```

profile of v0, /device:TPU:1, one launch (start us, length us, event | category | flops | bytes accessed | tf_op | source)
XLA Modules:
  0.0 493.6 jit_solution(8810949176157260889)
XLA Ops:
  6.5 0.9 reduce_window_sum.11
  7.4 0.7 sub.14
  8.1 0.6 dynamic_slice.20
  10.6 1.3 dynamic_slice.18
  13.3 12.2 %reduce.1 = bf16[270336]{0:T(1024)(128)(2,1)S(1)} reduce(bf16[1,270336]{1,0:T(2,128)(2,1)} %param.2, bf16[]{:T(256)} %constant.121), dimensions={0}, to_apply=%param.2.reduce_sub_computation | reduce | bytes 1081346 | tf_op args[0]
  25.5 0.8 fusion.7
  26.4 5.0 %dynamic_update_slice.3 = bf16[278528]{0:T(1024)(128)(2,1)S(1)} dynamic-update-slice(bf16[278528]{0:T(1024)(128)(2,1)S(1)} %broadcast_in_dim.30, bf16[270336]{0:T(1024)(128)(2,1)S(1)} %fusion.7, s32[]{:T(128)S(6)} %select_n.74) | dynamic-update-slice | bytes 1081348 | tf_op jit(solution)/shard_map/dynamic_update_slice | solution.py:43
  31.4 0.3 all_to_all.20
  31.7 1.1 copy.5
  32.8 10.0 %all-to-all-start = ((bf16[34,16,512]{2,0,1:T(8,128)(2,1)}), bf16[34,16,512]{2,0,1:T(8,128)(2,1)S(1)}, u32[]{:S(2)}, u32[]{:S(2)}) async-start(bf16[34,16,512]{2,0,1:T(8,128)(2,1)} %copy.5), calls=%async_computation | async-start | bytes 1310720 | tf_op jit(solution)/shard_map/all_to_all | solution.py:47
  43.1 19.8 %all-to-all-done = bf16[34,16,512]{2,0,1:T(8,128)(2,1)S(1)} async-done(((bf16[34,16,512]{2,0,1:T(8,128)(2,1)}), bf16[34,16,512]{2,0,1:T(8,128)(2,1)S(1)}, u32[]{:S(2)}, u32[]{:S(2)}) %all-to-all-start) | async-done | bytes 557088 | tf_op jit(solution)/shard_map/all_to_all | solution.py:47
  62.9 0.2 convert_bitcast_fusion
  63.0 0.1 reshape.103
  63.2 6.8 %scatter_custom_fusion = f32[386,512]{1,0:T(8,128)S(1)} fusion(s32[544]{0:T(1024)S(1)} %fusion.10, f32[544,512]{1,0:T(8,128)S(1)} %reshape.103, f32[]{:T(128)} %constant.106.clone.1), kind=kCustom, calls=%fused_computation.17 | custom fusion | flops 278528 | bytes 790532 | tf_op jit(solution)/shard_map/scatter-add | solution.py:50
  69.9 0.8 slice.9
  70.8 60.8 %all-gather.3.cloned.1.call-done = bf16[5632,512]{1,0:T(8,128)(2,1)} async-done(((bf16[352,512]{1,0:T(8,128)(2,1)}), bf16[5632,512]{1,0:T(8,128)(2,1)}) %all-gather.3.cloned.1.call-update) | async-done | bytes 5767184 | tf_op jit(solution)/shard_map/all_gather | solution.py:52
  131.6 6.8 %convolution_convert_fusion.1 = bf16[352,5632]{1,0:T(8,128)(2,1)} fusion(bf16[5632,512]{1,0:T(8,128)(2,1)} %all-gather.3.cloned.1.call-done, f32[386,512]{1,0:T(8,128)S(1)} %scatter_custom_fusion), kind=kOutput, calls=%fused_computation.3 | convolution fusion | flops 2032025600 | bytes 10092544 | tf_op jit(solution)/shard_map/dot_general | solution.py:53
  138.6 120.3 %all-reduce.4.cloned.1.call-done = bf16[352,5632]{1,0:T(8,128)(2,1)} async-done(((bf16[352,5632]{1,0:T(8,128)(2,1)}), bf16[352,5632]{1,0:T(8,128)(2,1)}) %all-reduce.4.cloned.1.call-update) | async-done | bytes 3964944 | tf_op jit(solution)/shard_map/psum | solution.py:18
  258.9 1.8 constant_dynamic-slice_fusion
  260.7 0.2 all-reduce.6.cloned.1.call-start
  261.0 58.5 %all-gather.5.cloned.1.call-done = bf16[5632,352]{1,0:T(8,128)(2,1)} async-done(((bf16[352,352]{1,0:T(8,128)(2,1)}), bf16[5632,352]{1,0:T(8,128)(2,1)}) %all-gather.5.cloned.1.call-update) | async-done | bytes 3964944 | tf_op jit(solution)/shard_map/all_gather | solution.py:60
  319.5 6.4 %convolution_convert_fusion = bf16[352,5632]{1,0:T(8,128)(2,1)} fusion(bf16[352,352]{1,0:T(8,128)(2,1)} %constant_dynamic-slice_fusion, bf16[5632,352]{1,0:T(8,128)(2,1)} %all-gather.5.cloned.1.call-done), kind=kOutput, calls=%fused_computation.2 | convolution fusion | flops 1397637120 | bytes 8177664 | tf_op jit(solution)/shard_map/dot_general | solution.py:58
  326.0 120.4 %all-reduce.6.cloned.1.call-done = bf16[352,5632]{1,0:T(8,128)(2,1)} async-done(((bf16[352,5632]{1,0:T(8,128)(2,1)}), bf16[352,5632]{1,0:T(8,128)(2,1)}) %all-reduce.6.cloned.1.call-update) | async-done | bytes 3964944 | tf_op jit(solution)/shard_map/psum | solution.py:18
  446.4 7.2 %fusion.5 = bf16[352,512]{1,0:T(8,128)(2,1)S(1)} fusion(bf16[5632,512]{1,0:T(8,128)(2,1)} %all-gather.3.cloned.1.call-done, bf16[352,5632]{1,0:T(8,128)(2,1)} %all-reduce.6.cloned.1.call-done, bf16[352,5632]{1,0:T(8,128)(2,1)} %all-reduce.4.cloned.1.call-done, f32[386,512]{1,0:T(8,128)S(1)} %scatter_custom_fusion), kind=kOutput, calls=%fused_computation.11 | convolution fusion | flops 2042839040 | bytes 14417920 | tf_op jit(solution)/shard_map/dot_general | solution.py:68
  453.7 2.7 gather_fusion
  456.4 0.2 gather.7
  456.6 0.2 broadcast_select_fusion
  456.7 27.0 %all_to_all.26 = bf16[16,34,512]{2,1,0:T(8,128)(2,1)S(1)} all-to-all(bf16[16,34,512]{2,1,0:T(8,128)(2,1)S(1)} %broadcast_select_fusion), channel_id=1, replica_groups=mesh['dp'=16,'row'=4,'col'=4] {'dp'}, dimensions={0} | all-to-all | bytes 1114112 | tf_op jit(solution)/shard_map/all_to_all | solution.py:75
  483.7 0.2 copy.6
  483.9 0.2 copy.7
  484.1 1.1 fusion.6
  485.2 1.9 broadcast_in_dim.33
  (15 shorter events, 0.5 us)
Async XLA Ops:
  32.8 30.0 %all-to-all-start = ((bf16[34,16,512]{2,0,1:T(8,128)(2,1)}), bf16[34,16,512]{2,0,1:T(8,128)(2,1)S(1)}, u32[]{:S(2)}, u32[]{:S(2)}) async-start(bf16[34,16,512]{2,0,1:T(8,128)(2,1)} %copy.5), calls=%async_computation | async-start | bytes 1310720 | tf_op jit(solution)/shard_map/all_to_all | solution.py:47
  42.8 88.8 %all-gather.3.cloned.1.call-start = ((), (), s32[]{:S(2)}) async-start(), calls=%async_computation.2 | async-start | bytes 6127616 | tf_op jit(solution)/shard_map/all_gather | solution.py:52
  70.7 188.1 %all-reduce.4.cloned.1.call-start = ((), (), s32[]{:S(2)}) async-start(), calls=%async_computation.3 | async-start | bytes 7929856 | tf_op jit(solution)/shard_map/psum | solution.py:18
  138.5 181.0 %all-gather.5.cloned.1.call-start = ((), (), s32[]{:S(2)}) async-start(), calls=%async_computation.4 | async-start | bytes 4595712 | tf_op jit(solution)/shard_map/all_gather | solution.py:60
  260.7 185.7 %all-reduce.6.cloned.1.call-start = ((), (), s32[]{:S(2)}) async-start(), calls=%async_computation.5 | async-start | bytes 7929856 | tf_op jit(solution)/shard_map/psum | solution.py:18
Sparse Core Ops, SparseCore 0:
  70.9 60.7 all-gather.2
  138.6 120.2 all-reduce.3
  261.6 57.8 all-gather.4
  326.1 120.3 all-reduce.5
where the time goes:
time: 494 us
  waiting for transfers between devices  380 us (77%)
  blocking collectives  27 us (5%)
  other arithmetic  22.9 us (5%)
  matrix products  20.5 us (4%)
  between operations  16.6 us (3%)
  local copies, waits for them, and re-layouts  16.4 us (3%)
  starting transfers between devices  10.3 us (2%)
    psum x2, waiting for transfers between devices, reduce_whole(): lax.psum(partial_value.astype(jnp.bfloat16), 'dp').astype(jnp.float32)  241 us
    all_gather x1, waiting for transfers between devices, local(): slab_all = lax.all_gather(own_block, ('row', 'col'), axis=0, tiled=True)  60.8 us
    all_gather x1, waiting for transfers between devices, local(): lax.all_gather(gram_share, ('row', 'col'), axis=0, tiled=True)  58.5 us
    all_to_all x1, blocking collectives, local(): lax.all_to_all(outgoing, 'dp', split_axis=0, concat_axis=1, tiled=True)  27 us
    all_to_all x1, waiting for transfers between devices, local(): lax.all_to_all(canvas, 'dp', split_axis=1, concat_axis=0, tiled=True)  19.8 us
    unnamed x1, other arithmetic  12.2 us
    all_to_all x1, starting transfers between devices, local(): lax.all_to_all(canvas, 'dp', split_axis=1, concat_axis=0, tiled=True)  9.99 us
  transfers between devices with their start and end apart: 5, of which 5 were waited for; matrix products, arithmetic and copies ran while one was open for 0% of the time, Pallas kernels for 0%

commit v1 on v0

v1 whole, which is shorter than its diff:
```python
import math

import jax
import jax.numpy as jnp
from jax import lax
from jax.experimental import pallas as pl
from jax.experimental.pallas import tpu as pltpu
from jax.sharding import PartitionSpec as P

COLS = 8192
ROWS = 5632


LINEAR_COEF = 3.4445
CUBIC_COEF = -4.775
QUINTIC_COEF = 2.0315

N_DP = 16
N_Z = 8
RING = 4
GROUP_ROWS = 352
HALF_ROWS = 176
SLAB = 512
BLOCK = 1408
CORE_ROWS = 704
SHARD = 96
HALF_SHARD = 48
FWD = 768
N_MESSAGES = 96
MESH = pl.DeviceIdType.MESH
SCALE = 0.2 * math.sqrt(max(ROWS, COLS))


def core_kernel(
    x_ref, out_ref, xr, xs, own_f32, to_sib, from_sib, gh, ring_f, ring_b, g_full,
    part, got_a, got_b, got_c, got_d, y_f32, ya, yb, part2, z_b, send_sem, recv_sem,
):
    dp = lax.axis_index("dp")
    y = lax.axis_index("row")
    x = lax.axis_index("col")
    z, c = dp // 2, dp % 2
    sib_dp = z * 2 + 1 - c
    up_dp = ((z + 1) % N_Z) * 2 + c
    down_dp = ((z + 7) % N_Z) * 2 + c
    dev_sib = (sib_dp, y, x)
    dev_up = (up_dp, y, x)
    dev_down = (down_dp, y, x)
    near = {
        "col": ((dp, y, (x + 1) % RING), (dp, y, (x + 3) % RING)),
        "row": ((dp, (y + 1) % RING, x), (dp, (y + 3) % RING, x)),
    }
    place = {"col": x, "row": y}

    barrier = pltpu.get_barrier_semaphore()
    for peer in (dev_sib, dev_up, dev_down) + near["col"] + near["row"]:
        pl.semaphore_signal(barrier, inc=1, device_id=peer, device_id_type=MESH)
    pl.semaphore_wait(barrier, 7)

    counter = [0]
    started = []

    def message(src, dst, device, slot=None):
        if slot is None:
            slot = counter[0]
            counter[0] += 1
        return pltpu.make_async_remote_copy(
            src_ref=src, dst_ref=dst, send_sem=send_sem.at[slot], recv_sem=recv_sem.at[slot],
            device_id=device, device_id_type=MESH,
        )

    def send(src, dst, device):
        copy = message(src, dst, device)
        copy.start()
        started.append(copy)
        return copy

    top, bottom = pl.ds(0, HALF_ROWS), pl.ds(HALF_ROWS, HALF_ROWS)

    def gather_start(axis, buf):
        p = place[axis]
        right, left = near[axis]
        a = [send(buf.at[p, h], buf.at[p, h], right) for h in (top, bottom)]
        b = [send(buf.at[p, h], buf.at[p, h], left) for h in (bottom, top)]
        return a, b

    def gather_pass(axis, buf, state):
        p = place[axis]
        right, left = near[axis]
        a, b = state
        before, after = (p + 3) % RING, (p + 1) % RING
        a[0].wait_recv()
        f = send(buf.at[before, top], buf.at[before, top], right)
        b[0].wait_recv()
        g = send(buf.at[after, bottom], buf.at[after, bottom], left)
        return a[1], b[1], f, g

    def gather_end(tail):
        for copy in tail:
            copy.wait_recv()

    xr[x] = x_ref[...]
    xs[y] = x_ref[...]
    s1 = gather_start("col", xr)
    s2 = gather_start("row", xs)
    t1 = gather_pass("col", xr, s1)
    t2 = gather_pass("row", xs, s2)
    gather_end(t1)
    gather_end(t2)

    base = counter[0]
    counter[0] += 4

    def sib_message(i):
        rows = pl.ds(pl.multiple_of(i * HALF_ROWS, 16), HALF_ROWS)
        return message(to_sib.at[rows], from_sib.at[rows], dev_sib, slot=base + i)

    def gram_tile(half, i):
        left = xr[2 * half + i // 2, pl.ds(pl.multiple_of((i % 2) * HALF_ROWS, 16), HALF_ROWS)]
        return lax.dot_general(
            left, xs[...].reshape(BLOCK, SLAB), (((1,), (1,)), ((), ())), preferred_element_type=jnp.float32
        )

    def sib_step(i, _):
        rows = pl.ds(pl.multiple_of(i * HALF_ROWS, 16), HALF_ROWS)
        to_sib[rows] = gram_tile(1 - c, i).astype(jnp.bfloat16)
        sib_message(i).start()
        return 0

    lax.fori_loop(0, 4, sib_step, 0)

    def own_step(i, _):
        rows = pl.ds(pl.multiple_of(i * HALF_ROWS, 16), HALF_ROWS)
        own_f32[rows] = gram_tile(c, i)
        return 0

    lax.fori_loop(0, 4, own_step, 0)
    gh[pl.ds(CORE_ROWS, N_Z * SHARD - CORE_ROWS)] = jnp.zeros((N_Z * SHARD - CORE_ROWS, BLOCK), jnp.bfloat16)

    def join_step(i, _):
        rows = pl.ds(pl.multiple_of(i * HALF_ROWS, 16), HALF_ROWS)
        sib_message(i).wait()
        gh[rows] = (own_f32[rows] + from_sib[rows].astype(jnp.float32)).astype(jnp.bfloat16)
        return 0

    lax.fori_loop(0, 4, join_step, 0)

    def shard_rows(s):
        return pl.ds(pl.multiple_of(s * SHARD, 16), SHARD)

    f_cols, b_cols = pl.ds(0, FWD), pl.ds(FWD, BLOCK - FWD)
    f_copy = b_copy = None
    for t in range(N_Z - 1):
        sf, sb = (z + 7 - t + N_Z) % N_Z, (z + 1 + t) % N_Z
        if t == 0:
            f_src, b_src = gh.at[shard_rows(sf), f_cols], gh.at[shard_rows(sb), b_cols]
        else:
            f_copy.wait_recv()
            ring_f[t - 1] = (ring_f[t - 1].astype(jnp.float32) + gh[shard_rows(sf), f_cols].astype(jnp.float32)).astype(jnp.bfloat16)
            f_src, b_src = ring_f.at[t - 1], ring_b.at[t - 1]
        f_next = send(f_src, ring_f.at[t], dev_up)
        if t > 0:
            b_copy.wait_recv()
            ring_b[t - 1] = (ring_b[t - 1].astype(jnp.float32) + gh[shard_rows(sb), b_cols].astype(jnp.float32)).astype(jnp.bfloat16)
        b_next = send(b_src, ring_b.at[t], dev_down)
        f_copy, b_copy = f_next, b_next
    mine = shard_rows(z)
    f_copy.wait_recv()
    g_full[c, mine, f_cols] = (ring_f[N_Z - 2].astype(jnp.float32) + gh[mine, f_cols].astype(jnp.float32)).astype(jnp.bfloat16)
    b_copy.wait_recv()
    g_full[c, mine, b_cols] = (ring_b[N_Z - 2].astype(jnp.float32) + gh[mine, b_cols].astype(jnp.float32)).astype(jnp.bfloat16)

    pending = []

    def relay(rows, device):
        ref = g_full.at[c, rows]
        return send(ref, ref, device)

    up = relay(mine, dev_up)
    down = relay(mine, dev_down)
    pending.append(relay(mine, dev_sib))
    for step in range(1, 4):
        before, after = shard_rows((z + N_Z - step) % N_Z), shard_rows((z + step) % N_Z)
        if step == 3:
            before_next = pl.ds(pl.multiple_of(((z + N_Z - step) % N_Z) * SHARD, 16), HALF_SHARD)
            after_next = pl.ds(pl.multiple_of(((z + step) % N_Z) * SHARD + HALF_SHARD, 16), HALF_SHARD)
        else:
            before_next, after_next = before, after
        up.wait_recv()
        up = relay(before_next, dev_up)
        pending.append(relay(before, dev_sib))
        down.wait_recv()
        down = relay(after_next, dev_down)
        pending.append(relay(after, dev_sib))
    far = ((z + 4) % N_Z) * SHARD
    up.wait_recv()
    pending.append(relay(pl.ds(pl.multiple_of(far, 16), HALF_SHARD), dev_sib))
    down.wait_recv()
    pending.append(relay(pl.ds(pl.multiple_of(far + HALF_SHARD, 16), HALF_SHARD), dev_sib))
    for copy in pending:
        copy.wait_recv()

    def reduce4(axis, buf, cols, a_ref, b_ref, c_ref, d_ref, make):
        p = place[axis]
        right, left = near[axis]
        after, before, far = (p + 1) % RING, (p + 3) % RING, (p + 2) % RING
        make(far)
        a = send(buf.at[far, top], a_ref, right)
        b = send(buf.at[far, bottom], b_ref, left)
        make(after)
        c1 = send(buf.at[after, bottom], c_ref.at[bottom], right)
        make(before)
        d1 = send(buf.at[before, top], d_ref.at[top], left)
        a.wait_recv()
        buf[after, top] = (buf[after, top].astype(jnp.float32) + a_ref[...].astype(jnp.float32)).astype(jnp.bfloat16)
        c2 = send(buf.at[after, top], c_ref.at[top], right)
        b.wait_recv()
        buf[before, bottom] = (buf[before, bottom].astype(jnp.float32) + b_ref[...].astype(jnp.float32)).astype(jnp.bfloat16)
        d2 = send(buf.at[before, bottom], d_ref.at[bottom], left)
        return (c1, d1, c2, d2)

    def g_rows(q):
        return g_full[q // 2, pl.ds(pl.multiple_of((q % 2) * GROUP_ROWS, 16), GROUP_ROWS)]

    def make_y(q):
        part[q] = jnp.dot(g_rows(q), xs[...].reshape(BLOCK, SLAB), preferred_element_type=jnp.float32).astype(jnp.bfloat16)

    tail = reduce4("col", part, SLAB, got_a, got_b, got_c, got_d, make_y)
    y_f32[...] = jnp.dot(g_rows(x), xs[...].reshape(BLOCK, SLAB), preferred_element_type=jnp.float32)
    gather_end(tail)
    y_f32[...] = y_f32[...] + got_c[...].astype(jnp.float32) + got_d[...].astype(jnp.float32)
    ya[y] = y_f32[:, : SLAB // 2].astype(jnp.bfloat16)
    yb[x] = y_f32[:, SLAB // 2 :].astype(jnp.bfloat16)
    s1 = gather_start("row", ya)
    s2 = gather_start("col", yb)
    t1 = gather_pass("row", ya, s1)
    t2 = gather_pass("col", yb, s2)
    gather_end(t1)
    gather_end(t2)

    first, second = pl.ds(0, SLAB // 2), pl.ds(SLAB // 2, SLAB // 2)

    def make_za(q):
        part2[0, q] = jnp.dot(g_rows(q), ya[...].reshape(BLOCK, SLAB // 2), preferred_element_type=jnp.float32).astype(jnp.bfloat16)

    z_b[...] = jnp.zeros_like(z_b)
    for q in range(4):
        z_b[...] += lax.dot_general(
            g_full[q // 2, pl.ds((q % 2) * GROUP_ROWS, GROUP_ROWS)], yb[q], (((0,), (0,)), ((), ())),
            preferred_element_type=jnp.float32,
        )
    part2[1] = z_b[...].astype(jnp.bfloat16).reshape(4, GROUP_ROWS, SLAB // 2)

    ta = reduce4("col", part2.at[0], None, got_a.at[:, first], got_b.at[:, first], got_c.at[:, first], got_d.at[:, first], make_za)
    tb = reduce4("row", part2.at[1], None, got_a.at[:, second], got_b.at[:, second], got_c.at[:, second], got_d.at[:, second], lambda q: None)
    za_own = jnp.dot(g_rows(x), ya[...].reshape(BLOCK, SLAB // 2), preferred_element_type=jnp.float32)
    gather_end(ta)
    gather_end(tb)
    for cols, own in ((first, za_own), (second, z_b[pl.ds(pl.multiple_of(y * GROUP_ROWS, 8), GROUP_ROWS)])):
        z_val = own + got_c[:, cols].astype(jnp.float32) + got_d[:, cols].astype(jnp.float32)
        out_ref[:, cols] = (
            SCALE * (LINEAR_COEF * x_ref[:, cols].astype(jnp.float32) + (CUBIC_COEF * y_f32[:, cols] + QUINTIC_COEF * z_val))
        ).astype(jnp.bfloat16)
    for copy in started:
        copy.wait_send()


def newton_schulz(own_block):
    bf, f32 = jnp.bfloat16, jnp.float32
    vmem = pltpu.VMEM
    return pl.pallas_call(
        core_kernel,
        out_shape=jax.ShapeDtypeStruct((GROUP_ROWS, SLAB), bf),
        in_specs=[pl.BlockSpec(memory_space=pltpu.VMEM)],
        out_specs=pl.BlockSpec(memory_space=pltpu.VMEM),
        scratch_shapes=[
            vmem((RING, GROUP_ROWS, SLAB), bf),
            vmem((RING, GROUP_ROWS, SLAB), bf),
            vmem((CORE_ROWS, BLOCK), f32),
            vmem((CORE_ROWS, BLOCK), bf),
            vmem((CORE_ROWS, BLOCK), bf),
            vmem((N_Z * SHARD, BLOCK), bf),
            vmem((N_Z - 1, SHARD, FWD), bf),
            vmem((N_Z - 1, SHARD, BLOCK - FWD), bf),
            vmem((2, N_Z * SHARD, BLOCK), bf),
            vmem((RING, GROUP_ROWS, SLAB), bf),
            vmem((HALF_ROWS, SLAB), bf),
            vmem((HALF_ROWS, SLAB), bf),
            vmem((GROUP_ROWS, SLAB), bf),
            vmem((GROUP_ROWS, SLAB), bf),
            vmem((GROUP_ROWS, SLAB), f32),
            vmem((RING, GROUP_ROWS, SLAB // 2), bf),
            vmem((RING, GROUP_ROWS, SLAB // 2), bf),
            vmem((2, RING, GROUP_ROWS, SLAB // 2), bf),
            vmem((BLOCK, SLAB // 2), f32),
            pltpu.SemaphoreType.DMA((N_MESSAGES,)),
            pltpu.SemaphoreType.DMA((N_MESSAGES,)),
        ],
        compiler_params=pltpu.CompilerParams(
            collective_id=0, has_side_effects=True, vmem_limit_bytes=56 * 1024 * 1024
        ),
    )(own_block)


def local(flat_iterate, lengths):
    dp_count = lax.axis_size("dp")
    row_count = lax.axis_size("row")
    col_count = lax.axis_size("col")
    groups = row_count * col_count
    dp_index = lax.axis_index("dp")
    group_index = lax.axis_index("row") * col_count + lax.axis_index("col")
    capacity = flat_iterate.shape[1]
    span_rows = (capacity + COLS - 1) // COLS + 1
    group_rows = ROWS // groups
    slab_width = COLS // dp_count
    shard_ends = jnp.cumsum(lengths, axis=1)
    starts = shard_ends - lengths
    own_starts = lax.dynamic_index_in_dim(starts, group_index, 0, keepdims=False)
    own_lengths = lax.dynamic_index_in_dim(lengths, group_index, 0, keepdims=False)
    first_rows = own_starts // COLS
    my_start = lax.dynamic_index_in_dim(own_starts, dp_index, 0, keepdims=False)
    my_length = lax.dynamic_index_in_dim(own_lengths, dp_index, 0, keepdims=False)
    lead_cols = my_start - my_start // COLS * COLS
    places = jnp.arange(capacity, dtype=jnp.int32)
    segment = jnp.where(places < my_length, flat_iterate[0], jnp.zeros((), jnp.bfloat16))
    canvas = lax.dynamic_update_slice(
        jnp.zeros((span_rows * COLS,), jnp.bfloat16), segment, (lead_cols,)
    )
    canvas = canvas.reshape(span_rows, COLS)
    arrived = lax.all_to_all(canvas, "dp", split_axis=1, concat_axis=0, tiled=True)
    targets = (first_rows[:, None] + jnp.arange(span_rows, dtype=jnp.int32)[None, :]).reshape(-1)
    landing = jnp.zeros((group_rows + span_rows, slab_width), jnp.float32)
    landing = landing.at[targets].add(arrived.astype(jnp.float32))
    own_block = landing[:group_rows].astype(jnp.bfloat16)
    update = newton_schulz(own_block)
    padded = jnp.concatenate([update, jnp.zeros((span_rows, slab_width), jnp.bfloat16)], axis=0)
    outgoing = jnp.take(padded, targets, axis=0)
    returned = lax.all_to_all(outgoing, "dp", split_axis=0, concat_axis=1, tiled=True)
    flat_back = lax.dynamic_slice_in_dim(returned.reshape(-1), lead_cols, capacity)
    flat_back = jnp.where(places < my_length, flat_back, jnp.zeros((), jnp.bfloat16))
    return flat_back[None, :]


def solution(mesh):
    return jax.shard_map(
        local,
        mesh=mesh,
        in_specs=(P(("dp", "row", "col"), None), P()),
        out_specs=P(("dp", "row", "col"), None),
        check_vma=False,
    )
```

time: 494 us -> 226 us (0.46)
  waiting for transfers between devices: 380 us -> 19.7 us
  Pallas kernels: 0 us -> 126 us
  matrix products: 20.5 us -> 0 us
  between operations: 16.6 us -> 3.4 us
    psum x2 -> x0, waiting for transfers between devices: 241 us -> none  [reduce_whole(): lax.psum(partial_value.astype(jnp.bfloat16), 'dp').astype(jnp.float32)]
    pallas_call x0 -> x1, Pallas kernels: none -> 126 us  [newton_schulz(): pl.pallas_call(core_kernel, out_shape=jax.ShapeDtypeStruct((GROUP_ROWS, S...]
    all_gather x2 -> x0, waiting for transfers between devices: 119 us -> none  [the longest x1 60.8 us: local(): slab_all = lax.all_gather(own_block, ('row', 'col'), axis=0, tiled=True)]
    dot_general x3 -> x0, matrix products: 20.5 us -> none  [the longest x1 7.19 us: local(): product = jnp.dot(poly_rows, slab_all, preferred_element_type=jnp.float32)]
  transfers between devices with their start and end apart: 5 -> 1, of which waited for: 5 -> 1; matrix products, arithmetic and copies ran while one was open for 0% -> 0% of each run, Pallas kernels for 0% -> 0%
where the time goes in v1:
time: 226 us
  Pallas kernels  126 us (56%)
  blocking collectives  28.3 us (13%)
  other arithmetic  23 us (10%)
  waiting for transfers between devices  19.7 us (9%)
  local copies, waits for them, and re-layouts  15.5 us (7%)
  starting transfers between devices  9.99 us (4%)
  between operations  3.4 us (2%)
    pallas_call x1, Pallas kernels, newton_schulz(): pl.pallas_call(core_kernel, out_shape=jax.ShapeDtypeStruct((GROUP_ROWS, S...  126 us
    all_to_all x1, blocking collectives, local(): lax.all_to_all(outgoing, 'dp', split_axis=0, concat_axis=1, tiled=True)  28.3 us
    all_to_all x1, waiting for transfers between devices, local(): lax.all_to_all(canvas, 'dp', split_axis=1, concat_axis=0, tiled=True)  19.7 us
    unnamed x1, other arithmetic  12.2 us
    all_to_all x1, starting transfers between devices, local(): lax.all_to_all(canvas, 'dp', split_axis=1, concat_axis=0, tiled=True)  9.99 us
    scatter-add x1, other arithmetic, local(): landing = landing.at[targets].add(arrived.astype(jnp.float32))  6.94 us
    dynamic_update_slice x1, local copies, waits for them, and re-layouts, local(): lax.dynamic_update_slice(jnp.zeros((span_rows * COLS,), jnp.bfloat16), se...  4.99 us
  transfers between devices with their start and end apart: 1, of which 1 were waited for; matrix products, arithmetic and copies ran while one was open for 0% of the time, Pallas kernels for 0%

profile of v1, /device:TPU:1, one launch (start us, length us, event | category | flops | bytes accessed | tf_op | source)
XLA Modules:
  0.0 225.5 jit_solution(235857165123094024)
XLA Ops:
  0.0 0.9 reduce_window_sum.11
  0.9 0.7 sub.14
  1.6 1.3 dynamic_slice.15
  2.8 0.6 dynamic_slice.17
  6.7 12.2 %reduce.1 = bf16[270336]{0:T(1024)(128)(2,1)S(1)} reduce(bf16[1,270336]{1,0:T(2,128)(2,1)} %param.2, bf16[]{:T(256)} %constant.109), dimensions={0}, to_apply=%param.2.reduce_sub_computation | reduce | bytes 1081346 | tf_op args[0]
  18.9 0.8 fusion.1
  19.7 5.0 %dynamic_update_slice.3 = bf16[278528]{0:T(1024)(128)(2,1)S(1)} dynamic-update-slice(bf16[278528]{0:T(1024)(128)(2,1)S(1)} %broadcast_in_dim.30, bf16[270336]{0:T(1024)(128)(2,1)S(1)} %fusion.1, s32[]{:T(128)S(6)} %select_n.71) | dynamic-update-slice | bytes 1081348 | tf_op jit(solution)/shard_map/dynamic_update_slice | solution.py:325
  24.7 0.3 all_to_all.20
  25.1 1.1 copy.5
  26.2 10.0 %all-to-all-start = ((bf16[34,16,512]{2,0,1:T(8,128)(2,1)}), bf16[34,16,512]{2,0,1:T(8,128)(2,1)S(1)}, u32[]{:S(2)}, u32[]{:S(2)}) async-start(bf16[34,16,512]{2,0,1:T(8,128)(2,1)} %copy.5), calls=%async_computation | async-start | bytes 1310720 | tf_op jit(solution)/shard_map/all_to_all | solution.py:329
  36.2 0.1 iota_add_fusion
  36.3 0.1 add.90
  36.4 0.1 compare_and_fusion
  36.5 19.7 %all-to-all-done = bf16[34,16,512]{2,0,1:T(8,128)(2,1)S(1)} async-done(((bf16[34,16,512]{2,0,1:T(8,128)(2,1)}), bf16[34,16,512]{2,0,1:T(8,128)(2,1)S(1)}, u32[]{:S(2)}, u32[]{:S(2)}) %all-to-all-start) | async-done | bytes 557088 | tf_op jit(solution)/shard_map/all_to_all | solution.py:329
  56.2 0.2 convert_bitcast_fusion
  56.4 0.1 reshape.103
  56.5 6.9 %scatter_custom_fusion = f32[386,512]{1,0:T(8,128)S(1)} fusion(s32[544]{0:T(1024)S(1)} %fusion.4, f32[544,512]{1,0:T(8,128)S(1)} %reshape.103, f32[]{:T(128)} %constant.100.clone.1), kind=kCustom, calls=%fused_computation.8 | custom fusion | flops 278528 | bytes 790532 | tf_op jit(solution)/shard_map/scatter-add | solution.py:332
  63.5 0.8 slice.9.x_ref
  64.3 125.6 %shard_map.28 = bf16[352,512]{1,0:T(8,128)(2,1)} custom-call(bf16[352,512]{1,0:T(8,128)(2,1)} %slice.9.x_ref), custom_call_target="tpu_custom_call" | custom-call | tf_op jit(solution)/shard_map/pallas_call | solution.py:270
  189.9 1.0 concatenate.3
  190.9 2.7 %gather_fusion = bf16[544,512]{1,0:T(8,128)(2,1)S(1)} fusion(bf16[386,512]{1,0:T(8,128)(2,1)S(1)} %concatenate.3, s32[1024]{0:T(1024)S(1)} %pad_clamp_fusion), kind=kCustom, calls=%fused_computation | custom fusion | bytes 1116288 | tf_op jit(solution)/shard_map/jit(_take)/gather | solution.py:336
  193.6 0.2 gather.7
  193.8 0.2 broadcast_select_fusion
  193.9 28.3 %all_to_all.26 = bf16[16,34,512]{2,1,0:T(8,128)(2,1)S(1)} all-to-all(bf16[16,34,512]{2,1,0:T(8,128)(2,1)S(1)} %broadcast_select_fusion), channel_id=1, replica_groups=mesh['dp'=16,'row'=4,'col'=4] {'dp'}, dimensions={0} | all-to-all | bytes 1114112 | tf_op jit(solution)/shard_map/all_to_all | solution.py:337
  222.3 0.2 copy.6
  222.4 0.2 copy.7
  222.7 1.0 fusion
  223.7 1.9 broadcast_in_dim.33
  (4 shorter events, 0.1 us)
Async XLA Ops:
  26.2 30.0 %all-to-all-start = ((bf16[34,16,512]{2,0,1:T(8,128)(2,1)}), bf16[34,16,512]{2,0,1:T(8,128)(2,1)S(1)}, u32[]{:S(2)}, u32[]{:S(2)}) async-start(bf16[34,16,512]{2,0,1:T(8,128)(2,1)} %copy.5), calls=%async_computation | async-start | bytes 1310720 | tf_op jit(solution)/shard_map/all_to_all | solution.py:329

commit v2 on v1

--- a/solution.py
+++ b/solution.py
@@ -25,15 +25,21 @@
 CORE_ROWS = 704
 SHARD = 96
 HALF_SHARD = 48
+LANES = 128
+CHUNKS = COLS // LANES
+FLAT_ROWS = 2112
+MAIN = 32
+EXTRA = 16
+LEAD = 72
 FWD = 768
-N_MESSAGES = 96
+N_MESSAGES = 160
 MESH = pl.DeviceIdType.MESH
 SCALE = 0.2 * math.sqrt(max(ROWS, COLS))
 
 
 def core_kernel(
-    x_ref, out_ref, xr, xs, own_f32, to_sib, from_sib, gh, ring_f, ring_b, g_full,
-    part, got_a, got_b, got_c, got_d, y_f32, ya, yb, part2, z_b, send_sem, recv_sem,
+    lengths_ref, flat_ref, out_ref, staged, canvas, extra_tmp, extra, arrived, arrived_extra, back, x_ref, xr, xs, own_f32, to_sib, from_sib, gh, ring_f, ring_b, g_full,
+    part, got_a, got_b, got_c, got_d, y_f32, ya, yb, part2, z_b, update, returned, returned_extra, send_sem, recv_sem,
 ):
     dp = lax.axis_index("dp")
     y = lax.axis_index("row")
@@ -52,11 +58,17 @@
     place = {"col": x, "row": y}
 
     barrier = pltpu.get_barrier_semaphore()
-    for peer in (dev_sib, dev_up, dev_down) + near["col"] + near["row"]:
+    for peer in near["col"] + near["row"]:
         pl.semaphore_signal(barrier, inc=1, device_id=peer, device_id_type=MESH)
-    pl.semaphore_wait(barrier, 7)
-
-    counter = [0]
+
+    def greet(o, _):
+        pl.semaphore_signal(barrier, inc=1, device_id=((dp + o) % N_DP, y, x), device_id_type=MESH)
+        return 0
+
+    lax.fori_loop(1, N_DP, greet, 0)
+    pl.semaphore_wait(barrier, 4 + N_DP - 1)
+
+    counter = [4 * N_DP]
     started = []
 
     def message(src, dst, device, slot=None):
@@ -97,6 +109,104 @@
     def gather_end(tail):
         for copy in tail:
             copy.wait_recv()
+
+    group = y * RING + x
+    my_start = jnp.int32(0)
+    begin = jnp.int32(0)
+    first_rows = []
+    for d in range(N_DP):
+        first_rows.append(begin // COLS)
+        my_start = jnp.where(dp == d, begin, my_start)
+        begin = begin + lengths_ref[group, d]
+    my_length = lengths_ref[group, dp]
+    lead = my_start % COLS
+    lead_rows, lead_lanes = lead // LANES, lead % LANES
+    staged[pl.ds(0, LEAD)] = jnp.zeros((LEAD, LANES), jnp.float32)
+    tail_rows = staged.shape[0] - LEAD - FLAT_ROWS
+    staged[pl.ds(LEAD + FLAT_ROWS, tail_rows)] = jnp.zeros((tail_rows, LANES), jnp.float32)
+    STEP = 176
+
+    def slots(i):
+        return (
+            i * (STEP * LANES)
+            + lax.broadcasted_iota(jnp.int32, (STEP, LANES), 0) * LANES
+            + lax.broadcasted_iota(jnp.int32, (STEP, LANES), 1)
+        )
+
+    def stage(i, _):
+        rows = pl.ds(pl.multiple_of(i * STEP, 8), STEP)
+        value = jnp.where(slots(i) < my_length, flat_ref[rows], 0.0)
+        staged[pl.ds(pl.multiple_of(i * STEP + LEAD, 8), STEP)] = pltpu.roll(value, lead_lanes, 1)
+        return 0
+
+    lax.fori_loop(0, FLAT_ROWS // STEP, stage, 0)
+    extra_tmp[...] = jnp.zeros_like(extra_tmp)
+
+    def exchange(o, base, src, src_extra, dst, dst_extra, there):
+        device = (there, y, x)
+        return (
+            message(src, dst, device, slot=base + o),
+            message(src_extra, dst_extra, device, slot=base + N_DP + o),
+        )
+
+    def out_copies(o):
+        there = (dp + o) % N_DP
+        return exchange(o, 0, canvas.at[there], extra.at[there], arrived.at[dp], arrived_extra.at[dp], there)
+
+    def place_part(o, _):
+        there = (dp + o) % N_DP
+        lane = lax.broadcasted_iota(jnp.int32, (MAIN, LANES), 1)
+        lane2 = lax.broadcasted_iota(jnp.int32, (2, LANES), 1)
+        start = LEAD - lead_rows + there * 4
+        before = staged[pl.ds(start - 1, MAIN, stride=CHUNKS)]
+        before2 = staged[pl.ds(start - 1 + MAIN * CHUNKS, 2, stride=CHUNKS)]
+        for j in range(4):
+            here = staged[pl.ds(start + j, MAIN, stride=CHUNKS)]
+            here2 = staged[pl.ds(start + j + MAIN * CHUNKS, 2, stride=CHUNKS)]
+            canvas[there, :, pl.ds(j * LANES, LANES)] = jnp.where(lane >= lead_lanes, here, before).astype(jnp.bfloat16)
+            extra_tmp[pl.ds(j * 2, 2)] = jnp.where(lane2 >= lead_lanes, here2, before2)
+            before, before2 = here, here2
+        extra[there] = extra_tmp[...].astype(jnp.bfloat16)
+
+        @pl.when(o < N_DP)
+        def _():
+            for copy in out_copies(o):
+                copy.start()
+
+        return 0
+
+    lax.fori_loop(1, N_DP + 1, place_part, 0)
+    arrived[dp] = canvas[dp]
+    arrived_extra[dp] = extra[dp]
+
+    def targets(length, width, offset, shape, dim):
+        k = lax.broadcasted_iota(jnp.int32, shape, dim)
+        found = jnp.full(shape, -1, jnp.int32)
+        for d in range(N_DP):
+            inside = k // width == d
+            found = jnp.where(inside, first_rows[d] + k % width + offset, found)
+        return k, found
+
+    k, row_of = targets(N_DP * MAIN, MAIN, 0, (1, N_DP * MAIN), 1)
+    pick = (lax.broadcasted_iota(jnp.int32, (GROUP_ROWS, N_DP * MAIN), 0) == row_of).astype(jnp.float32).astype(jnp.bfloat16)
+    ke, row_e = targets(N_DP * EXTRA, EXTRA, MAIN, (1, N_DP * EXTRA), 1)
+    ke = ke % EXTRA
+
+    def wait_out(o, _):
+        for copy in out_copies(o):
+            copy.wait()
+        return 0
+
+    lax.fori_loop(1, N_DP, wait_out, 0)
+    x_main = jnp.dot(pick, arrived[...].reshape(N_DP * MAIN, SLAB), preferred_element_type=jnp.float32)
+    late = arrived_extra[...].reshape(N_DP * EXTRA, LANES)
+    for j in range(4):
+        row_j = jnp.where(ke // 2 == j, row_e - 2 * j, -1)
+        pick_j = (lax.broadcasted_iota(jnp.int32, (GROUP_ROWS, N_DP * EXTRA), 0) == row_j).astype(jnp.float32).astype(jnp.bfloat16)
+        cols = slice(j * LANES, (j + 1) * LANES)
+        x_ref[:, cols] = (
+            x_main[:, cols] + jnp.dot(pick_j, late, preferred_element_type=jnp.float32)
+        ).astype(jnp.bfloat16)
 
     xr[x] = x_ref[...]
     xs[y] = x_ref[...]
@@ -257,22 +367,84 @@
     gather_end(tb)
     for cols, own in ((first, za_own), (second, z_b[pl.ds(pl.multiple_of(y * GROUP_ROWS, 8), GROUP_ROWS)])):
         z_val = own + got_c[:, cols].astype(jnp.float32) + got_d[:, cols].astype(jnp.float32)
-        out_ref[:, cols] = (
+        update[:, cols] = (
             SCALE * (LINEAR_COEF * x_ref[:, cols].astype(jnp.float32) + (CUBIC_COEF * y_f32[:, cols] + QUINTIC_COEF * z_val))
         ).astype(jnp.bfloat16)
+
+    _, row_of = targets(N_DP * MAIN, MAIN, 0, (N_DP * MAIN, 1), 0)
+    pick = (lax.broadcasted_iota(jnp.int32, (N_DP * MAIN, GROUP_ROWS), 1) == row_of).astype(jnp.float32).astype(jnp.bfloat16)
+    canvas[...] = jnp.dot(pick, update[...], preferred_element_type=jnp.float32).astype(jnp.bfloat16).reshape(N_DP, MAIN, SLAB)
+    ke, row_e = targets(N_DP * EXTRA, EXTRA, MAIN, (N_DP * EXTRA, 1), 0)
+    ke = ke % EXTRA
+    late = jnp.zeros((N_DP * EXTRA, LANES), jnp.float32)
+    for j in range(4):
+        row_j = jnp.where(ke // 2 == j, row_e - 2 * j, -1)
+        pick_j = (lax.broadcasted_iota(jnp.int32, (N_DP * EXTRA, GROUP_ROWS), 1) == row_j).astype(jnp.float32).astype(jnp.bfloat16)
+        late += jnp.dot(pick_j, update[:, j * LANES : (j + 1) * LANES], preferred_element_type=jnp.float32)
+    extra[...] = late.astype(jnp.bfloat16).reshape(N_DP, EXTRA, LANES)
+
+    def back_copies(o):
+        there = (dp + o) % N_DP
+        return exchange(o, 2 * N_DP, canvas.at[there], extra.at[there], returned.at[dp], returned_extra.at[dp], there)
+
+    def send_back(o, _):
+        for copy in back_copies(o):
+            copy.start()
+        return 0
+
+    lax.fori_loop(1, N_DP, send_back, 0)
+    returned[dp] = canvas[dp]
+    returned_extra[dp] = extra[dp]
+
+    def wait_back(o, _):
+        for copy in back_copies(o):
+            copy.wait()
+        return 0
+
+    lax.fori_loop(1, N_DP, wait_back, 0)
+
+    def unpack(d, _):
+        extra_tmp[...] = returned_extra[d].astype(jnp.float32)
+        for j in range(4):
+            back[pl.ds(d * 4 + j, MAIN, stride=CHUNKS)] = pltpu.roll(
+                returned[d, :, pl.ds(j * LANES, LANES)].astype(jnp.float32), (LANES - lead_lanes) % LANES, 1)
+            back[pl.ds(d * 4 + j + MAIN * CHUNKS, 2, stride=CHUNKS)] = pltpu.roll(
+                extra_tmp[...], (LANES - lead_lanes) % LANES, 1)[2 * j : 2 * j + 2]
+        return 0
+
+    lax.fori_loop(0, N_DP, unpack, 0)
+    back[pl.ds(34 * CHUNKS, 8)] = jnp.zeros((8, LANES), jnp.float32)
+
+    def finish(i, _):
+        here = back[pl.ds(i * STEP + lead_rows, STEP)]
+        after = back[pl.ds(i * STEP + lead_rows + 1, STEP)]
+        lane = lax.broadcasted_iota(jnp.int32, (STEP, LANES), 1)
+        value = jnp.where(lane + lead_lanes < LANES, here, after)
+        out_ref[pl.ds(pl.multiple_of(i * STEP, 8), STEP)] = jnp.where(slots(i) < my_length, value, 0.0)
+        return 0
+
+    lax.fori_loop(0, FLAT_ROWS // STEP, finish, 0)
     for copy in started:
         copy.wait_send()
 
 
-def newton_schulz(own_block):
+def newton_schulz(lengths, flat):
     bf, f32 = jnp.bfloat16, jnp.float32
     vmem = pltpu.VMEM
     return pl.pallas_call(
         core_kernel,
-        out_shape=jax.ShapeDtypeStruct((GROUP_ROWS, SLAB), bf),
-        in_specs=[pl.BlockSpec(memory_space=pltpu.VMEM)],
+        out_shape=jax.ShapeDtypeStruct((FLAT_ROWS, LANES), f32),
+        in_specs=[pl.BlockSpec(memory_space=pltpu.SMEM), pl.BlockSpec(memory_space=pltpu.VMEM)],
         out_specs=pl.BlockSpec(memory_space=pltpu.VMEM),
         scratch_shapes=[
+            vmem((LEAD + FLAT_ROWS + 88, LANES), f32),
+            vmem((N_DP, MAIN, SLAB), bf),
+            vmem((EXTRA, LANES), f32),
+            vmem((N_DP, EXTRA, LANES), bf),
+            vmem((N_DP, MAIN, SLAB), bf),
+            vmem((N_DP, EXTRA, LANES), bf),
+            vmem((34 * CHUNKS + 8, LANES), f32),
+            vmem((GROUP_ROWS, SLAB), bf),
             vmem((RING, GROUP_ROWS, SLAB), bf),
             vmem((RING, GROUP_ROWS, SLAB), bf),
             vmem((CORE_ROWS, BLOCK), f32),
@@ -292,52 +464,21 @@
             vmem((RING, GROUP_ROWS, SLAB // 2), bf),
             vmem((2, RING, GROUP_ROWS, SLAB // 2), bf),
             vmem((BLOCK, SLAB // 2), f32),
+            vmem((GROUP_ROWS, SLAB), bf),
+            vmem((N_DP, MAIN, SLAB), bf),
+            vmem((N_DP, EXTRA, LANES), bf),
             pltpu.SemaphoreType.DMA((N_MESSAGES,)),
             pltpu.SemaphoreType.DMA((N_MESSAGES,)),
         ],
         compiler_params=pltpu.CompilerParams(
             collective_id=0, has_side_effects=True, vmem_limit_bytes=56 * 1024 * 1024
         ),
-    )(own_block)
+    )(lengths, flat)
 
 
 def local(flat_iterate, lengths):
-    dp_count = lax.axis_size("dp")
-    row_count = lax.axis_size("row")
-    col_count = lax.axis_size("col")
-    groups = row_count * col_count
-    dp_index = lax.axis_index("dp")
-    group_index = lax.axis_index("row") * col_count + lax.axis_index("col")
-    capacity = flat_iterate.shape[1]
-    span_rows = (capacity + COLS - 1) // COLS + 1
-    group_rows = ROWS // groups
-    slab_width = COLS // dp_count
-    shard_ends = jnp.cumsum(lengths, axis=1)
-    starts = shard_ends - lengths
-    own_starts = lax.dynamic_index_in_dim(starts, group_index, 0, keepdims=False)
-    own_lengths = lax.dynamic_index_in_dim(lengths, group_index, 0, keepdims=False)
-    first_rows = own_starts // COLS
-    my_start = lax.dynamic_index_in_dim(own_starts, dp_index, 0, keepdims=False)
-    my_length = lax.dynamic_index_in_dim(own_lengths, dp_index, 0, keepdims=False)
-    lead_cols = my_start - my_start // COLS * COLS
-    places = jnp.arange(capacity, dtype=jnp.int32)
-    segment = jnp.where(places < my_length, flat_iterate[0], jnp.zeros((), jnp.bfloat16))
-    canvas = lax.dynamic_update_slice(
-        jnp.zeros((span_rows * COLS,), jnp.bfloat16), segment, (lead_cols,)
-    )
-    canvas = canvas.reshape(span_rows, COLS)
-    arrived = lax.all_to_all(canvas, "dp", split_axis=1, concat_axis=0, tiled=True)
-    targets = (first_rows[:, None] + jnp.arange(span_rows, dtype=jnp.int32)[None, :]).reshape(-1)
-    landing = jnp.zeros((group_rows + span_rows, slab_width), jnp.float32)
-    landing = landing.at[targets].add(arrived.astype(jnp.float32))
-    own_block = landing[:group_rows].astype(jnp.bfloat16)
-    update = newton_schulz(own_block)
-    padded = jnp.concatenate([update, jnp.zeros((span_rows, slab_width), jnp.bfloat16)], axis=0)
-    outgoing = jnp.take(padded, targets, axis=0)
-    returned = lax.all_to_all(outgoing, "dp", split_axis=0, concat_axis=1, tiled=True)
-    flat_back = lax.dynamic_slice_in_dim(returned.reshape(-1), lead_cols, capacity)
-    flat_back = jnp.where(places < my_length, flat_back, jnp.zeros((), jnp.bfloat16))
-    return flat_back[None, :]
+    flat = flat_iterate.astype(jnp.float32).reshape(FLAT_ROWS, LANES)
+    return newton_schulz(lengths, flat).reshape(1, FLAT_ROWS * LANES).astype(jnp.bfloat16)
 
 
 def solution(mesh):

time: 226 us -> 189 us (0.84)
  Pallas kernels: 126 us -> 175 us
  blocking collectives: 28.3 us -> 0 us
  waiting for transfers between devices: 19.7 us -> 0 us
  other arithmetic: 23 us -> 4.87 us
  starting transfers between devices: 9.99 us -> 0 us
  local copies, waits for them, and re-layouts: 15.5 us -> 9.31 us
  between operations: 3.4 us -> 0.01 us
    pallas_call x1, Pallas kernels: 126 us -> 175 us  [newton_schulz(): pl.pallas_call(core_kernel, out_shape=jax.ShapeDtypeStruct((FLAT_ROWS, LA...]
    all_to_all x1 -> x0, blocking collectives: 28.3 us -> none  [local(): lax.all_to_all(outgoing, 'dp', split_axis=0, concat_axis=1, tiled=True)]
    all_to_all x1 -> x0, waiting for transfers between devices: 19.7 us -> none  [local(): lax.all_to_all(canvas, 'dp', split_axis=1, concat_axis=0, tiled=True)]
    unnamed x1, other arithmetic: 12.2 us -> 1.29 us
    all_to_all x1 -> x0, starting transfers between devices: 9.99 us -> none  [local(): lax.all_to_all(canvas, 'dp', split_axis=1, concat_axis=0, tiled=True)]
    unnamed x1, local copies, waits for them, and re-layouts: 0.22 us -> 9.31 us
    scatter-add x1 -> x0, other arithmetic: 6.94 us -> none  [local(): landing = landing.at[targets].add(arrived.astype(jnp.float32))]
    dynamic_update_slice x1 -> x0, local copies, waits for them, and re-layouts: 4.99 us -> none  [local(): lax.dynamic_update_slice(jnp.zeros((span_rows * COLS,), jnp.bfloat16), se...]
  transfers between devices with their start and end apart: 1 -> 0, of which waited for: 1 -> 0; matrix products, arithmetic and copies ran while one was open for 0% -> 0% of each run, Pallas kernels for 0% -> 0%
where the time goes in v2:
time: 189 us
  Pallas kernels  175 us (93%)
  local copies, waits for them, and re-layouts  9.31 us (5%)
  other arithmetic  4.87 us (3%)
    pallas_call x1, Pallas kernels, newton_schulz(): pl.pallas_call(core_kernel, out_shape=jax.ShapeDtypeStruct((FLAT_ROWS, LA...  175 us
    unnamed x1, local copies, waits for them, and re-layouts  9.31 us

profile of v2, /device:TPU:1, one launch (start us, length us, event | category | flops | bytes accessed | tf_op | source)
XLA Modules:
  0.0 188.8 jit_solution(5294033331010297481)
XLA Ops:
  0.0 3.6 %reshape.21 = f32[1,270336]{1,0:T(1,128)} convert(bf16[1,270336]{1,0:T(2,128)(2,1)} %param.2) | non-fusion elementwise | flops 270336 | bytes 1622016 | tf_op jit(solution)/shard_map/reshape | solution.py:480
  3.6 174.6 %shard_map.28 = f32[2112,128]{1,0:T(8,128)} custom-call(s32[16,16]{1,0:T(8,128)} %lengths_ref.1, f32[2112,128]{1,0:T(8,128)} %bitcast.7), custom_call_target="tpu_custom_call" | custom-call | tf_op jit(solution)/shard_map/pallas_call | solution.py:434
  178.2 1.3 convert_bitcast_fusion
  179.5 9.3 %copy.5 = bf16[1,1,2112,128]{3,1,2,0:T(2,128)(2,1)} copy(bf16[1,1,2112,128]{3,2,1,0:T(8,128)(2,1)S(1)} %convert_bitcast_fusion) | data formatting | bytes 1081344

commit v3 on v2

--- a/solution.py
+++ b/solution.py
@@ -23,15 +23,15 @@
 SLAB = 512
 BLOCK = 1408
 CORE_ROWS = 704
-SHARD = 96
-HALF_SHARD = 48
+SHARD = 48
+PANEL = N_Z * SHARD
+HALF_SLAB = SLAB // 2
 LANES = 128
 CHUNKS = COLS // LANES
 FLAT_ROWS = 2112
 MAIN = 32
 EXTRA = 16
 LEAD = 72
-FWD = 768
 N_MESSAGES = 160
 MESH = pl.DeviceIdType.MESH
 SCALE = 0.2 * math.sqrt(max(ROWS, COLS))
@@ -39,7 +39,7 @@
 
 def core_kernel(
     lengths_ref, flat_ref, out_ref, staged, canvas, extra_tmp, extra, arrived, arrived_extra, back, x_ref, xr, xs, own_f32, to_sib, from_sib, gh, ring_f, ring_b, g_full,
-    part, got_a, got_b, got_c, got_d, y_f32, ya, yb, part2, z_b, update, returned, returned_extra, send_sem, recv_sem,
+    part, got_a, got_b, got_c, got_d, y_f32, ya, yb, part2, z_b, z_f32, update, returned, returned_extra, send_sem, recv_sem,
 ):
     dp = lax.axis_index("dp")
     y = lax.axis_index("row")
@@ -66,7 +66,6 @@
         return 0
 
     lax.fori_loop(1, N_DP, greet, 0)
-    pl.semaphore_wait(barrier, 4 + N_DP - 1)
 
     counter = [4 * N_DP]
     started = []
@@ -167,15 +166,17 @@
             extra_tmp[pl.ds(j * 2, 2)] = jnp.where(lane2 >= lead_lanes, here2, before2)
             before, before2 = here, here2
         extra[there] = extra_tmp[...].astype(jnp.bfloat16)
-
-        @pl.when(o < N_DP)
-        def _():
-            for copy in out_copies(o):
-                copy.start()
-
         return 0
 
     lax.fori_loop(1, N_DP + 1, place_part, 0)
+    pl.semaphore_wait(barrier, 4 + N_DP - 1)
+
+    def send_out(o, _):
+        for copy in out_copies(o):
+            copy.start()
+        return 0
+
+    lax.fori_loop(1, N_DP, send_out, 0)
     arrived[dp] = canvas[dp]
     arrived_extra[dp] = extra[dp]
 
@@ -208,7 +209,13 @@
             x_main[:, cols] + jnp.dot(pick_j, late, preferred_element_type=jnp.float32)
         ).astype(jnp.bfloat16)
 
-    xr[x] = x_ref[...]
+    pad = pl.ds(GROUP_ROWS, PANEL - GROUP_ROWS)
+    for q in range(RING):
+        xr[q, pad] = jnp.zeros((PANEL - GROUP_ROWS, SLAB), jnp.bfloat16)
+        yb[q, pad] = jnp.zeros((PANEL - GROUP_ROWS, HALF_SLAB), jnp.bfloat16)
+    for p in range(2):
+        gh[p, pad] = jnp.zeros((PANEL - GROUP_ROWS, BLOCK), jnp.bfloat16)
+    xr[x, pl.ds(0, GROUP_ROWS)] = x_ref[...]
     xs[y] = x_ref[...]
     s1 = gather_start("col", xr)
     s2 = gather_start("row", xs)
@@ -244,102 +251,134 @@
         return 0
 
     lax.fori_loop(0, 4, own_step, 0)
-    gh[pl.ds(CORE_ROWS, N_Z * SHARD - CORE_ROWS)] = jnp.zeros((N_Z * SHARD - CORE_ROWS, BLOCK), jnp.bfloat16)
-
     def join_step(i, _):
         rows = pl.ds(pl.multiple_of(i * HALF_ROWS, 16), HALF_ROWS)
         sib_message(i).wait()
-        gh[rows] = (own_f32[rows] + from_sib[rows].astype(jnp.float32)).astype(jnp.bfloat16)
+        part_rows = pl.ds(pl.multiple_of((i % 2) * HALF_ROWS, 16), HALF_ROWS)
+        gh[i // 2, part_rows] = (own_f32[rows] + from_sib[rows].astype(jnp.float32)).astype(jnp.bfloat16)
         return 0
 
     lax.fori_loop(0, 4, join_step, 0)
 
     def shard_rows(s):
-        return pl.ds(pl.multiple_of(s * SHARD, 16), SHARD)
-
-    f_cols, b_cols = pl.ds(0, FWD), pl.ds(FWD, BLOCK - FWD)
-    f_copy = b_copy = None
-    for t in range(N_Z - 1):
-        sf, sb = (z + 7 - t + N_Z) % N_Z, (z + 1 + t) % N_Z
-        if t == 0:
-            f_src, b_src = gh.at[shard_rows(sf), f_cols], gh.at[shard_rows(sb), b_cols]
-        else:
-            f_copy.wait_recv()
-            ring_f[t - 1] = (ring_f[t - 1].astype(jnp.float32) + gh[shard_rows(sf), f_cols].astype(jnp.float32)).astype(jnp.bfloat16)
-            f_src, b_src = ring_f.at[t - 1], ring_b.at[t - 1]
-        f_next = send(f_src, ring_f.at[t], dev_up)
-        if t > 0:
-            b_copy.wait_recv()
-            ring_b[t - 1] = (ring_b[t - 1].astype(jnp.float32) + gh[shard_rows(sb), b_cols].astype(jnp.float32)).astype(jnp.bfloat16)
-        b_next = send(b_src, ring_b.at[t], dev_down)
-        f_copy, b_copy = f_next, b_next
+        return pl.ds(pl.multiple_of(((s + N_Z) % N_Z) * SHARD, 16), SHARD)
+
+    f32 = jnp.float32
+    up_in, down_in = [], []
+    for k in range(7):
+        distance = 4 - (k + 1) // 2
+        for upward in (True, False):
+            panel = k % 2 if upward else 1 - k % 2
+            rows = shard_rows(z + distance if upward else z - distance)
+            arrivals, ring, device = (up_in, ring_f, dev_up) if upward else (down_in, ring_b, dev_down)
+            if k < 2:
+                src = gh.at[panel, rows]
+            else:
+                arrivals[k - 2].wait_recv()
+                ring[k - 2] = (ring[k - 2].astype(f32) + gh[panel, rows].astype(f32)).astype(jnp.bfloat16)
+                src = ring.at[k - 2]
+            arrivals.append(send(src, ring.at[k], device))
     mine = shard_rows(z)
-    f_copy.wait_recv()
-    g_full[c, mine, f_cols] = (ring_f[N_Z - 2].astype(jnp.float32) + gh[mine, f_cols].astype(jnp.float32)).astype(jnp.bfloat16)
-    b_copy.wait_recv()
-    g_full[c, mine, b_cols] = (ring_b[N_Z - 2].astype(jnp.float32) + gh[mine, b_cols].astype(jnp.float32)).astype(jnp.bfloat16)
+    for panel, k_up, k_down in ((0, 6, 5), (1, 5, 6)):
+        up_in[k_up].wait_recv()
+        down_in[k_down].wait_recv()
+        g_full[2 * c + panel, mine] = (
+            gh[panel, mine].astype(f32) + ring_f[k_up].astype(f32) + ring_b[k_down].astype(f32)
+        ).astype(jnp.bfloat16)
 
     pending = []
 
-    def relay(rows, device):
-        ref = g_full.at[c, rows]
+    def relay(panel, rows, device):
+        ref = g_full.at[2 * c + panel, rows]
         return send(ref, ref, device)
 
-    up = relay(mine, dev_up)
-    down = relay(mine, dev_down)
-    pending.append(relay(mine, dev_sib))
-    for step in range(1, 4):
-        before, after = shard_rows((z + N_Z - step) % N_Z), shard_rows((z + step) % N_Z)
-        if step == 3:
-            before_next = pl.ds(pl.multiple_of(((z + N_Z - step) % N_Z) * SHARD, 16), HALF_SHARD)
-            after_next = pl.ds(pl.multiple_of(((z + step) % N_Z) * SHARD + HALF_SHARD, 16), HALF_SHARD)
-        else:
-            before_next, after_next = before, after
-        up.wait_recv()
-        up = relay(before_next, dev_up)
-        pending.append(relay(before, dev_sib))
-        down.wait_recv()
-        down = relay(after_next, dev_down)
-        pending.append(relay(after, dev_sib))
-    far = ((z + 4) % N_Z) * SHARD
-    up.wait_recv()
-    pending.append(relay(pl.ds(pl.multiple_of(far, 16), HALF_SHARD), dev_sib))
-    down.wait_recv()
-    pending.append(relay(pl.ds(pl.multiple_of(far + HALF_SHARD, 16), HALF_SHARD), dev_sib))
+    up_in, down_in = [], []
+    for k in range(9):
+        back_by = k // 2
+        up_part, down_part = (k % 2, shard_rows(z - back_by)), (1 - k % 2, shard_rows(z + back_by))
+        if k >= 2:
+            up_in[k - 2].wait_recv()
+        if k < 7:
+            up_in.append(relay(*up_part, dev_up))
+        if k >= 2:
+            down_in[k - 2].wait_recv()
+        if k < 7:
+            down_in.append(relay(*down_part, dev_down))
+        pending.append(relay(*up_part, dev_sib))
+        if k >= 2:
+            pending.append(relay(*down_part, dev_sib))
     for copy in pending:
         copy.wait_recv()
 
-    def reduce4(axis, buf, cols, a_ref, b_ref, c_ref, d_ref, make):
+    def reduce_start(axis, buf, a_ref, b_ref):
         p = place[axis]
         right, left = near[axis]
-        after, before, far = (p + 1) % RING, (p + 3) % RING, (p + 2) % RING
-        make(far)
-        a = send(buf.at[far, top], a_ref, right)
-        b = send(buf.at[far, bottom], b_ref, left)
-        make(after)
-        c1 = send(buf.at[after, bottom], c_ref.at[bottom], right)
-        make(before)
-        d1 = send(buf.at[before, top], d_ref.at[top], left)
-        a.wait_recv()
-        buf[after, top] = (buf[after, top].astype(jnp.float32) + a_ref[...].astype(jnp.float32)).astype(jnp.bfloat16)
+        far = (p + 2) % RING
+        return (send(buf.at[far, top], a_ref, right), send(buf.at[far, bottom], b_ref, left))
+
+    def reduce_near(axis, buf, c_ref, d_ref):
+        p = place[axis]
+        right, left = near[axis]
+        after, before = (p + 1) % RING, (p + 3) % RING
+        return (
+            send(buf.at[after, bottom], c_ref.at[bottom], right),
+            send(buf.at[before, top], d_ref.at[top], left),
+        )
+
+    def reduce_pass(axis, buf, a_ref, b_ref, c_ref, d_ref, state):
+        p = place[axis]
+        right, left = near[axis]
+        after, before = (p + 1) % RING, (p + 3) % RING
+        state[0].wait_recv()
+        buf[after, top] = (buf[after, top].astype(f32) + a_ref[...].astype(f32)).astype(jnp.bfloat16)
         c2 = send(buf.at[after, top], c_ref.at[top], right)
-        b.wait_recv()
-        buf[before, bottom] = (buf[before, bottom].astype(jnp.float32) + b_ref[...].astype(jnp.float32)).astype(jnp.bfloat16)
+        state[1].wait_recv()
+        buf[before, bottom] = (buf[before, bottom].astype(f32) + b_ref[...].astype(f32)).astype(jnp.bfloat16)
         d2 = send(buf.at[before, bottom], d_ref.at[bottom], left)
-        return (c1, d1, c2, d2)
-
-    def g_rows(q):
-        return g_full[q // 2, pl.ds(pl.multiple_of((q % 2) * GROUP_ROWS, 16), GROUP_ROWS)]
-
-    def make_y(q):
-        part[q] = jnp.dot(g_rows(q), xs[...].reshape(BLOCK, SLAB), preferred_element_type=jnp.float32).astype(jnp.bfloat16)
-
-    tail = reduce4("col", part, SLAB, got_a, got_b, got_c, got_d, make_y)
-    y_f32[...] = jnp.dot(g_rows(x), xs[...].reshape(BLOCK, SLAB), preferred_element_type=jnp.float32)
-    gather_end(tail)
-    y_f32[...] = y_f32[...] + got_c[...].astype(jnp.float32) + got_d[...].astype(jnp.float32)
-    ya[y] = y_f32[:, : SLAB // 2].astype(jnp.bfloat16)
-    yb[x] = y_f32[:, SLAB // 2 :].astype(jnp.bfloat16)
+        return (c2, d2)
+
+    first, second = pl.ds(0, HALF_SLAB), pl.ds(HALF_SLAB, HALF_SLAB)
+
+    def apply_gram(right_a, right_b, buf, total):
+        def make(q):
+            return jnp.dot(g_full[q, pl.ds(0, GROUP_ROWS)], right_a(), preferred_element_type=f32)
+
+        far, after, before = (x + 2) % RING, (x + 1) % RING, (x + 3) % RING
+        buf_a, buf_b = buf.at[0], buf.at[1]
+        slots = [[r.at[i] for r in (got_a, got_b, got_c, got_d)] for i in range(2)]
+        buf_a[far] = make(far).astype(jnp.bfloat16)
+        sa = reduce_start("col", buf_a, *slots[0][:2])
+
+        def columns(j, _):
+            cols = pl.ds(pl.multiple_of(j * LANES, LANES), LANES)
+            z_b[cols] = lax.dot_general(
+                g_full[:, :, cols].reshape(RING * PANEL, LANES), right_b(), (((0,), (0,)), ((), ())),
+                preferred_element_type=f32,
+            )
+            return 0
+
+        lax.fori_loop(0, BLOCK // LANES, columns, 0)
+        buf_b[...] = z_b[...].astype(jnp.bfloat16).reshape(RING, GROUP_ROWS, HALF_SLAB)
+        sb = reduce_start("row", buf_b, *slots[1][:2])
+        nb = reduce_near("row", buf_b, *slots[1][2:])
+        buf_a[after] = make(after).astype(jnp.bfloat16)
+        buf_a[before] = make(before).astype(jnp.bfloat16)
+        na = reduce_near("col", buf_a, *slots[0][2:])
+        pa = reduce_pass("col", buf_a, *slots[0], sa)
+        pb = reduce_pass("row", buf_b, *slots[1], sb)
+        total[:, first] = make(x)
+        total[:, second] = z_b[pl.ds(pl.multiple_of(y * GROUP_ROWS, 8), GROUP_ROWS)]
+        for i, (cols, tail) in enumerate(((first, na + pa), (second, nb + pb))):
+            gather_end(tail)
+            total[:, cols] = total[:, cols] + got_c[i].astype(f32) + got_d[i].astype(f32)
+
+    apply_gram(
+        lambda: xs[:, :, :HALF_SLAB].reshape(BLOCK, HALF_SLAB),
+        lambda: xr[:, :, HALF_SLAB:].reshape(RING * PANEL, HALF_SLAB),
+        part, y_f32,
+    )
+    ya[y] = y_f32[:, :HALF_SLAB].astype(jnp.bfloat16)
+    yb[x, pl.ds(0, GROUP_ROWS)] = y_f32[:, HALF_SLAB:].astype(jnp.bfloat16)
     s1 = gather_start("row", ya)
     s2 = gather_start("col", yb)
     t1 = gather_pass("row", ya, s1)
@@ -347,29 +386,14 @@
     gather_end(t1)
     gather_end(t2)
 
-    first, second = pl.ds(0, SLAB // 2), pl.ds(SLAB // 2, SLAB // 2)
-
-    def make_za(q):
-        part2[0, q] = jnp.dot(g_rows(q), ya[...].reshape(BLOCK, SLAB // 2), preferred_element_type=jnp.float32).astype(jnp.bfloat16)
-
-    z_b[...] = jnp.zeros_like(z_b)
-    for q in range(4):
-        z_b[...] += lax.dot_general(
-            g_full[q // 2, pl.ds((q % 2) * GROUP_ROWS, GROUP_ROWS)], yb[q], (((0,), (0,)), ((), ())),
-            preferred_element_type=jnp.float32,
-        )
-    part2[1] = z_b[...].astype(jnp.bfloat16).reshape(4, GROUP_ROWS, SLAB // 2)
-
-    ta = reduce4("col", part2.at[0], None, got_a.at[:, first], got_b.at[:, first], got_c.at[:, first], got_d.at[:, first], make_za)
-    tb = reduce4("row", part2.at[1], None, got_a.at[:, second], got_b.at[:, second], got_c.at[:, second], got_d.at[:, second], lambda q: None)
-    za_own = jnp.dot(g_rows(x), ya[...].reshape(BLOCK, SLAB // 2), preferred_element_type=jnp.float32)
-    gather_end(ta)
-    gather_end(tb)
-    for cols, own in ((first, za_own), (second, z_b[pl.ds(pl.multiple_of(y * GROUP_ROWS, 8), GROUP_ROWS)])):
-        z_val = own + got_c[:, cols].astype(jnp.float32) + got_d[:, cols].astype(jnp.float32)
-        update[:, cols] = (
-            SCALE * (LINEAR_COEF * x_ref[:, cols].astype(jnp.float32) + (CUBIC_COEF * y_f32[:, cols] + QUINTIC_COEF * z_val))
-        ).astype(jnp.bfloat16)
+    apply_gram(
+        lambda: ya[...].reshape(BLOCK, HALF_SLAB),
+        lambda: yb[...].reshape(RING * PANEL, HALF_SLAB),
+        part2, z_f32,
+    )
+    update[...] = (
+        SCALE * (LINEAR_COEF * x_ref[...].astype(f32) + (CUBIC_COEF * y_f32[...] + QUINTIC_COEF * z_f32[...]))
+    ).astype(jnp.bfloat16)
 
     _, row_of = targets(N_DP * MAIN, MAIN, 0, (N_DP * MAIN, 1), 0)
     pick = (lax.broadcasted_iota(jnp.int32, (N_DP * MAIN, GROUP_ROWS), 1) == row_of).astype(jnp.float32).astype(jnp.bfloat16)
@@ -445,25 +469,26 @@
             vmem((N_DP, EXTRA, LANES), bf),
             vmem((34 * CHUNKS + 8, LANES), f32),
             vmem((GROUP_ROWS, SLAB), bf),
-            vmem((RING, GROUP_ROWS, SLAB), bf),
+            vmem((RING, PANEL, SLAB), bf),
             vmem((RING, GROUP_ROWS, SLAB), bf),
             vmem((CORE_ROWS, BLOCK), f32),
             vmem((CORE_ROWS, BLOCK), bf),
             vmem((CORE_ROWS, BLOCK), bf),
-            vmem((N_Z * SHARD, BLOCK), bf),
-            vmem((N_Z - 1, SHARD, FWD), bf),
-            vmem((N_Z - 1, SHARD, BLOCK - FWD), bf),
-            vmem((2, N_Z * SHARD, BLOCK), bf),
-            vmem((RING, GROUP_ROWS, SLAB), bf),
-            vmem((HALF_ROWS, SLAB), bf),
-            vmem((HALF_ROWS, SLAB), bf),
-            vmem((GROUP_ROWS, SLAB), bf),
-            vmem((GROUP_ROWS, SLAB), bf),
+            vmem((2, PANEL, BLOCK), bf),
+            vmem((7, SHARD, BLOCK), bf),
+            vmem((7, SHARD, BLOCK), bf),
+            vmem((RING, PANEL, BLOCK), bf),
+            vmem((2, RING, GROUP_ROWS, HALF_SLAB), bf),
+            vmem((2, HALF_ROWS, HALF_SLAB), bf),
+            vmem((2, HALF_ROWS, HALF_SLAB), bf),
+            vmem((2, GROUP_ROWS, HALF_SLAB), bf),
+            vmem((2, GROUP_ROWS, HALF_SLAB), bf),
             vmem((GROUP_ROWS, SLAB), f32),
-            vmem((RING, GROUP_ROWS, SLAB // 2), bf),
-            vmem((RING, GROUP_ROWS, SLAB // 2), bf),
-            vmem((2, RING, GROUP_ROWS, SLAB // 2), bf),
-            vmem((BLOCK, SLAB // 2), f32),
+            vmem((RING, GROUP_ROWS, HALF_SLAB), bf),
+            vmem((RING, PANEL, HALF_SLAB), bf),
+            vmem((2, RING, GROUP_ROWS, HALF_SLAB), bf),
+            vmem((BLOCK, HALF_SLAB), f32),
+            vmem((GROUP_ROWS, SLAB), f32),
             vmem((GROUP_ROWS, SLAB), bf),
             vmem((N_DP, MAIN, SLAB), bf),
             vmem((N_DP, EXTRA, LANES), bf),
@@ -478,7 +503,8 @@
 
 def local(flat_iterate, lengths):
     flat = flat_iterate.astype(jnp.float32).reshape(FLAT_ROWS, LANES)
-    return newton_schulz(lengths, flat).reshape(1, FLAT_ROWS * LANES).astype(jnp.bfloat16)
+    new_flat = newton_schulz(lengths, flat).reshape(1, FLAT_ROWS * LANES)
+    return lax.optimization_barrier(new_flat).astype(jnp.bfloat16)
 
 
 def solution(mesh):

time: 189 us -> 155 us (0.82)
  Pallas kernels: 175 us -> 148 us
  local copies, waits for them, and re-layouts: 9.31 us -> 0 us
  other arithmetic: 4.87 us -> 6.92 us
    pallas_call x1, Pallas kernels: 175 us -> 148 us  [newton_schulz(): pl.pallas_call(core_kernel, out_shape=jax.ShapeDtypeStruct((FLAT_ROWS, LA...]
    unnamed x1 -> x0, local copies, waits for them, and re-layouts: 9.31 us -> none
    convert_element_type x0 -> x1, other arithmetic: none -> 3.34 us  [local(): return lax.optimization_barrier(new_flat).astype(jnp.bfloat16)]
where the time goes in v3:
time: 155 us
  Pallas kernels  148 us (95%)
  other arithmetic  6.92 us (4%)
    pallas_call x1, Pallas kernels, newton_schulz(): pl.pallas_call(core_kernel, out_shape=jax.ShapeDtypeStruct((FLAT_ROWS, LA...  148 us
    reshape x1, other arithmetic, local(): flat = flat_iterate.astype(jnp.float32).reshape(FLAT_ROWS, LANES)  3.58 us
    convert_element_type x1, other arithmetic, local(): return lax.optimization_barrier(new_flat).astype(jnp.bfloat16)  3.34 us

profile of v3, /device:TPU:1, one launch (start us, length us, event | category | flops | bytes accessed | tf_op | source)
XLA Modules:
  0.0 154.9 jit_solution(16035120676638795296)
XLA Ops:
  0.0 3.6 %reshape.11 = f32[1,270336]{1,0:T(1,128)} convert(bf16[1,270336]{1,0:T(2,128)(2,1)} %param.2) | non-fusion elementwise | flops 270336 | bytes 1622016 | tf_op jit(solution)/shard_map/reshape | solution.py:505
  3.6 148.0 %shard_map.28 = f32[2112,128]{1,0:T(8,128)} custom-call(s32[16,16]{1,0:T(8,128)} %lengths_ref.1, f32[2112,128]{1,0:T(8,128)} %bitcast.3), custom_call_target="tpu_custom_call" | custom-call | tf_op jit(solution)/shard_map/pallas_call | solution.py:458
  151.6 3.3 %convert_element_type.4 = bf16[1,270336]{1,0:T(2,128)(2,1)} convert(f32[1,270336]{1,0:T(1,128)} %bitcast.2) | non-fusion elementwise | flops 270336 | bytes 1622016 | tf_op jit(solution)/shard_map/convert_element_type | solution.py:507

commit v4 on v3

--- a/solution.py
+++ b/solution.py
@@ -32,13 +32,13 @@
 MAIN = 32
 EXTRA = 16
 LEAD = 72
-N_MESSAGES = 160
+N_MESSAGES = 256
 MESH = pl.DeviceIdType.MESH
 SCALE = 0.2 * math.sqrt(max(ROWS, COLS))
 
 
 def core_kernel(
-    lengths_ref, flat_ref, out_ref, staged, canvas, extra_tmp, extra, arrived, arrived_extra, back, x_ref, xr, xs, own_f32, to_sib, from_sib, gh, ring_f, ring_b, g_full,
+    lengths_ref, flat_ref, out_ref, staged, canvas, outgoing, extra_tmp, extra, arrived, arrived_extra, back, x_ref, xr, xs, own_f32, sib_f32, to_sib, from_sib, gh, ring_f, ring_b, g_full,
     part, got_a, got_b, got_c, got_d, y_f32, ya, yb, part2, z_b, z_f32, update, returned, returned_extra, send_sem, recv_sem,
 ):
     dp = lax.axis_index("dp")
@@ -67,7 +67,7 @@
 
     lax.fori_loop(1, N_DP, greet, 0)
 
-    counter = [4 * N_DP]
+    counter = [5 * N_DP]
     started = []
 
     def message(src, dst, device, slot=None):
@@ -87,22 +87,22 @@
 
     top, bottom = pl.ds(0, HALF_ROWS), pl.ds(HALF_ROWS, HALF_ROWS)
 
-    def gather_start(axis, buf):
+    def gather_start(axis, buf, cols):
         p = place[axis]
         right, left = near[axis]
-        a = [send(buf.at[p, h], buf.at[p, h], right) for h in (top, bottom)]
-        b = [send(buf.at[p, h], buf.at[p, h], left) for h in (bottom, top)]
+        a = [send(buf.at[p, h, cols], buf.at[p, h, cols], right) for h in (top, bottom)]
+        b = [send(buf.at[p, h, cols], buf.at[p, h, cols], left) for h in (bottom, top)]
         return a, b
 
-    def gather_pass(axis, buf, state):
+    def gather_pass(axis, buf, state, cols):
         p = place[axis]
         right, left = near[axis]
         a, b = state
         before, after = (p + 3) % RING, (p + 1) % RING
         a[0].wait_recv()
-        f = send(buf.at[before, top], buf.at[before, top], right)
+        f = send(buf.at[before, top, cols], buf.at[before, top, cols], right)
         b[0].wait_recv()
-        g = send(buf.at[after, bottom], buf.at[after, bottom], left)
+        g = send(buf.at[after, bottom, cols], buf.at[after, bottom, cols], left)
         return a[1], b[1], f, g
 
     def gather_end(tail):
@@ -133,24 +133,22 @@
         )
 
     def stage(i, _):
-        rows = pl.ds(pl.multiple_of(i * STEP, 8), STEP)
-        value = jnp.where(slots(i) < my_length, flat_ref[rows], 0.0)
+        value = flat_ref[:, pl.ds(pl.multiple_of(i * STEP * LANES, LANES), STEP * LANES)].astype(jnp.float32).reshape(STEP, LANES)
+        value = jnp.where(slots(i) < my_length, value, 0.0)
         staged[pl.ds(pl.multiple_of(i * STEP + LEAD, 8), STEP)] = pltpu.roll(value, lead_lanes, 1)
         return 0
 
     lax.fori_loop(0, FLAT_ROWS // STEP, stage, 0)
     extra_tmp[...] = jnp.zeros_like(extra_tmp)
 
-    def exchange(o, base, src, src_extra, dst, dst_extra, there):
+    def out_copies(o):
+        there = (dp + o) % N_DP
         device = (there, y, x)
         return (
-            message(src, dst, device, slot=base + o),
-            message(src_extra, dst_extra, device, slot=base + N_DP + o),
+            message(extra.at[there], arrived_extra.at[dp], device, slot=o),
+            message(canvas.at[0, there], arrived.at[0, dp], device, slot=N_DP + o),
+            message(canvas.at[1, there], arrived.at[1, dp], device, slot=2 * N_DP + o),
         )
-
-    def out_copies(o):
-        there = (dp + o) % N_DP
-        return exchange(o, 0, canvas.at[there], extra.at[there], arrived.at[dp], arrived_extra.at[dp], there)
 
     def place_part(o, _):
         there = (dp + o) % N_DP
@@ -162,7 +160,7 @@
         for j in range(4):
             here = staged[pl.ds(start + j, MAIN, stride=CHUNKS)]
             here2 = staged[pl.ds(start + j + MAIN * CHUNKS, 2, stride=CHUNKS)]
-            canvas[there, :, pl.ds(j * LANES, LANES)] = jnp.where(lane >= lead_lanes, here, before).astype(jnp.bfloat16)
+            canvas[j // 2, there, :, pl.ds(j % 2 * LANES, LANES)] = jnp.where(lane >= lead_lanes, here, before).astype(jnp.bfloat16)
             extra_tmp[pl.ds(j * 2, 2)] = jnp.where(lane2 >= lead_lanes, here2, before2)
             before, before2 = here, here2
         extra[there] = extra_tmp[...].astype(jnp.bfloat16)
@@ -172,12 +170,18 @@
     pl.semaphore_wait(barrier, 4 + N_DP - 1)
 
     def send_out(o, _):
-        for copy in out_copies(o):
+        for copy in out_copies(o)[:2]:
             copy.start()
         return 0
 
+    def send_out_more(o, _):
+        out_copies(o)[2].start()
+        return 0
+
     lax.fori_loop(1, N_DP, send_out, 0)
-    arrived[dp] = canvas[dp]
+    lax.fori_loop(1, N_DP, send_out_more, 0)
+    for h in range(2):
+        arrived[h, dp] = canvas[h, dp]
     arrived_extra[dp] = extra[dp]
 
     def targets(length, width, offset, shape, dim):
@@ -193,98 +197,116 @@
     ke, row_e = targets(N_DP * EXTRA, EXTRA, MAIN, (1, N_DP * EXTRA), 1)
     ke = ke % EXTRA
 
-    def wait_out(o, _):
-        for copy in out_copies(o):
-            copy.wait()
-        return 0
-
-    lax.fori_loop(1, N_DP, wait_out, 0)
-    x_main = jnp.dot(pick, arrived[...].reshape(N_DP * MAIN, SLAB), preferred_element_type=jnp.float32)
-    late = arrived_extra[...].reshape(N_DP * EXTRA, LANES)
-    for j in range(4):
-        row_j = jnp.where(ke // 2 == j, row_e - 2 * j, -1)
-        pick_j = (lax.broadcasted_iota(jnp.int32, (GROUP_ROWS, N_DP * EXTRA), 0) == row_j).astype(jnp.float32).astype(jnp.bfloat16)
-        cols = slice(j * LANES, (j + 1) * LANES)
-        x_ref[:, cols] = (
-            x_main[:, cols] + jnp.dot(pick_j, late, preferred_element_type=jnp.float32)
-        ).astype(jnp.bfloat16)
-
+    def land(h):
+        def wait_out(o, _):
+            for copy in out_copies(o)[2 * h : 2 + h]:
+                copy.wait()
+            return 0
+
+        lax.fori_loop(1, N_DP, wait_out, 0)
+        value = jnp.dot(pick, arrived[h].reshape(N_DP * MAIN, HALF_SLAB), preferred_element_type=jnp.float32)
+        late = arrived_extra[...].reshape(N_DP * EXTRA, LANES)
+        parts = []
+        for j in (2 * h, 2 * h + 1):
+            row_j = jnp.where(ke // 2 == j, row_e - 2 * j, -1)
+            pick_j = (lax.broadcasted_iota(jnp.int32, (GROUP_ROWS, N_DP * EXTRA), 0) == row_j).astype(jnp.float32).astype(jnp.bfloat16)
+            parts.append(jnp.dot(pick_j, late, preferred_element_type=jnp.float32))
+        value = (value + jnp.concatenate(parts, axis=1)).astype(jnp.bfloat16)
+        cols = halves[h]
+        x_ref[:, cols] = value
+        xr[x, group_rows, cols] = value
+        xs[y, :, cols] = value
+
+    halves = (pl.ds(0, HALF_SLAB), pl.ds(HALF_SLAB, HALF_SLAB))
+    group_rows = pl.ds(0, GROUP_ROWS)
     pad = pl.ds(GROUP_ROWS, PANEL - GROUP_ROWS)
     for q in range(RING):
         xr[q, pad] = jnp.zeros((PANEL - GROUP_ROWS, SLAB), jnp.bfloat16)
         yb[q, pad] = jnp.zeros((PANEL - GROUP_ROWS, HALF_SLAB), jnp.bfloat16)
     for p in range(2):
-        gh[p, pad] = jnp.zeros((PANEL - GROUP_ROWS, BLOCK), jnp.bfloat16)
-    xr[x, pl.ds(0, GROUP_ROWS)] = x_ref[...]
-    xs[y] = x_ref[...]
-    s1 = gather_start("col", xr)
-    s2 = gather_start("row", xs)
-    t1 = gather_pass("col", xr, s1)
-    t2 = gather_pass("row", xs, s2)
+        to_sib[p, pad] = jnp.zeros((PANEL - GROUP_ROWS, BLOCK), jnp.bfloat16)
+        own_f32[p, pad] = jnp.zeros((PANEL - GROUP_ROWS, BLOCK), jnp.float32)
+
+    def gram(core, h, store):
+        def tile(i, _):
+            rows = pl.ds(pl.multiple_of((i % 2) * HALF_ROWS, 16), HALF_ROWS)
+            value = lax.dot_general(
+                xr[2 * core + i // 2, rows, halves[h]], xs[:, :, halves[h]].reshape(BLOCK, HALF_SLAB),
+                (((1,), (1,)), ((), ())), preferred_element_type=jnp.float32,
+            )
+            store(i // 2, rows, value)
+            return 0
+
+        lax.fori_loop(0, 4, tile, 0)
+
+    def keep_own(p, rows, value):
+        own_f32[p, rows] = value
+
+    def keep_sib(p, rows, value):
+        sib_f32[p, rows] = value
+
+    def add_own(p, rows, value):
+        own_f32[p, rows] += value
+
+    def add_sib(p, rows, value):
+        to_sib[p, rows] = (sib_f32[p, rows] + value).astype(jnp.bfloat16)
+
+    land(0)
+    s1 = gather_start("col", xr, halves[0])
+    s2 = gather_start("row", xs, halves[0])
+    t1 = gather_pass("col", xr, s1, halves[0])
+    t2 = gather_pass("row", xs, s2, halves[0])
+    land(1)
+    s1 = gather_start("col", xr, halves[1])
+    s2 = gather_start("row", xs, halves[1])
     gather_end(t1)
     gather_end(t2)
-
-    base = counter[0]
-    counter[0] += 4
-
-    def sib_message(i):
-        rows = pl.ds(pl.multiple_of(i * HALF_ROWS, 16), HALF_ROWS)
-        return message(to_sib.at[rows], from_sib.at[rows], dev_sib, slot=base + i)
-
-    def gram_tile(half, i):
-        left = xr[2 * half + i // 2, pl.ds(pl.multiple_of((i % 2) * HALF_ROWS, 16), HALF_ROWS)]
-        return lax.dot_general(
-            left, xs[...].reshape(BLOCK, SLAB), (((1,), (1,)), ((), ())), preferred_element_type=jnp.float32
-        )
-
-    def sib_step(i, _):
-        rows = pl.ds(pl.multiple_of(i * HALF_ROWS, 16), HALF_ROWS)
-        to_sib[rows] = gram_tile(1 - c, i).astype(jnp.bfloat16)
-        sib_message(i).start()
-        return 0
-
-    lax.fori_loop(0, 4, sib_step, 0)
-
-    def own_step(i, _):
-        rows = pl.ds(pl.multiple_of(i * HALF_ROWS, 16), HALF_ROWS)
-        own_f32[rows] = gram_tile(c, i)
-        return 0
-
-    lax.fori_loop(0, 4, own_step, 0)
-    def join_step(i, _):
-        rows = pl.ds(pl.multiple_of(i * HALF_ROWS, 16), HALF_ROWS)
-        sib_message(i).wait()
-        part_rows = pl.ds(pl.multiple_of((i % 2) * HALF_ROWS, 16), HALF_ROWS)
-        gh[i // 2, part_rows] = (own_f32[rows] + from_sib[rows].astype(jnp.float32)).astype(jnp.bfloat16)
-        return 0
-
-    lax.fori_loop(0, 4, join_step, 0)
+    gram(1 - c, 0, keep_sib)
+    gram(c, 0, keep_own)
+    t1 = gather_pass("col", xr, s1, halves[1])
+    t2 = gather_pass("row", xs, s2, halves[1])
+    gather_end(t1)
+    gather_end(t2)
+    gram(1 - c, 1, add_sib)
 
     def shard_rows(s):
         return pl.ds(pl.multiple_of(((s + N_Z) % N_Z) * SHARD, 16), SHARD)
 
     f32 = jnp.float32
+    plan = []
+    for k in range(8):
+        distance = 4 - (k + 1) // 2
+        plan.append((True, k % 2, distance))
+        plan.append((False, 1 - k % 2, distance))
+    sib_in = []
+    for upward, panel, distance in plan:
+        rows = shard_rows(z + distance if upward else z - distance)
+        sib_in.append(send(to_sib.at[panel, rows], from_sib.at[panel, rows], dev_sib))
+    gram(c, 1, add_own)
+
     up_in, down_in = [], []
-    for k in range(7):
-        distance = 4 - (k + 1) // 2
-        for upward in (True, False):
-            panel = k % 2 if upward else 1 - k % 2
-            rows = shard_rows(z + distance if upward else z - distance)
-            arrivals, ring, device = (up_in, ring_f, dev_up) if upward else (down_in, ring_b, dev_down)
-            if k < 2:
-                src = gh.at[panel, rows]
-            else:
-                arrivals[k - 2].wait_recv()
-                ring[k - 2] = (ring[k - 2].astype(f32) + gh[panel, rows].astype(f32)).astype(jnp.bfloat16)
-                src = ring.at[k - 2]
-            arrivals.append(send(src, ring.at[k], device))
+    for (upward, panel, distance), arrival in zip(plan, sib_in):
+        rows = shard_rows(z + distance if upward else z - distance)
+        arrival.wait_recv()
+        term = own_f32[panel, rows] + from_sib[panel, rows].astype(f32)
+        if distance == 0:
+            up, down = (6, 5) if panel == 0 else (5, 6)
+            up_in[up].wait_recv()
+            down_in[down].wait_recv()
+            term = term + ring_f[up].astype(f32) + ring_b[down].astype(f32)
+            g_full[2 * c + panel, rows] = term.astype(jnp.bfloat16)
+            continue
+        arrivals, ring, device = (up_in, ring_f, dev_up) if upward else (down_in, ring_b, dev_down)
+        k = len(arrivals)
+        if k < 2:
+            src = gh.at[2 * k + int(upward)]
+        else:
+            arrivals[k - 2].wait_recv()
+            src = ring.at[k - 2]
+            term = term + ring[k - 2].astype(f32)
+        src[...] = term.astype(jnp.bfloat16)
+        arrivals.append(send(src, ring.at[k], device))
     mine = shard_rows(z)
-    for panel, k_up, k_down in ((0, 6, 5), (1, 5, 6)):
-        up_in[k_up].wait_recv()
-        down_in[k_down].wait_recv()
-        g_full[2 * c + panel, mine] = (
-            gh[panel, mine].astype(f32) + ring_f[k_up].astype(f32) + ring_b[k_down].astype(f32)
-        ).astype(jnp.bfloat16)
 
     pending = []
 
@@ -379,10 +401,10 @@
     )
     ya[y] = y_f32[:, :HALF_SLAB].astype(jnp.bfloat16)
     yb[x, pl.ds(0, GROUP_ROWS)] = y_f32[:, HALF_SLAB:].astype(jnp.bfloat16)
-    s1 = gather_start("row", ya)
-    s2 = gather_start("col", yb)
-    t1 = gather_pass("row", ya, s1)
-    t2 = gather_pass("col", yb, s2)
+    s1 = gather_start("row", ya, first)
+    s2 = gather_start("col", yb, first)
+    t1 = gather_pass("row", ya, s1, first)
+    t2 = gather_pass("col", yb, s2, first)
     gather_end(t1)
     gather_end(t2)
 
@@ -397,7 +419,7 @@
 
     _, row_of = targets(N_DP * MAIN, MAIN, 0, (N_DP * MAIN, 1), 0)
     pick = (lax.broadcasted_iota(jnp.int32, (N_DP * MAIN, GROUP_ROWS), 1) == row_of).astype(jnp.float32).astype(jnp.bfloat16)
-    canvas[...] = jnp.dot(pick, update[...], preferred_element_type=jnp.float32).astype(jnp.bfloat16).reshape(N_DP, MAIN, SLAB)
+    outgoing[...] = jnp.dot(pick, update[...], preferred_element_type=jnp.float32).astype(jnp.bfloat16).reshape(N_DP, MAIN, SLAB)
     ke, row_e = targets(N_DP * EXTRA, EXTRA, MAIN, (N_DP * EXTRA, 1), 0)
     ke = ke % EXTRA
     late = jnp.zeros((N_DP * EXTRA, LANES), jnp.float32)
@@ -409,7 +431,11 @@
 
     def back_copies(o):
         there = (dp + o) % N_DP
-        return exchange(o, 2 * N_DP, canvas.at[there], extra.at[there], returned.at[dp], returned_extra.at[dp], there)
+        device = (there, y, x)
+        return (
+            message(outgoing.at[there], returned.at[dp], device, slot=3 * N_DP + o),
+            message(extra.at[there], returned_extra.at[dp], device, slot=4 * N_DP + o),
+        )
 
     def send_back(o, _):
         for copy in back_copies(o):
@@ -417,7 +443,7 @@
         return 0
 
     lax.fori_loop(1, N_DP, send_back, 0)
-    returned[dp] = canvas[dp]
+    returned[dp] = outgoing[dp]
     returned_extra[dp] = extra[dp]
 
     def wait_back(o, _):
@@ -444,7 +470,8 @@
         after = back[pl.ds(i * STEP + lead_rows + 1, STEP)]
         lane = lax.broadcasted_iota(jnp.int32, (STEP, LANES), 1)
         value = jnp.where(lane + lead_lanes < LANES, here, after)
-        out_ref[pl.ds(pl.multiple_of(i * STEP, 8), STEP)] = jnp.where(slots(i) < my_length, value, 0.0)
+        value = jnp.where(slots(i) < my_length, value, 0.0).reshape(1, STEP * LANES)
+        out_ref[:, pl.ds(pl.multiple_of(i * STEP * LANES, LANES), STEP * LANES)] = value.astype(jnp.bfloat16)
         return 0
 
     lax.fori_loop(0, FLAT_ROWS // STEP, finish, 0)
@@ -457,24 +484,26 @@
     vmem = pltpu.VMEM
     return pl.pallas_call(
         core_kernel,
-        out_shape=jax.ShapeDtypeStruct((FLAT_ROWS, LANES), f32),
+        out_shape=jax.ShapeDtypeStruct((1, FLAT_ROWS * LANES), bf),
         in_specs=[pl.BlockSpec(memory_space=pltpu.SMEM), pl.BlockSpec(memory_space=pltpu.VMEM)],
         out_specs=pl.BlockSpec(memory_space=pltpu.VMEM),
         scratch_shapes=[
             vmem((LEAD + FLAT_ROWS + 88, LANES), f32),
+            vmem((2, N_DP, MAIN, HALF_SLAB), bf),
             vmem((N_DP, MAIN, SLAB), bf),
             vmem((EXTRA, LANES), f32),
             vmem((N_DP, EXTRA, LANES), bf),
-            vmem((N_DP, MAIN, SLAB), bf),
+            vmem((2, N_DP, MAIN, HALF_SLAB), bf),
             vmem((N_DP, EXTRA, LANES), bf),
             vmem((34 * CHUNKS + 8, LANES), f32),
             vmem((GROUP_ROWS, SLAB), bf),
             vmem((RING, PANEL, SLAB), bf),
             vmem((RING, GROUP_ROWS, SLAB), bf),
-            vmem((CORE_ROWS, BLOCK), f32),
-            vmem((CORE_ROWS, BLOCK), bf),
-            vmem((CORE_ROWS, BLOCK), bf),
+            vmem((2, PANEL, BLOCK), f32),
+            vmem((2, PANEL, BLOCK), f32),
             vmem((2, PANEL, BLOCK), bf),
+            vmem((2, PANEL, BLOCK), bf),
+            vmem((4, SHARD, BLOCK), bf),
             vmem((7, SHARD, BLOCK), bf),
             vmem((7, SHARD, BLOCK), bf),
             vmem((RING, PANEL, BLOCK), bf),
@@ -502,9 +531,7 @@
 
 
 def local(flat_iterate, lengths):
-    flat = flat_iterate.astype(jnp.float32).reshape(FLAT_ROWS, LANES)
-    new_flat = newton_schulz(lengths, flat).reshape(1, FLAT_ROWS * LANES)
-    return lax.optimization_barrier(new_flat).astype(jnp.bfloat16)
+    return newton_schulz(lengths, flat_iterate)
 
 
 def solution(mesh):

time: 155 us -> 151 us (0.974)
  other arithmetic: 6.92 us -> 0 us
  local copies, waits for them, and re-layouts: 0 us -> 3.59 us
    unnamed x0 -> x1, local copies, waits for them, and re-layouts: none -> 3.59 us
    reshape x1 -> x0, other arithmetic: 3.58 us -> none  [local(): flat = flat_iterate.astype(jnp.float32).reshape(FLAT_ROWS, LANES)]
    convert_element_type x1 -> x0, other arithmetic: 3.34 us -> none  [local(): return lax.optimization_barrier(new_flat).astype(jnp.bfloat16)]
where the time goes in v4:
time: 151 us
  Pallas kernels  147 us (97%)
  local copies, waits for them, and re-layouts  3.59 us (2%)
    pallas_call x1, Pallas kernels, newton_schulz(): pl.pallas_call(core_kernel, out_shape=jax.ShapeDtypeStruct((1, FLAT_ROWS...  147 us
    unnamed x1, local copies, waits for them, and re-layouts  3.59 us

profile of v4, /device:TPU:1, one launch (start us, length us, event | category | flops | bytes accessed | tf_op | source)
XLA Modules:
  0.0 150.5 jit_solution(1669825842754916965)
XLA Ops:
  0.0 146.9 %shard_map.28 = bf16[1,270336]{1,0:T(2,128)(2,1)} custom-call(s32[16,16]{1,0:T(8,128)} %lengths_ref.1, bf16[1,270336]{1,0:T(2,128)(2,1)} %flat_ref.1), custom_call_target="tpu_custom_call" | custom-call | tf_op jit(solution)/shard_map/pallas_call | solution.py:485
  146.9 3.6 %copy.4 = bf16[1,270336]{1,0:T(2,128)(2,1)} copy(bf16[1,270336]{1,0:T(2,128)(2,1)} %shard_map.28) | data formatting | bytes 1081344

commit v5 on v4

--- a/solution.py
+++ b/solution.py
@@ -32,14 +32,23 @@
 MAIN = 32
 EXTRA = 16
 LEAD = 72
+STEP = 176
 N_MESSAGES = 256
 MESH = pl.DeviceIdType.MESH
 SCALE = 0.2 * math.sqrt(max(ROWS, COLS))
 
 
+def slots(i):
+    return (
+        i * (STEP * LANES)
+        + lax.broadcasted_iota(jnp.int32, (STEP, LANES), 0) * LANES
+        + lax.broadcasted_iota(jnp.int32, (STEP, LANES), 1)
+    )
+
+
 def core_kernel(
-    lengths_ref, flat_ref, out_ref, staged, canvas, outgoing, extra_tmp, extra, arrived, arrived_extra, back, x_ref, xr, xs, own_f32, sib_f32, to_sib, from_sib, gh, ring_f, ring_b, g_full,
-    part, got_a, got_b, got_c, got_d, y_f32, ya, yb, part2, z_b, z_f32, update, returned, returned_extra, send_sem, recv_sem,
+    lengths_ref, flat_ref, returned, returned_extra, staged, canvas, outgoing, extra_tmp, extra, arrived, arrived_extra, x_ref, xr, xs, own_f32, sib_f32, to_sib, from_sib, gh, ring_f, ring_b, g_full,
+    part, got_a, got_b, got_c, got_d, y_f32, ya, yb, part2, z_b, z_f32, update, send_sem, recv_sem,
 ):
     dp = lax.axis_index("dp")
     y = lax.axis_index("row")
@@ -67,7 +76,7 @@
 
     lax.fori_loop(1, N_DP, greet, 0)
 
-    counter = [5 * N_DP]
+    counter = [6 * N_DP]
     started = []
 
     def message(src, dst, device, slot=None):
@@ -87,22 +96,22 @@
 
     top, bottom = pl.ds(0, HALF_ROWS), pl.ds(HALF_ROWS, HALF_ROWS)
 
-    def gather_start(axis, buf, cols):
+    def gather_start(axis, buf):
         p = place[axis]
         right, left = near[axis]
-        a = [send(buf.at[p, h, cols], buf.at[p, h, cols], right) for h in (top, bottom)]
-        b = [send(buf.at[p, h, cols], buf.at[p, h, cols], left) for h in (bottom, top)]
+        a = [send(buf.at[p, h], buf.at[p, h], right) for h in (top, bottom)]
+        b = [send(buf.at[p, h], buf.at[p, h], left) for h in (bottom, top)]
         return a, b
 
-    def gather_pass(axis, buf, state, cols):
+    def gather_pass(axis, buf, state):
         p = place[axis]
         right, left = near[axis]
         a, b = state
         before, after = (p + 3) % RING, (p + 1) % RING
         a[0].wait_recv()
-        f = send(buf.at[before, top, cols], buf.at[before, top, cols], right)
+        f = send(buf.at[before, top], buf.at[before, top], right)
         b[0].wait_recv()
-        g = send(buf.at[after, bottom, cols], buf.at[after, bottom, cols], left)
+        g = send(buf.at[after, bottom], buf.at[after, bottom], left)
         return a[1], b[1], f, g
 
     def gather_end(tail):
@@ -123,14 +132,6 @@
     staged[pl.ds(0, LEAD)] = jnp.zeros((LEAD, LANES), jnp.float32)
     tail_rows = staged.shape[0] - LEAD - FLAT_ROWS
     staged[pl.ds(LEAD + FLAT_ROWS, tail_rows)] = jnp.zeros((tail_rows, LANES), jnp.float32)
-    STEP = 176
-
-    def slots(i):
-        return (
-            i * (STEP * LANES)
-            + lax.broadcasted_iota(jnp.int32, (STEP, LANES), 0) * LANES
-            + lax.broadcasted_iota(jnp.int32, (STEP, LANES), 1)
-        )
 
     def stage(i, _):
         value = flat_ref[:, pl.ds(pl.multiple_of(i * STEP * LANES, LANES), STEP * LANES)].astype(jnp.float32).reshape(STEP, LANES)
@@ -212,16 +213,16 @@
             pick_j = (lax.broadcasted_iota(jnp.int32, (GROUP_ROWS, N_DP * EXTRA), 0) == row_j).astype(jnp.float32).astype(jnp.bfloat16)
             parts.append(jnp.dot(pick_j, late, preferred_element_type=jnp.float32))
         value = (value + jnp.concatenate(parts, axis=1)).astype(jnp.bfloat16)
-        cols = halves[h]
-        x_ref[:, cols] = value
-        xr[x, group_rows, cols] = value
-        xs[y, :, cols] = value
+        x_ref[:, halves[h]] = value
+        xr[h, x, group_rows] = value
+        xs[h, y] = value
 
     halves = (pl.ds(0, HALF_SLAB), pl.ds(HALF_SLAB, HALF_SLAB))
     group_rows = pl.ds(0, GROUP_ROWS)
     pad = pl.ds(GROUP_ROWS, PANEL - GROUP_ROWS)
     for q in range(RING):
-        xr[q, pad] = jnp.zeros((PANEL - GROUP_ROWS, SLAB), jnp.bfloat16)
+        for h in range(2):
+            xr[h, q, pad] = jnp.zeros((PANEL - GROUP_ROWS, HALF_SLAB), jnp.bfloat16)
         yb[q, pad] = jnp.zeros((PANEL - GROUP_ROWS, HALF_SLAB), jnp.bfloat16)
     for p in range(2):
         to_sib[p, pad] = jnp.zeros((PANEL - GROUP_ROWS, BLOCK), jnp.bfloat16)
@@ -231,7 +232,7 @@
         def tile(i, _):
             rows = pl.ds(pl.multiple_of((i % 2) * HALF_ROWS, 16), HALF_ROWS)
             value = lax.dot_general(
-                xr[2 * core + i // 2, rows, halves[h]], xs[:, :, halves[h]].reshape(BLOCK, HALF_SLAB),
+                xr[h, 2 * core + i // 2, rows], xs[h].reshape(BLOCK, HALF_SLAB),
                 (((1,), (1,)), ((), ())), preferred_element_type=jnp.float32,
             )
             store(i // 2, rows, value)
@@ -252,21 +253,19 @@
         to_sib[p, rows] = (sib_f32[p, rows] + value).astype(jnp.bfloat16)
 
     land(0)
-    s1 = gather_start("col", xr, halves[0])
-    s2 = gather_start("row", xs, halves[0])
-    t1 = gather_pass("col", xr, s1, halves[0])
-    t2 = gather_pass("row", xs, s2, halves[0])
+    a0 = gather_start("col", xr.at[0])
+    b0 = gather_start("row", xs.at[0])
+    a0 = gather_pass("col", xr.at[0], a0)
+    b0 = gather_pass("row", xs.at[0], b0)
     land(1)
-    s1 = gather_start("col", xr, halves[1])
-    s2 = gather_start("row", xs, halves[1])
-    gather_end(t1)
-    gather_end(t2)
+    a1 = gather_start("col", xr.at[1])
+    b1 = gather_start("row", xs.at[1])
+    gather_end(a0 + b0)
     gram(1 - c, 0, keep_sib)
+    a1 = gather_pass("col", xr.at[1], a1)
+    b1 = gather_pass("row", xs.at[1], b1)
     gram(c, 0, keep_own)
-    t1 = gather_pass("col", xr, s1, halves[1])
-    t2 = gather_pass("row", xs, s2, halves[1])
-    gather_end(t1)
-    gather_end(t2)
+    gather_end(a1 + b1)
     gram(1 - c, 1, add_sib)
 
     def shard_rows(s):
@@ -360,90 +359,113 @@
         return (c2, d2)
 
     first, second = pl.ds(0, HALF_SLAB), pl.ds(HALF_SLAB, HALF_SLAB)
-
-    def apply_gram(right_a, right_b, buf, total):
-        def make(q):
-            return jnp.dot(g_full[q, pl.ds(0, GROUP_ROWS)], right_a(), preferred_element_type=f32)
-
-        far, after, before = (x + 2) % RING, (x + 1) % RING, (x + 3) % RING
-        buf_a, buf_b = buf.at[0], buf.at[1]
-        slots = [[r.at[i] for r in (got_a, got_b, got_c, got_d)] for i in range(2)]
-        buf_a[far] = make(far).astype(jnp.bfloat16)
-        sa = reduce_start("col", buf_a, *slots[0][:2])
-
+    slots_a, slots_b, slots_a2, slots_b2 = [[r.at[i] for r in (got_a, got_b, got_c, got_d)] for i in range(4)]
+    far, after, before = (x + 2) % RING, (x + 1) % RING, (x + 3) % RING
+
+    def times(q, right):
+        return jnp.dot(g_full[q, group_rows], right, preferred_element_type=f32)
+
+    def open_a(buf, right, slots):
+        buf[far] = times(far, right()).astype(jnp.bfloat16)
+        state = reduce_start("col", buf, *slots[:2])
+        buf[after] = times(after, right()).astype(jnp.bfloat16)
+        buf[before] = times(before, right()).astype(jnp.bfloat16)
+        near_copies = reduce_near("col", buf, *slots[2:])
+        return state, near_copies
+
+    def open_b(buf, right, slots):
         def columns(j, _):
             cols = pl.ds(pl.multiple_of(j * LANES, LANES), LANES)
             z_b[cols] = lax.dot_general(
-                g_full[:, :, cols].reshape(RING * PANEL, LANES), right_b(), (((0,), (0,)), ((), ())),
+                g_full[:, :, cols].reshape(RING * PANEL, LANES), right, (((0,), (0,)), ((), ())),
                 preferred_element_type=f32,
             )
             return 0
 
         lax.fori_loop(0, BLOCK // LANES, columns, 0)
-        buf_b[...] = z_b[...].astype(jnp.bfloat16).reshape(RING, GROUP_ROWS, HALF_SLAB)
-        sb = reduce_start("row", buf_b, *slots[1][:2])
-        nb = reduce_near("row", buf_b, *slots[1][2:])
-        buf_a[after] = make(after).astype(jnp.bfloat16)
-        buf_a[before] = make(before).astype(jnp.bfloat16)
-        na = reduce_near("col", buf_a, *slots[0][2:])
-        pa = reduce_pass("col", buf_a, *slots[0], sa)
-        pb = reduce_pass("row", buf_b, *slots[1], sb)
-        total[:, first] = make(x)
+        buf[...] = z_b[...].astype(jnp.bfloat16).reshape(RING, GROUP_ROWS, HALF_SLAB)
+        state = reduce_start("row", buf, *slots[:2])
+        return state, reduce_near("row", buf, *slots[2:])
+
+    def pass_on(axis, buf, slots, opened):
+        return opened[1] + reduce_pass(axis, buf, *slots, opened[0])
+
+    def close(tail, slots, total, cols):
+        gather_end(tail)
+        total[:, cols] = total[:, cols] + slots[2][...].astype(f32) + slots[3][...].astype(f32)
+
+    def own_b(total):
         total[:, second] = z_b[pl.ds(pl.multiple_of(y * GROUP_ROWS, 8), GROUP_ROWS)]
-        for i, (cols, tail) in enumerate(((first, na + pa), (second, nb + pb))):
-            gather_end(tail)
-            total[:, cols] = total[:, cols] + got_c[i].astype(f32) + got_d[i].astype(f32)
-
-    apply_gram(
-        lambda: xs[:, :, :HALF_SLAB].reshape(BLOCK, HALF_SLAB),
-        lambda: xr[:, :, HALF_SLAB:].reshape(RING * PANEL, HALF_SLAB),
-        part, y_f32,
-    )
-    ya[y] = y_f32[:, :HALF_SLAB].astype(jnp.bfloat16)
-    yb[x, pl.ds(0, GROUP_ROWS)] = y_f32[:, HALF_SLAB:].astype(jnp.bfloat16)
-    s1 = gather_start("row", ya, first)
-    s2 = gather_start("col", yb, first)
-    t1 = gather_pass("row", ya, s1, first)
-    t2 = gather_pass("col", yb, s2, first)
-    gather_end(t1)
-    gather_end(t2)
-
-    apply_gram(
-        lambda: ya[...].reshape(BLOCK, HALF_SLAB),
-        lambda: yb[...].reshape(RING * PANEL, HALF_SLAB),
-        part2, z_f32,
-    )
-    update[...] = (
-        SCALE * (LINEAR_COEF * x_ref[...].astype(f32) + (CUBIC_COEF * y_f32[...] + QUINTIC_COEF * z_f32[...]))
-    ).astype(jnp.bfloat16)
+
+    oa = open_a(part.at[0], lambda: xs[0].reshape(BLOCK, HALF_SLAB), slots_a)
+    ob = open_b(part.at[1], xr[1].reshape(RING * PANEL, HALF_SLAB), slots_b)
+    y_f32[:, first] = times(x, xs[0].reshape(BLOCK, HALF_SLAB))
+    own_b(y_f32)
+    oa = pass_on("col", part.at[0], slots_a, oa)
+    ob = pass_on("row", part.at[1], slots_b, ob)
+    close(oa, slots_a, y_f32, first)
+    ya[y] = y_f32[:, first].astype(jnp.bfloat16)
+    sa = gather_start("row", ya)
+    close(ob, slots_b, y_f32, second)
+    yb[x, group_rows] = y_f32[:, second].astype(jnp.bfloat16)
+    sb = gather_start("col", yb)
+    sa = gather_pass("row", ya, sa)
+    sb = gather_pass("col", yb, sb)
+    gather_end(sa)
+
+    oa = open_a(part2.at[0], lambda: ya[...].reshape(BLOCK, HALF_SLAB), slots_a2)
+    gather_end(sb)
+    ob = open_b(part2.at[1], yb[...].reshape(RING * PANEL, HALF_SLAB), slots_b2)
+    z_f32[:, first] = times(x, ya[...].reshape(BLOCK, HALF_SLAB))
+    own_b(z_f32)
+    oa = pass_on("col", part2.at[0], slots_a2, oa)
+    ob = pass_on("row", part2.at[1], slots_b2, ob)
 
     _, row_of = targets(N_DP * MAIN, MAIN, 0, (N_DP * MAIN, 1), 0)
-    pick = (lax.broadcasted_iota(jnp.int32, (N_DP * MAIN, GROUP_ROWS), 1) == row_of).astype(jnp.float32).astype(jnp.bfloat16)
-    outgoing[...] = jnp.dot(pick, update[...], preferred_element_type=jnp.float32).astype(jnp.bfloat16).reshape(N_DP, MAIN, SLAB)
+    pick = (lax.broadcasted_iota(jnp.int32, (N_DP * MAIN, GROUP_ROWS), 1) == row_of).astype(f32).astype(jnp.bfloat16)
     ke, row_e = targets(N_DP * EXTRA, EXTRA, MAIN, (N_DP * EXTRA, 1), 0)
     ke = ke % EXTRA
-    late = jnp.zeros((N_DP * EXTRA, LANES), jnp.float32)
-    for j in range(4):
-        row_j = jnp.where(ke // 2 == j, row_e - 2 * j, -1)
-        pick_j = (lax.broadcasted_iota(jnp.int32, (N_DP * EXTRA, GROUP_ROWS), 1) == row_j).astype(jnp.float32).astype(jnp.bfloat16)
-        late += jnp.dot(pick_j, update[:, j * LANES : (j + 1) * LANES], preferred_element_type=jnp.float32)
-    extra[...] = late.astype(jnp.bfloat16).reshape(N_DP, EXTRA, LANES)
 
     def back_copies(o):
         there = (dp + o) % N_DP
         device = (there, y, x)
         return (
-            message(outgoing.at[there], returned.at[dp], device, slot=3 * N_DP + o),
-            message(extra.at[there], returned_extra.at[dp], device, slot=4 * N_DP + o),
+            message(outgoing.at[0, there], returned.at[0, dp], device, slot=3 * N_DP + o),
+            message(outgoing.at[1, there], returned.at[1, dp], device, slot=4 * N_DP + o),
+            message(extra.at[there], returned_extra.at[dp], device, slot=5 * N_DP + o),
         )
 
-    def send_back(o, _):
-        for copy in back_copies(o):
-            copy.start()
-        return 0
-
-    lax.fori_loop(1, N_DP, send_back, 0)
-    returned[dp] = outgoing[dp]
+    def leave(h, cols):
+        update[:, cols] = (
+            SCALE * (LINEAR_COEF * x_ref[:, cols].astype(f32) + (CUBIC_COEF * y_f32[:, cols] + QUINTIC_COEF * z_f32[:, cols]))
+        ).astype(jnp.bfloat16)
+        outgoing[h] = (
+            jnp.dot(pick, update[:, cols], preferred_element_type=f32).astype(jnp.bfloat16).reshape(N_DP, MAIN, HALF_SLAB)
+        )
+
+        def send_back(o, _):
+            back_copies(o)[h].start()
+            return 0
+
+        lax.fori_loop(1, N_DP, send_back, 0)
+        returned[h, dp] = outgoing[h, dp]
+
+    close(oa, slots_a2, z_f32, first)
+    leave(0, first)
+    close(ob, slots_b2, z_f32, second)
+    leave(1, second)
+    late = jnp.zeros((N_DP * EXTRA, LANES), f32)
+    for j in range(4):
+        row_j = jnp.where(ke // 2 == j, row_e - 2 * j, -1)
+        pick_j = (lax.broadcasted_iota(jnp.int32, (N_DP * EXTRA, GROUP_ROWS), 1) == row_j).astype(f32).astype(jnp.bfloat16)
+        late += jnp.dot(pick_j, update[:, j * LANES : (j + 1) * LANES], preferred_element_type=f32)
+    extra[...] = late.astype(jnp.bfloat16).reshape(N_DP, EXTRA, LANES)
+
+    def send_extra(o, _):
+        back_copies(o)[2].start()
+        return 0
+
+    lax.fori_loop(1, N_DP, send_extra, 0)
     returned_extra[dp] = extra[dp]
 
     def wait_back(o, _):
@@ -452,14 +474,27 @@
         return 0
 
     lax.fori_loop(1, N_DP, wait_back, 0)
+    for copy in started:
+        copy.wait_send()
+
+
+def finish_kernel(lengths_ref, returned, returned_extra, out_ref, back, extra_tmp):
+    dp = lax.axis_index("dp")
+    group = lax.axis_index("row") * RING + lax.axis_index("col")
+    my_start = jnp.int32(0)
+    for d in range(N_DP):
+        my_start = my_start + jnp.where(d < dp, lengths_ref[group, d], 0)
+    my_length = lengths_ref[group, dp]
+    lead = my_start % COLS
+    lead_rows, lead_lanes = lead // LANES, lead % LANES
+    turn = (LANES - lead_lanes) % LANES
 
     def unpack(d, _):
-        extra_tmp[...] = returned_extra[d].astype(jnp.float32)
+        extra_tmp[...] = pltpu.roll(returned_extra[d].astype(jnp.float32), turn, 1)
         for j in range(4):
             back[pl.ds(d * 4 + j, MAIN, stride=CHUNKS)] = pltpu.roll(
-                returned[d, :, pl.ds(j * LANES, LANES)].astype(jnp.float32), (LANES - lead_lanes) % LANES, 1)
-            back[pl.ds(d * 4 + j + MAIN * CHUNKS, 2, stride=CHUNKS)] = pltpu.roll(
-                extra_tmp[...], (LANES - lead_lanes) % LANES, 1)[2 * j : 2 * j + 2]
+                returned[j // 2, d, :, pl.ds(j % 2 * LANES, LANES)].astype(jnp.float32), turn, 1)
+            back[pl.ds(d * 4 + j + MAIN * CHUNKS, 2, stride=CHUNKS)] = extra_tmp[2 * j : 2 * j + 2]
         return 0
 
     lax.fori_loop(0, N_DP, unpack, 0)
@@ -475,30 +510,30 @@
         return 0
 
     lax.fori_loop(0, FLAT_ROWS // STEP, finish, 0)
-    for copy in started:
-        copy.wait_send()
 
 
 def newton_schulz(lengths, flat):
     bf, f32 = jnp.bfloat16, jnp.float32
     vmem = pltpu.VMEM
-    return pl.pallas_call(
+    returned, returned_extra = pl.pallas_call(
         core_kernel,
-        out_shape=jax.ShapeDtypeStruct((1, FLAT_ROWS * LANES), bf),
+        out_shape=(
+            jax.ShapeDtypeStruct((2, N_DP, MAIN, HALF_SLAB), bf),
+            jax.ShapeDtypeStruct((N_DP, EXTRA, LANES), bf),
+        ),
         in_specs=[pl.BlockSpec(memory_space=pltpu.SMEM), pl.BlockSpec(memory_space=pltpu.VMEM)],
-        out_specs=pl.BlockSpec(memory_space=pltpu.VMEM),
+        out_specs=[pl.BlockSpec(memory_space=pltpu.VMEM)] * 2,
         scratch_shapes=[
             vmem((LEAD + FLAT_ROWS + 88, LANES), f32),
             vmem((2, N_DP, MAIN, HALF_SLAB), bf),
-            vmem((N_DP, MAIN, SLAB), bf),
+            vmem((2, N_DP, MAIN, HALF_SLAB), bf),
             vmem((EXTRA, LANES), f32),
             vmem((N_DP, EXTRA, LANES), bf),
             vmem((2, N_DP, MAIN, HALF_SLAB), bf),
             vmem((N_DP, EXTRA, LANES), bf),
-            vmem((34 * CHUNKS + 8, LANES), f32),
             vmem((GROUP_ROWS, SLAB), bf),
-            vmem((RING, PANEL, SLAB), bf),
-            vmem((RING, GROUP_ROWS, SLAB), bf),
+            vmem((2, RING, PANEL, HALF_SLAB), bf),
+            vmem((2, RING, GROUP_ROWS, HALF_SLAB), bf),
             vmem((2, PANEL, BLOCK), f32),
             vmem((2, PANEL, BLOCK), f32),
             vmem((2, PANEL, BLOCK), bf),
@@ -508,10 +543,10 @@
             vmem((7, SHARD, BLOCK), bf),
             vmem((RING, PANEL, BLOCK), bf),
             vmem((2, RING, GROUP_ROWS, HALF_SLAB), bf),
-            vmem((2, HALF_ROWS, HALF_SLAB), bf),
-            vmem((2, HALF_ROWS, HALF_SLAB), bf),
-            vmem((2, GROUP_ROWS, HALF_SLAB), bf),
-            vmem((2, GROUP_ROWS, HALF_SLAB), bf),
+            vmem((4, HALF_ROWS, HALF_SLAB), bf),
+            vmem((4, HALF_ROWS, HALF_SLAB), bf),
+            vmem((4, GROUP_ROWS, HALF_SLAB), bf),
+            vmem((4, GROUP_ROWS, HALF_SLAB), bf),
             vmem((GROUP_ROWS, SLAB), f32),
             vmem((RING, GROUP_ROWS, HALF_SLAB), bf),
             vmem((RING, PANEL, HALF_SLAB), bf),
@@ -519,8 +554,6 @@
             vmem((BLOCK, HALF_SLAB), f32),
             vmem((GROUP_ROWS, SLAB), f32),
             vmem((GROUP_ROWS, SLAB), bf),
-            vmem((N_DP, MAIN, SLAB), bf),
-            vmem((N_DP, EXTRA, LANES), bf),
             pltpu.SemaphoreType.DMA((N_MESSAGES,)),
             pltpu.SemaphoreType.DMA((N_MESSAGES,)),
         ],
@@ -528,6 +561,14 @@
             collective_id=0, has_side_effects=True, vmem_limit_bytes=56 * 1024 * 1024
         ),
     )(lengths, flat)
+    return pl.pallas_call(
+        finish_kernel,
+        out_shape=jax.ShapeDtypeStruct((1, FLAT_ROWS * LANES), bf),
+        in_specs=[pl.BlockSpec(memory_space=pltpu.SMEM)] + [pl.BlockSpec(memory_space=pltpu.VMEM)] * 2,
+        out_specs=pl.BlockSpec(memory_space=pltpu.VMEM),
+        scratch_shapes=[vmem((34 * CHUNKS + 8, LANES), f32), vmem((EXTRA, LANES), f32)],
+        compiler_params=pltpu.CompilerParams(vmem_limit_bytes=32 * 1024 * 1024),
+    )(lengths, returned, returned_extra)
 
 
 def local(flat_iterate, lengths):

time: 151 us -> 147 us (0.974)
  Pallas kernels: 147 us -> 145 us
  local copies, waits for them, and re-layouts: 3.59 us -> 1.88 us
    pallas_call x1 -> x2, Pallas kernels: 147 us -> 145 us  [the longest x1 140 us: newton_schulz(): pl.pallas_call(core_kernel, out_shape=(jax.ShapeDtypeStruct((2, N_DP, MAI...]
    unnamed x1 -> x6, local copies, waits for them, and re-layouts: 3.59 us -> 1.88 us
where the time goes in v5:
time: 147 us; the launch traced here: 146 us
  Pallas kernels  145 us (99%)
  local copies, waits for them, and re-layouts  1.88 us (1%)
    pallas_call x1, Pallas kernels, newton_schulz(): pl.pallas_call(core_kernel, out_shape=(jax.ShapeDtypeStruct((2, N_DP, MAI...  140 us
    pallas_call x1, Pallas kernels, newton_schulz(): pl.pallas_call(finish_kernel, out_shape=jax.ShapeDtypeStruct((1, FLAT_ROW...  4.94 us

profile of v5, /device:TPU:1, one launch (start us, length us, event | category | flops | bytes accessed | tf_op | source)
XLA Modules:
  0.0 146.5 jit_solution(229540476436650800)
XLA Ops:
  0.0 0.0 copy-start.2
  0.0 139.6 %shard_map.28 = (bf16[2,16,32,256]{3,2,1,0:T(8,128)(2,1)}, bf16[16,16,128]{2,1,0:T(8,128)(2,1)}) custom-call(s32[16,16]{1,0:T(8,128)} %lengths_ref.3, bf16[1,270336]{1,0:T(2,128)(2,1)} %flat_ref.1), custom_call_target="tpu_custom_call" | custom-call | tf_op jit(solution)/shard_map/pallas_call | solution.py:518
  139.6 0.0 copy-done.2
  139.6 0.0 copy-start
  139.7 1.0 copy-done
  140.7 0.0 copy-start.1
  140.7 0.8 copy-done.1
  141.5 4.9 %shard_map.29 = bf16[1,270336]{1,0:T(2,128)(2,1)} custom-call(s32[16,16]{1,0:T(8,128)S(1)} %copy-done.2, bf16[2,16,32,256]{3,2,1,0:T(8,128)(2,1)S(1)} %copy-done, bf16[16,16,128]{2,1,0:T(8,128)(2,1)S(1)} %copy-done.1), custom_call_target="tpu_custom_call" | custom-call | tf_op jit(solution)/shard_map/pallas_call | solution.py:564
Async XLA Ops:
  0.0 139.6 %copy-start.2 = (s32[16,16]{1,0:T(8,128)S(1)}, s32[16,16]{1,0:T(8,128)}, u32[]{:S(2)}) copy-start(s32[16,16]{1,0:T(8,128)} %lengths_ref.3) | copy-start | bytes 3076
  139.6 1.0 copy-start
  140.7 0.8 copy-start.1

commit v6 on v5

--- a/solution.py
+++ b/solution.py
@@ -33,7 +33,7 @@
 EXTRA = 16
 LEAD = 72
 STEP = 176
-N_MESSAGES = 256
+N_MESSAGES = 320
 MESH = pl.DeviceIdType.MESH
 SCALE = 0.2 * math.sqrt(max(ROWS, COLS))
 
@@ -48,7 +48,7 @@
 
 def core_kernel(
     lengths_ref, flat_ref, returned, returned_extra, staged, canvas, outgoing, extra_tmp, extra, arrived, arrived_extra, x_ref, xr, xs, own_f32, sib_f32, to_sib, from_sib, gh, ring_f, ring_b, g_full,
-    part, got_a, got_b, got_c, got_d, y_f32, ya, yb, part2, z_b, z_f32, update, send_sem, recv_sem,
+    part, got_a, got_b, got_c, got_d, y_f32, ya, yb, y_tmp, y_out, y_in, y_own, z_b, z_f32, update, send_sem, recv_sem,
 ):
     dp = lax.axis_index("dp")
     y = lax.axis_index("row")
@@ -76,6 +76,9 @@
 
     lax.fori_loop(1, N_DP, greet, 0)
 
+    def by_distance(i):
+        return N_DP // 2 + (i + 1) // 2 * (1 - 2 * (i % 2))
+
     counter = [6 * N_DP]
     started = []
 
@@ -170,17 +173,17 @@
     lax.fori_loop(1, N_DP + 1, place_part, 0)
     pl.semaphore_wait(barrier, 4 + N_DP - 1)
 
-    def send_out(o, _):
-        for copy in out_copies(o)[:2]:
+    def send_out(i, _):
+        for copy in out_copies(by_distance(i))[:2]:
             copy.start()
         return 0
 
-    def send_out_more(o, _):
-        out_copies(o)[2].start()
-        return 0
-
-    lax.fori_loop(1, N_DP, send_out, 0)
-    lax.fori_loop(1, N_DP, send_out_more, 0)
+    def send_out_more(i, _):
+        out_copies(by_distance(i))[2].start()
+        return 0
+
+    lax.fori_loop(0, N_DP - 1, send_out, 0)
+    lax.fori_loop(0, N_DP - 1, send_out_more, 0)
     for h in range(2):
         arrived[h, dp] = canvas[h, dp]
     arrived_extra[dp] = extra[dp]
@@ -223,7 +226,6 @@
     for q in range(RING):
         for h in range(2):
             xr[h, q, pad] = jnp.zeros((PANEL - GROUP_ROWS, HALF_SLAB), jnp.bfloat16)
-        yb[q, pad] = jnp.zeros((PANEL - GROUP_ROWS, HALF_SLAB), jnp.bfloat16)
     for p in range(2):
         to_sib[p, pad] = jnp.zeros((PANEL - GROUP_ROWS, BLOCK), jnp.bfloat16)
         own_f32[p, pad] = jnp.zeros((PANEL - GROUP_ROWS, BLOCK), jnp.float32)
@@ -255,15 +257,15 @@
     land(0)
     a0 = gather_start("col", xr.at[0])
     b0 = gather_start("row", xs.at[0])
-    a0 = gather_pass("col", xr.at[0], a0)
-    b0 = gather_pass("row", xs.at[0], b0)
     land(1)
     a1 = gather_start("col", xr.at[1])
     b1 = gather_start("row", xs.at[1])
+    a0 = gather_pass("col", xr.at[0], a0)
+    b0 = gather_pass("row", xs.at[0], b0)
+    a1 = gather_pass("col", xr.at[1], a1)
+    b1 = gather_pass("row", xs.at[1], b1)
     gather_end(a0 + b0)
     gram(1 - c, 0, keep_sib)
-    a1 = gather_pass("col", xr.at[1], a1)
-    b1 = gather_pass("row", xs.at[1], b1)
     gram(c, 0, keep_own)
     gather_end(a1 + b1)
     gram(1 - c, 1, add_sib)
@@ -307,11 +309,40 @@
         arrivals.append(send(src, ring.at[k], device))
     mine = shard_rows(z)
 
-    pending = []
+    sib_parts = {}
 
     def relay(panel, rows, device):
         ref = g_full.at[2 * c + panel, rows]
         return send(ref, ref, device)
+
+    y_sums, y_left, y_right = {}, [], []
+    order = (0, -1, 1, -2, 2, -3, 3, 4)
+
+    def multiply(shift):
+        i, rows = order.index(shift), shard_rows(z + shift)
+        for copy in sib_parts[shift]:
+            copy.wait_recv()
+        left = g_full[:, rows, :].reshape(RING * SHARD, BLOCK)
+        for h in range(2):
+            value = jnp.dot(left, xs[h].reshape(BLOCK, HALF_SLAB), preferred_element_type=f32)
+            y_tmp[:, :, halves[h]] = value.reshape(RING, SHARD, HALF_SLAB)
+        y_out[i] = y_tmp[...].astype(jnp.bfloat16)
+        y_sums[shift] = [
+            send(y_out.at[i, (x + o) % RING], y_in.at[i, o - 1], (dp, y, (x + o) % RING)) for o in (2, 1, 3)
+        ]
+        y_own[i] = y_tmp[x]
+
+    def add_up(shift):
+        i, rows = order.index(shift), shard_rows(z + shift)
+        for copy in y_sums[shift]:
+            copy.wait_recv()
+        value = y_own[i] + y_in[i, 0].astype(f32) + y_in[i, 1].astype(f32) + y_in[i, 2].astype(f32)
+        y_f32[rows] = value
+        ya[y, rows] = value[:, :HALF_SLAB].astype(jnp.bfloat16)
+        yb[x, rows] = value[:, HALF_SLAB:].astype(jnp.bfloat16)
+        for o in (2, 1, 3):
+            y_left.append(send(ya.at[y, rows], ya.at[y, rows], (dp, (y + o) % RING, x)))
+            y_right.append(send(yb.at[x, rows], yb.at[x, rows], (dp, y, (x + o) % RING)))
 
     up_in, down_in = [], []
     for k in range(9):
@@ -325,11 +356,13 @@
             down_in[k - 2].wait_recv()
         if k < 7:
             down_in.append(relay(*down_part, dev_down))
-        pending.append(relay(*up_part, dev_sib))
+        sib_parts.setdefault(4 if k == 8 else -back_by, []).append(relay(*up_part, dev_sib))
         if k >= 2:
-            pending.append(relay(*down_part, dev_sib))
-    for copy in pending:
-        copy.wait_recv()
+            sib_parts.setdefault(back_by, []).append(relay(*down_part, dev_sib))
+        for shift in {2: (0,), 4: (-1, 1), 6: (-2, 2), 7: (-3, 3), 8: (4,)}.get(k, ()):
+            multiply(shift)
+        for shift in {5: (0,), 6: (-1, 1), 8: (-2, 2, -3, 3, 4)}.get(k, ()):
+            add_up(shift)
 
     def reduce_start(axis, buf, a_ref, b_ref):
         p = place[axis]
@@ -359,7 +392,7 @@
         return (c2, d2)
 
     first, second = pl.ds(0, HALF_SLAB), pl.ds(HALF_SLAB, HALF_SLAB)
-    slots_a, slots_b, slots_a2, slots_b2 = [[r.at[i] for r in (got_a, got_b, got_c, got_d)] for i in range(4)]
+    slots_a, slots_b = [[r.at[i] for r in (got_a, got_b, got_c, got_d)] for i in range(2)]
     far, after, before = (x + 2) % RING, (x + 1) % RING, (x + 3) % RING
 
     def times(q, right):
@@ -397,29 +430,14 @@
     def own_b(total):
         total[:, second] = z_b[pl.ds(pl.multiple_of(y * GROUP_ROWS, 8), GROUP_ROWS)]
 
-    oa = open_a(part.at[0], lambda: xs[0].reshape(BLOCK, HALF_SLAB), slots_a)
-    ob = open_b(part.at[1], xr[1].reshape(RING * PANEL, HALF_SLAB), slots_b)
-    y_f32[:, first] = times(x, xs[0].reshape(BLOCK, HALF_SLAB))
-    own_b(y_f32)
+    gather_end(y_left)
+    oa = open_a(part.at[0], lambda: ya[:, :GROUP_ROWS].reshape(BLOCK, HALF_SLAB), slots_a)
+    gather_end(y_right)
+    ob = open_b(part.at[1], yb[...].reshape(RING * PANEL, HALF_SLAB), slots_b)
+    z_f32[:, first] = times(x, ya[:, :GROUP_ROWS].reshape(BLOCK, HALF_SLAB))
+    own_b(z_f32)
     oa = pass_on("col", part.at[0], slots_a, oa)
     ob = pass_on("row", part.at[1], slots_b, ob)
-    close(oa, slots_a, y_f32, first)
-    ya[y] = y_f32[:, first].astype(jnp.bfloat16)
-    sa = gather_start("row", ya)
-    close(ob, slots_b, y_f32, second)
-    yb[x, group_rows] = y_f32[:, second].astype(jnp.bfloat16)
-    sb = gather_start("col", yb)
-    sa = gather_pass("row", ya, sa)
-    sb = gather_pass("col", yb, sb)
-    gather_end(sa)
-
-    oa = open_a(part2.at[0], lambda: ya[...].reshape(BLOCK, HALF_SLAB), slots_a2)
-    gather_end(sb)
-    ob = open_b(part2.at[1], yb[...].reshape(RING * PANEL, HALF_SLAB), slots_b2)
-    z_f32[:, first] = times(x, ya[...].reshape(BLOCK, HALF_SLAB))
-    own_b(z_f32)
-    oa = pass_on("col", part2.at[0], slots_a2, oa)
-    ob = pass_on("row", part2.at[1], slots_b2, ob)
 
     _, row_of = targets(N_DP * MAIN, MAIN, 0, (N_DP * MAIN, 1), 0)
     pick = (lax.broadcasted_iota(jnp.int32, (N_DP * MAIN, GROUP_ROWS), 1) == row_of).astype(f32).astype(jnp.bfloat16)
@@ -437,22 +455,22 @@
 
     def leave(h, cols):
         update[:, cols] = (
-            SCALE * (LINEAR_COEF * x_ref[:, cols].astype(f32) + (CUBIC_COEF * y_f32[:, cols] + QUINTIC_COEF * z_f32[:, cols]))
+            SCALE * (LINEAR_COEF * x_ref[:, cols].astype(f32) + (CUBIC_COEF * y_f32[group_rows, cols] + QUINTIC_COEF * z_f32[:, cols]))
         ).astype(jnp.bfloat16)
         outgoing[h] = (
             jnp.dot(pick, update[:, cols], preferred_element_type=f32).astype(jnp.bfloat16).reshape(N_DP, MAIN, HALF_SLAB)
         )
 
-        def send_back(o, _):
-            back_copies(o)[h].start()
+        def send_back(i, _):
+            back_copies(by_distance(i))[h].start()
             return 0
 
-        lax.fori_loop(1, N_DP, send_back, 0)
+        lax.fori_loop(0, N_DP - 1, send_back, 0)
         returned[h, dp] = outgoing[h, dp]
 
-    close(oa, slots_a2, z_f32, first)
+    close(oa, slots_a, z_f32, first)
     leave(0, first)
-    close(ob, slots_b2, z_f32, second)
+    close(ob, slots_b, z_f32, second)
     leave(1, second)
     late = jnp.zeros((N_DP * EXTRA, LANES), f32)
     for j in range(4):
@@ -543,14 +561,17 @@
             vmem((7, SHARD, BLOCK), bf),
             vmem((RING, PANEL, BLOCK), bf),
             vmem((2, RING, GROUP_ROWS, HALF_SLAB), bf),
-            vmem((4, HALF_ROWS, HALF_SLAB), bf),
-            vmem((4, HALF_ROWS, HALF_SLAB), bf),
-            vmem((4, GROUP_ROWS, HALF_SLAB), bf),
-            vmem((4, GROUP_ROWS, HALF_SLAB), bf),
-            vmem((GROUP_ROWS, SLAB), f32),
-            vmem((RING, GROUP_ROWS, HALF_SLAB), bf),
+            vmem((2, HALF_ROWS, HALF_SLAB), bf),
+            vmem((2, HALF_ROWS, HALF_SLAB), bf),
+            vmem((2, GROUP_ROWS, HALF_SLAB), bf),
+            vmem((2, GROUP_ROWS, HALF_SLAB), bf),
+            vmem((PANEL, SLAB), f32),
             vmem((RING, PANEL, HALF_SLAB), bf),
-            vmem((2, RING, GROUP_ROWS, HALF_SLAB), bf),
+            vmem((RING, PANEL, HALF_SLAB), bf),
+            vmem((RING, SHARD, SLAB), f32),
+            vmem((N_Z, RING, SHARD, SLAB), bf),
+            vmem((N_Z, RING - 1, SHARD, SLAB), bf),
+            vmem((N_Z, SHARD, SLAB), f32),
             vmem((BLOCK, HALF_SLAB), f32),
             vmem((GROUP_ROWS, SLAB), f32),
             vmem((GROUP_ROWS, SLAB), bf),

time: 147 us -> 141 us (0.959)
  Pallas kernels: 145 us -> 138 us
    pallas_call x1, Pallas kernels: 140 us -> 134 us  [newton_schulz(): pl.pallas_call(core_kernel, out_shape=(jax.ShapeDtypeStruct((2, N_DP, MAI...]
where the time goes in v6:
time: 141 us; the launch traced here: 140 us
  Pallas kernels  138 us (98%)
  local copies, waits for them, and re-layouts  1.88 us (1%)
    pallas_call x1, Pallas kernels, newton_schulz(): pl.pallas_call(core_kernel, out_shape=(jax.ShapeDtypeStruct((2, N_DP, MAI...  134 us
    pallas_call x1, Pallas kernels, newton_schulz(): pl.pallas_call(finish_kernel, out_shape=jax.ShapeDtypeStruct((1, FLAT_ROW...  4.94 us

profile of v6, /device:TPU:1, one launch (start us, length us, event | category | flops | bytes accessed | tf_op | source)
XLA Modules:
  0.0 140.4 jit_solution(13173843950070478392)
XLA Ops:
  0.0 0.0 copy-start.2
  0.0 133.5 %shard_map.28 = (bf16[2,16,32,256]{3,2,1,0:T(8,128)(2,1)}, bf16[16,16,128]{2,1,0:T(8,128)(2,1)}) custom-call(s32[16,16]{1,0:T(8,128)} %lengths_ref.3, bf16[1,270336]{1,0:T(2,128)(2,1)} %flat_ref.1), custom_call_target="tpu_custom_call" | custom-call | tf_op jit(solution)/shard_map/pallas_call | solution.py:536
  133.5 0.0 copy-done.2
  133.6 0.0 copy-start
  133.6 1.0 copy-done
  134.6 0.0 copy-start.1
  134.6 0.8 copy-done.1
  135.4 4.9 %shard_map.29 = bf16[1,270336]{1,0:T(2,128)(2,1)} custom-call(s32[16,16]{1,0:T(8,128)S(1)} %copy-done.2, bf16[2,16,32,256]{3,2,1,0:T(8,128)(2,1)S(1)} %copy-done, bf16[16,16,128]{2,1,0:T(8,128)(2,1)S(1)} %copy-done.1), custom_call_target="tpu_custom_call" | custom-call | tf_op jit(solution)/shard_map/pallas_call | solution.py:585
Async XLA Ops:
  0.0 133.5 %copy-start.2 = (s32[16,16]{1,0:T(8,128)S(1)}, s32[16,16]{1,0:T(8,128)}, u32[]{:S(2)}) copy-start(s32[16,16]{1,0:T(8,128)} %lengths_ref.3) | copy-start | bytes 3076
  133.6 1.0 copy-start
  134.6 0.8 copy-start.1

commit v7 on v6

--- a/solution.py
+++ b/solution.py
@@ -33,7 +33,13 @@
 EXTRA = 16
 LEAD = 72
 STEP = 176
-N_MESSAGES = 320
+PEERS = N_DP - 1
+BACK_GROUP = 5
+(
+    OUT_0, OUT_1, OUT_EXTRA, BACK_0, BACK_1, BACK_EXTRA, X_R0, X_R1, X_S0, X_S1,
+    TO_SIB, RING_UP, RING_DOWN, G_UP, G_DOWN, G_SIB, Y_SUM, Y_GATHER, Z_A, Z_B, N_SENT,
+) = range(21)
+N_RECEIVED = 128
 MESH = pl.DeviceIdType.MESH
 SCALE = 0.2 * math.sqrt(max(ROWS, COLS))
 
@@ -47,8 +53,8 @@
 
 
 def core_kernel(
-    lengths_ref, flat_ref, returned, returned_extra, staged, canvas, outgoing, extra_tmp, extra, arrived, arrived_extra, x_ref, xr, xs, own_f32, sib_f32, to_sib, from_sib, gh, ring_f, ring_b, g_full,
-    part, got_a, got_b, got_c, got_d, y_f32, ya, yb, y_tmp, y_out, y_in, y_own, z_b, z_f32, update, send_sem, recv_sem,
+    lengths_ref, flat_ref, out_ref, staged, canvas, outgoing, extra_tmp, extra, arrived, arrived_extra, x_ref, xr, xs, own_f32, sib_f32, to_sib, from_sib, gh, ring_f, ring_b, g_full,
+    part, got_a, got_b, got_c, got_d, y_f32, ya, yb, y_tmp, y_out, y_in, y_own, z_b, z_f32, update, outgoing_extra, returned, returned_extra, back, send_sem, recv_sem,
 ):
     dp = lax.axis_index("dp")
     y = lax.axis_index("row")
@@ -79,42 +85,47 @@
     def by_distance(i):
         return N_DP // 2 + (i + 1) // 2 * (1 - 2 * (i % 2))
 
-    counter = [6 * N_DP]
-    started = []
-
-    def message(src, dst, device, slot=None):
-        if slot is None:
-            slot = counter[0]
-            counter[0] += 1
+    counter = [10]
+
+    def message(src, dst, device, group, slot):
         return pltpu.make_async_remote_copy(
-            src_ref=src, dst_ref=dst, send_sem=send_sem.at[slot], recv_sem=recv_sem.at[slot],
+            src_ref=src, dst_ref=dst, send_sem=send_sem.at[group], recv_sem=recv_sem.at[slot],
             device_id=device, device_id_type=MESH,
         )
 
-    def send(src, dst, device):
-        copy = message(src, dst, device)
+    def new_slot():
+        counter[0] += 1
+        return counter[0] - 1
+
+    def send(src, dst, device, group, slot=None):
+        copy = message(src, dst, device, group, new_slot() if slot is None else slot)
         copy.start()
-        started.append(copy)
         return copy
 
+    def all_sent(ref, group):
+        message(ref, ref, dev_sib, group, 0).wait_send()
+
+    def all_received(ref, slot):
+        message(ref, ref, dev_sib, 0, slot).wait_recv()
+
     top, bottom = pl.ds(0, HALF_ROWS), pl.ds(HALF_ROWS, HALF_ROWS)
 
-    def gather_start(axis, buf):
+    def gather_start(axis, buf, group):
         p = place[axis]
         right, left = near[axis]
-        a = [send(buf.at[p, h], buf.at[p, h], right) for h in (top, bottom)]
-        b = [send(buf.at[p, h], buf.at[p, h], left) for h in (bottom, top)]
+        a = [send(buf.at[p, h], buf.at[p, h], right, group) for h in (top, bottom)]
+        b = [send(buf.at[p, h], buf.at[p, h], left, group) for h in (bottom, top)]
         return a, b
 
-    def gather_pass(axis, buf, state):
+    def gather_pass(axis, buf, state, group):
         p = place[axis]
         right, left = near[axis]
         a, b = state
         before, after = (p + 3) % RING, (p + 1) % RING
         a[0].wait_recv()
-        f = send(buf.at[before, top], buf.at[before, top], right)
+        f = send(buf.at[before, top], buf.at[before, top], right, group)
         b[0].wait_recv()
-        g = send(buf.at[after, bottom], buf.at[after, bottom], left)
+        g = send(buf.at[after, bottom], buf.at[after, bottom], left, group)
         return a[1], b[1], f, g
 
     def gather_end(tail):
@@ -145,13 +156,16 @@
     lax.fori_loop(0, FLAT_ROWS // STEP, stage, 0)
     extra_tmp[...] = jnp.zeros_like(extra_tmp)
 
-    def out_copies(o):
-        there = (dp + o) % N_DP
-        device = (there, y, x)
+    def partner(i):
+        there = (dp + by_distance(i)) % N_DP
+        return there, (there, y, x)
+
+    def out_copies(i):
+        there, device = partner(i)
         return (
-            message(extra.at[there], arrived_extra.at[dp], device, slot=o),
-            message(canvas.at[0, there], arrived.at[0, dp], device, slot=N_DP + o),
-            message(canvas.at[1, there], arrived.at[1, dp], device, slot=2 * N_DP + o),
+            message(extra.at[there], arrived_extra.at[i], device, OUT_EXTRA, 0),
+            message(canvas.at[0, there], arrived.at[0, i], device, OUT_0, 1),
+            message(canvas.at[1, there], arrived.at[1, i], device, OUT_1, 2),
         )
 
     def place_part(o, _):
@@ -174,40 +188,42 @@
     pl.semaphore_wait(barrier, 4 + N_DP - 1)
 
     def send_out(i, _):
-        for copy in out_copies(by_distance(i))[:2]:
+        for copy in out_copies(i)[:2]:
             copy.start()
         return 0
 
     def send_out_more(i, _):
-        out_copies(by_distance(i))[2].start()
+        out_copies(i)[2].start()
         return 0
 
-    lax.fori_loop(0, N_DP - 1, send_out, 0)
-    lax.fori_loop(0, N_DP - 1, send_out_more, 0)
+    lax.fori_loop(0, PEERS, send_out, 0)
+    lax.fori_loop(0, PEERS, send_out_more, 0)
     for h in range(2):
-        arrived[h, dp] = canvas[h, dp]
-    arrived_extra[dp] = extra[dp]
-
-    def targets(length, width, offset, shape, dim):
+        arrived[h, PEERS] = canvas[h, dp]
+    arrived_extra[PEERS] = extra[dp]
+
+    def targets(length, width, offset, shape, dim, slot_of):
         k = lax.broadcasted_iota(jnp.int32, shape, dim)
         found = jnp.full(shape, -1, jnp.int32)
         for d in range(N_DP):
-            inside = k // width == d
+            inside = k // width == slot_of(d)
             found = jnp.where(inside, first_rows[d] + k % width + offset, found)
         return k, found
 
-    k, row_of = targets(N_DP * MAIN, MAIN, 0, (1, N_DP * MAIN), 1)
+    def arrival_slot(d):
+        ahead = (dp - d + N_DP) % N_DP - N_DP // 2
+        return jnp.where(ahead >= 0, 2 * ahead, -2 * ahead - 1)
+
+    k, row_of = targets(N_DP * MAIN, MAIN, 0, (1, N_DP * MAIN), 1, arrival_slot)
     pick = (lax.broadcasted_iota(jnp.int32, (GROUP_ROWS, N_DP * MAIN), 0) == row_of).astype(jnp.float32).astype(jnp.bfloat16)
-    ke, row_e = targets(N_DP * EXTRA, EXTRA, MAIN, (1, N_DP * EXTRA), 1)
+    ke, row_e = targets(N_DP * EXTRA, EXTRA, MAIN, (1, N_DP * EXTRA), 1, arrival_slot)
     ke = ke % EXTRA
 
     def land(h):
-        def wait_out(o, _):
-            for copy in out_copies(o)[2 * h : 2 + h]:
-                copy.wait()
-            return 0
-
-        lax.fori_loop(1, N_DP, wait_out, 0)
+        remote = pl.ds(0, PEERS)
+        if h == 0:
+            all_received(arrived_extra.at[remote], 0)
+        all_received(arrived.at[h, remote], 1 + h)
         value = jnp.dot(pick, arrived[h].reshape(N_DP * MAIN, HALF_SLAB), preferred_element_type=jnp.float32)
         late = arrived_extra[...].reshape(N_DP * EXTRA, LANES)
         parts = []
@@ -255,15 +271,15 @@
         to_sib[p, rows] = (sib_f32[p, rows] + value).astype(jnp.bfloat16)
 
     land(0)
-    a0 = gather_start("col", xr.at[0])
-    b0 = gather_start("row", xs.at[0])
+    a0 = gather_start("col", xr.at[0], X_R0)
+    b0 = gather_start("row", xs.at[0], X_S0)
     land(1)
-    a1 = gather_start("col", xr.at[1])
-    b1 = gather_start("row", xs.at[1])
-    a0 = gather_pass("col", xr.at[0], a0)
-    b0 = gather_pass("row", xs.at[0], b0)
-    a1 = gather_pass("col", xr.at[1], a1)
-    b1 = gather_pass("row", xs.at[1], b1)
+    a1 = gather_start("col", xr.at[1], X_R1)
+    b1 = gather_start("row", xs.at[1], X_S1)
+    a0 = gather_pass("col", xr.at[0], a0, X_R0)
+    b0 = gather_pass("row", xs.at[0], b0, X_S0)
+    a1 = gather_pass("col", xr.at[1], a1, X_R1)
+    b1 = gather_pass("row", xs.at[1], b1, X_S1)
     gather_end(a0 + b0)
     gram(1 - c, 0, keep_sib)
     gram(c, 0, keep_own)
@@ -282,7 +298,7 @@
     sib_in = []
     for upward, panel, distance in plan:
         rows = shard_rows(z + distance if upward else z - distance)
-        sib_in.append(send(to_sib.at[panel, rows], from_sib.at[panel, rows], dev_sib))
+        sib_in.append(send(to_sib.at[panel, rows], from_sib.at[panel, rows], dev_sib, TO_SIB))
     gram(c, 1, add_own)
 
     up_in, down_in = [], []
@@ -306,43 +322,42 @@
             src = ring.at[k - 2]
             term = term + ring[k - 2].astype(f32)
         src[...] = term.astype(jnp.bfloat16)
-        arrivals.append(send(src, ring.at[k], device))
+        arrivals.append(send(src, ring.at[k], device, RING_UP if upward else RING_DOWN))
     mine = shard_rows(z)
 
-    sib_parts = {}
-
-    def relay(panel, rows, device):
+    sib_slots = {shift: new_slot() for shift in (0, -1, 1, -2, 2, -3, 3, 4)}
+
+    def relay(panel, rows, device, group, slot=None):
         ref = g_full.at[2 * c + panel, rows]
-        return send(ref, ref, device)
-
-    y_sums, y_left, y_right = {}, [], []
+        return send(ref, ref, device, group, slot)
+
+    y_slots = [new_slot() for _ in range(N_Z)]
+    y_left, y_right = new_slot(), new_slot()
     order = (0, -1, 1, -2, 2, -3, 3, 4)
 
     def multiply(shift):
         i, rows = order.index(shift), shard_rows(z + shift)
-        for copy in sib_parts[shift]:
-            copy.wait_recv()
+        all_received(g_full.at[pl.ds(2 * (1 - c), 2), rows], sib_slots[shift])
         left = g_full[:, rows, :].reshape(RING * SHARD, BLOCK)
         for h in range(2):
             value = jnp.dot(left, xs[h].reshape(BLOCK, HALF_SLAB), preferred_element_type=f32)
             y_tmp[:, :, halves[h]] = value.reshape(RING, SHARD, HALF_SLAB)
         y_out[i] = y_tmp[...].astype(jnp.bfloat16)
-        y_sums[shift] = [
-            send(y_out.at[i, (x + o) % RING], y_in.at[i, o - 1], (dp, y, (x + o) % RING)) for o in (2, 1, 3)
-        ]
+        for o in (2, 1, 3):
+            there = (x + o) % RING
+            send(y_out.at[i, there], y_in.at[i, o - 1], (dp, y, there), Y_SUM, y_slots[i])
         y_own[i] = y_tmp[x]
 
     def add_up(shift):
         i, rows = order.index(shift), shard_rows(z + shift)
-        for copy in y_sums[shift]:
-            copy.wait_recv()
+        all_received(y_in.at[i], y_slots[i])
         value = y_own[i] + y_in[i, 0].astype(f32) + y_in[i, 1].astype(f32) + y_in[i, 2].astype(f32)
         y_f32[rows] = value
         ya[y, rows] = value[:, :HALF_SLAB].astype(jnp.bfloat16)
         yb[x, rows] = value[:, HALF_SLAB:].astype(jnp.bfloat16)
         for o in (2, 1, 3):
-            y_left.append(send(ya.at[y, rows], ya.at[y, rows], (dp, (y + o) % RING, x)))
-            y_right.append(send(yb.at[x, rows], yb.at[x, rows], (dp, y, (x + o) % RING)))
+            send(ya.at[y, rows], ya.at[y, rows], (dp, (y + o) % RING, x), Y_GATHER, y_left)
+            send(yb.at[x, rows], yb.at[x, rows], (dp, y, (x + o) % RING), Y_GATHER, y_right)
 
     up_in, down_in = [], []
     for k in range(9):
@@ -351,44 +366,44 @@
         if k >= 2:
             up_in[k - 2].wait_recv()
         if k < 7:
-            up_in.append(relay(*up_part, dev_up))
+            up_in.append(relay(*up_part, dev_up, G_UP))
         if k >= 2:
             down_in[k - 2].wait_recv()
         if k < 7:
-            down_in.append(relay(*down_part, dev_down))
-        sib_parts.setdefault(4 if k == 8 else -back_by, []).append(relay(*up_part, dev_sib))
+            down_in.append(relay(*down_part, dev_down, G_DOWN))
+        relay(*up_part, dev_sib, G_SIB, sib_slots[4 if k == 8 else -back_by])
         if k >= 2:
-            sib_parts.setdefault(back_by, []).append(relay(*down_part, dev_sib))
-        for shift in {2: (0,), 4: (-1, 1), 6: (-2, 2), 7: (-3, 3), 8: (4,)}.get(k, ()):
+            relay(*down_part, dev_sib, G_SIB, sib_slots[back_by])
+        for shift in {1: (0,), 3: (-1, 1), 5: (-2, 2), 7: (-3, 3), 8: (4,)}.get(k, ()):
             multiply(shift)
-        for shift in {5: (0,), 6: (-1, 1), 8: (-2, 2, -3, 3, 4)}.get(k, ()):
+        for shift in {3: (0,), 6: (-1, 1), 8: (-2, 2, -3, 3, 4)}.get(k, ()):
             add_up(shift)
 
-    def reduce_start(axis, buf, a_ref, b_ref):
+    def reduce_start(axis, buf, a_ref, b_ref, group):
         p = place[axis]
         right, left = near[axis]
         far = (p + 2) % RING
-        return (send(buf.at[far, top], a_ref, right), send(buf.at[far, bottom], b_ref, left))
-
-    def reduce_near(axis, buf, c_ref, d_ref):
+        return (send(buf.at[far, top], a_ref, right, group), send(buf.at[far, bottom], b_ref, left, group))
+
+    def reduce_near(axis, buf, c_ref, d_ref, group):
         p = place[axis]
         right, left = near[axis]
         after, before = (p + 1) % RING, (p + 3) % RING
         return (
-            send(buf.at[after, bottom], c_ref.at[bottom], right),
-            send(buf.at[before, top], d_ref.at[top], left),
+            send(buf.at[after, bottom], c_ref.at[bottom], right, group),
+            send(buf.at[before, top], d_ref.at[top], left, group),
         )
 
-    def reduce_pass(axis, buf, a_ref, b_ref, c_ref, d_ref, state):
+    def reduce_pass(axis, buf, a_ref, b_ref, c_ref, d_ref, state, group):
         p = place[axis]
         right, left = near[axis]
         after, before = (p + 1) % RING, (p + 3) % RING
         state[0].wait_recv()
         buf[after, top] = (buf[after, top].astype(f32) + a_ref[...].astype(f32)).astype(jnp.bfloat16)
-        c2 = send(buf.at[after, top], c_ref.at[top], right)
+        c2 = send(buf.at[after, top], c_ref.at[top], right, group)
         state[1].wait_recv()
         buf[before, bottom] = (buf[before, bottom].astype(f32) + b_ref[...].astype(f32)).astype(jnp.bfloat16)
-        d2 = send(buf.at[before, bottom], d_ref.at[bottom], left)
+        d2 = send(buf.at[before, bottom], d_ref.at[bottom], left, group)
         return (c2, d2)
 
     first, second = pl.ds(0, HALF_SLAB), pl.ds(HALF_SLAB, HALF_SLAB)
@@ -400,10 +415,10 @@
 
     def open_a(buf, right, slots):
         buf[far] = times(far, right()).astype(jnp.bfloat16)
-        state = reduce_start("col", buf, *slots[:2])
+        state = reduce_start("col", buf, *slots[:2], Z_A)
         buf[after] = times(after, right()).astype(jnp.bfloat16)
         buf[before] = times(before, right()).astype(jnp.bfloat16)
-        near_copies = reduce_near("col", buf, *slots[2:])
+        near_copies = reduce_near("col", buf, *slots[2:], Z_A)
         return state, near_copies
 
     def open_b(buf, right, slots):
@@ -417,11 +432,11 @@
 
         lax.fori_loop(0, BLOCK // LANES, columns, 0)
         buf[...] = z_b[...].astype(jnp.bfloat16).reshape(RING, GROUP_ROWS, HALF_SLAB)
-        state = reduce_start("row", buf, *slots[:2])
-        return state, reduce_near("row", buf, *slots[2:])
+        state = reduce_start("row", buf, *slots[:2], Z_B)
+        return state, reduce_near("row", buf, *slots[2:], Z_B)
 
     def pass_on(axis, buf, slots, opened):
-        return opened[1] + reduce_pass(axis, buf, *slots, opened[0])
+        return opened[1] + reduce_pass(axis, buf, *slots, opened[0], Z_A if axis == "col" else Z_B)
 
     def close(tail, slots, total, cols):
         gather_end(tail)
@@ -430,27 +445,46 @@
     def own_b(total):
         total[:, second] = z_b[pl.ds(pl.multiple_of(y * GROUP_ROWS, 8), GROUP_ROWS)]
 
-    gather_end(y_left)
+    three = pl.ds(0, RING - 1)
+    all_received(ya.at[three], y_left)
     oa = open_a(part.at[0], lambda: ya[:, :GROUP_ROWS].reshape(BLOCK, HALF_SLAB), slots_a)
-    gather_end(y_right)
+    all_received(yb.at[three], y_right)
     ob = open_b(part.at[1], yb[...].reshape(RING * PANEL, HALF_SLAB), slots_b)
     z_f32[:, first] = times(x, ya[:, :GROUP_ROWS].reshape(BLOCK, HALF_SLAB))
     own_b(z_f32)
     oa = pass_on("col", part.at[0], slots_a, oa)
     ob = pass_on("row", part.at[1], slots_b, ob)
 
-    _, row_of = targets(N_DP * MAIN, MAIN, 0, (N_DP * MAIN, 1), 0)
+    _, row_of = targets(N_DP * MAIN, MAIN, 0, (N_DP * MAIN, 1), 0, lambda d: d)
     pick = (lax.broadcasted_iota(jnp.int32, (N_DP * MAIN, GROUP_ROWS), 1) == row_of).astype(f32).astype(jnp.bfloat16)
-    ke, row_e = targets(N_DP * EXTRA, EXTRA, MAIN, (N_DP * EXTRA, 1), 0)
+    ke, row_e = targets(N_DP * EXTRA, EXTRA, MAIN, (N_DP * EXTRA, 1), 0, lambda d: d)
     ke = ke % EXTRA
-
-    def back_copies(o):
-        there = (dp + o) % N_DP
-        device = (there, y, x)
+    late_picks = []
+    for j in range(4):
+        row_j = jnp.where(ke // 2 == j, row_e - 2 * j, -1)
+        pick_j = lax.broadcasted_iota(jnp.int32, (N_DP * EXTRA, GROUP_ROWS), 1) == row_j
+        late_picks.append(pick_j.astype(f32).astype(jnp.bfloat16))
+
+    def back_copies(i):
+        there, device = partner(i)
+        group = i // BACK_GROUP
         return (
-            message(outgoing.at[0, there], returned.at[0, dp], device, slot=3 * N_DP + o),
-            message(outgoing.at[1, there], returned.at[1, dp], device, slot=4 * N_DP + o),
-            message(extra.at[there], returned_extra.at[dp], device, slot=5 * N_DP + o),
+            message(outgoing.at[0, there], returned.at[0, i], device, BACK_0, 3 + group),
+            message(outgoing.at[1, there], returned.at[1, i], device, BACK_1, 6 + group),
+            message(outgoing_extra.at[there], returned_extra.at[i], device, BACK_EXTRA, 9),
+        )
+
+    def send_back(n):
+        def step(i, _):
+            back_copies(i)[n].start()
+            return 0
+
+        lax.fori_loop(0, PEERS, step, 0)
+
+    def late_rows(h):
+        return sum(
+            jnp.dot(late_picks[j], update[:, j * LANES : (j + 1) * LANES], preferred_element_type=f32)
+            for j in (2 * h, 2 * h + 1)
         )
 
     def leave(h, cols):
@@ -460,87 +494,89 @@
         outgoing[h] = (
             jnp.dot(pick, update[:, cols], preferred_element_type=f32).astype(jnp.bfloat16).reshape(N_DP, MAIN, HALF_SLAB)
         )
-
-        def send_back(i, _):
-            back_copies(by_distance(i))[h].start()
-            return 0
-
-        lax.fori_loop(0, N_DP - 1, send_back, 0)
-        returned[h, dp] = outgoing[h, dp]
+        send_back(h)
+        returned[h, PEERS] = outgoing[h, dp]
 
     close(oa, slots_a, z_f32, first)
     leave(0, first)
+    late = late_rows(0)
     close(ob, slots_b, z_f32, second)
     leave(1, second)
-    late = jnp.zeros((N_DP * EXTRA, LANES), f32)
-    for j in range(4):
-        row_j = jnp.where(ke // 2 == j, row_e - 2 * j, -1)
-        pick_j = (lax.broadcasted_iota(jnp.int32, (N_DP * EXTRA, GROUP_ROWS), 1) == row_j).astype(f32).astype(jnp.bfloat16)
-        late += jnp.dot(pick_j, update[:, j * LANES : (j + 1) * LANES], preferred_element_type=f32)
-    extra[...] = late.astype(jnp.bfloat16).reshape(N_DP, EXTRA, LANES)
-
-    def send_extra(o, _):
-        back_copies(o)[2].start()
-        return 0
-
-    lax.fori_loop(1, N_DP, send_extra, 0)
-    returned_extra[dp] = extra[dp]
-
-    def wait_back(o, _):
-        for copy in back_copies(o):
-            copy.wait()
-        return 0
-
-    lax.fori_loop(1, N_DP, wait_back, 0)
-    for copy in started:
-        copy.wait_send()
-
-
-def finish_kernel(lengths_ref, returned, returned_extra, out_ref, back, extra_tmp):
-    dp = lax.axis_index("dp")
-    group = lax.axis_index("row") * RING + lax.axis_index("col")
-    my_start = jnp.int32(0)
-    for d in range(N_DP):
-        my_start = my_start + jnp.where(d < dp, lengths_ref[group, d], 0)
-    my_length = lengths_ref[group, dp]
-    lead = my_start % COLS
-    lead_rows, lead_lanes = lead // LANES, lead % LANES
+    outgoing_extra[...] = (late + late_rows(1)).astype(jnp.bfloat16).reshape(N_DP, EXTRA, LANES)
+    send_back(2)
+    returned_extra[PEERS] = outgoing_extra[dp]
+
     turn = (LANES - lead_lanes) % LANES
 
-    def unpack(d, _):
-        extra_tmp[...] = pltpu.roll(returned_extra[d].astype(jnp.float32), turn, 1)
+    def unpack(h, i):
+        d = (dp - by_distance(i) + N_DP) % N_DP
+        for j in range(2):
+            back[pl.ds(d * 4 + 2 * h + j, MAIN, stride=CHUNKS)] = pltpu.roll(
+                returned[h, i, :, pl.ds(j * LANES, LANES)].astype(f32), turn, 1)
+
+    def unpack_late(i, _):
+        d = (dp - by_distance(i) + N_DP) % N_DP
+        extra_tmp[...] = pltpu.roll(returned_extra[i].astype(f32), turn, 1)
         for j in range(4):
-            back[pl.ds(d * 4 + j, MAIN, stride=CHUNKS)] = pltpu.roll(
-                returned[j // 2, d, :, pl.ds(j % 2 * LANES, LANES)].astype(jnp.float32), turn, 1)
             back[pl.ds(d * 4 + j + MAIN * CHUNKS, 2, stride=CHUNKS)] = extra_tmp[2 * j : 2 * j + 2]
         return 0
 
-    lax.fori_loop(0, N_DP, unpack, 0)
-    back[pl.ds(34 * CHUNKS, 8)] = jnp.zeros((8, LANES), jnp.float32)
+    def unpack_step(h):
+        def step(i, _):
+            unpack(h, i)
+            return 0
+
+        return step
+
+    back[pl.ds(34 * CHUNKS, 8)] = jnp.zeros((8, LANES), f32)
+    for h in range(2):
+        unpack(h, jnp.int32(PEERS))
+    for h in range(2):
+        for group in range(3):
+            all_received(returned.at[h, pl.ds(group * BACK_GROUP, BACK_GROUP)], 3 + 3 * h + group)
+            lax.fori_loop(group * BACK_GROUP, (group + 1) * BACK_GROUP, unpack_step(h), 0)
+    all_received(returned_extra.at[pl.ds(0, PEERS)], 9)
+    lax.fori_loop(0, N_DP, unpack_late, 0)
 
     def finish(i, _):
         here = back[pl.ds(i * STEP + lead_rows, STEP)]
-        after = back[pl.ds(i * STEP + lead_rows + 1, STEP)]
+        after_rows = back[pl.ds(i * STEP + lead_rows + 1, STEP)]
         lane = lax.broadcasted_iota(jnp.int32, (STEP, LANES), 1)
-        value = jnp.where(lane + lead_lanes < LANES, here, after)
+        value = jnp.where(lane + lead_lanes < LANES, here, after_rows)
         value = jnp.where(slots(i) < my_length, value, 0.0).reshape(1, STEP * LANES)
         out_ref[:, pl.ds(pl.multiple_of(i * STEP * LANES, LANES), STEP * LANES)] = value.astype(jnp.bfloat16)
         return 0
 
     lax.fori_loop(0, FLAT_ROWS // STEP, finish, 0)
 
+    remote = pl.ds(0, PEERS)
+    halves_of_three = xs.at[0, pl.ds(0, RING - 1)]
+    for ref, groups in (
+        (arrived.at[0, remote], (OUT_0, OUT_1, BACK_0, BACK_1)),
+        (arrived_extra.at[remote], (OUT_EXTRA, BACK_EXTRA)),
+        (halves_of_three, (X_R0, X_R1, X_S0, X_S1, Z_A, Z_B)),
+        (to_sib, (TO_SIB, G_SIB)),
+        (ring_f, (RING_UP, RING_DOWN, G_UP, G_DOWN)),
+        (y_in, (Y_SUM, Y_GATHER)),
+    ):
+        for group in groups:
+            all_sent(ref, group)
+
+
+def hand_on_kernel(value_ref, out_ref, sem):
+    copy = pltpu.make_async_copy(value_ref, out_ref, sem)
+    copy.start()
+    copy.wait()
+
 
 def newton_schulz(lengths, flat):
     bf, f32 = jnp.bfloat16, jnp.float32
     vmem = pltpu.VMEM
-    returned, returned_extra = pl.pallas_call(
+    value = pl.pallas_call(
         core_kernel,
-        out_shape=(
-            jax.ShapeDtypeStruct((2, N_DP, MAIN, HALF_SLAB), bf),
-            jax.ShapeDtypeStruct((N_DP, EXTRA, LANES), bf),
-        ),
+        out_shape=jax.ShapeDtypeStruct((1, FLAT_ROWS * LANES), bf),
         in_specs=[pl.BlockSpec(memory_space=pltpu.SMEM), pl.BlockSpec(memory_space=pltpu.VMEM)],
-        out_specs=[pl.BlockSpec(memory_space=pltpu.VMEM)] * 2,
+        out_specs=pl.BlockSpec(memory_space=pltpu.VMEM),
         scratch_shapes=[
             vmem((LEAD + FLAT_ROWS + 88, LANES), f32),
             vmem((2, N_DP, MAIN, HALF_SLAB), bf),
@@ -575,21 +611,25 @@
             vmem((BLOCK, HALF_SLAB), f32),
             vmem((GROUP_ROWS, SLAB), f32),
             vmem((GROUP_ROWS, SLAB), bf),
-            pltpu.SemaphoreType.DMA((N_MESSAGES,)),
-            pltpu.SemaphoreType.DMA((N_MESSAGES,)),
+            vmem((N_DP, EXTRA, LANES), bf),
+            vmem((2, N_DP, MAIN, HALF_SLAB), bf),
+            vmem((N_DP, EXTRA, LANES), bf),
+            vmem((34 * CHUNKS + 8, LANES), f32),
+            pltpu.SemaphoreType.DMA((N_SENT,)),
+            pltpu.SemaphoreType.DMA((N_RECEIVED,)),
         ],
         compiler_params=pltpu.CompilerParams(
             collective_id=0, has_side_effects=True, vmem_limit_bytes=56 * 1024 * 1024
         ),
     )(lengths, flat)
     return pl.pallas_call(
-        finish_kernel,
+        hand_on_kernel,
         out_shape=jax.ShapeDtypeStruct((1, FLAT_ROWS * LANES), bf),
-        in_specs=[pl.BlockSpec(memory_space=pltpu.SMEM)] + [pl.BlockSpec(memory_space=pltpu.VMEM)] * 2,
-        out_specs=pl.BlockSpec(memory_space=pltpu.VMEM),
-        scratch_shapes=[vmem((34 * CHUNKS + 8, LANES), f32), vmem((EXTRA, LANES), f32)],
-        compiler_params=pltpu.CompilerParams(vmem_limit_bytes=32 * 1024 * 1024),
-    )(lengths, returned, returned_extra)
+        in_specs=[pl.BlockSpec(memory_space=pl.ANY)],
+        out_specs=pl.BlockSpec(memory_space=pl.ANY),
+        scratch_shapes=[pltpu.SemaphoreType.DMA],
+        compiler_params=pltpu.CompilerParams(vmem_limit_bytes=60 * 1024 * 1024),
+    )(value)
 
 
 def local(flat_iterate, lengths):

time: 141 us -> 164 us (1.16)
  Pallas kernels: 138 us -> 164 us
  local copies, waits for them, and re-layouts: 1.88 us -> 0 us
    pallas_call x2, Pallas kernels: 138 us -> 164 us  [the longest x1 130 us: newton_schulz(): pl.pallas_call(core_kernel, out_shape=jax.ShapeDtypeStruct((1, FLAT_ROWS...]
    unnamed x6 -> x0, local copies, waits for them, and re-layouts: 1.88 us -> none
where the time goes in v7:
time: 164 us
  Pallas kernels  164 us (100%)
    pallas_call x1, Pallas kernels, newton_schulz(): pl.pallas_call(core_kernel, out_shape=jax.ShapeDtypeStruct((1, FLAT_ROWS...  130 us
    pallas_call x1, Pallas kernels, newton_schulz(): pl.pallas_call(hand_on_kernel, out_shape=jax.ShapeDtypeStruct((1, FLAT_RO...  33.9 us

profile of v7, /device:TPU:1, one launch (start us, length us, event | category | flops | bytes accessed | tf_op | source)
XLA Modules:
  0.0 163.6 jit_solution(3361869192672924289)
XLA Ops:
  0.0 129.8 %shard_map.28.value_ref = bf16[1,270336]{1,0:T(2,128)(2,1)} custom-call(s32[16,16]{1,0:T(8,128)} %lengths_ref.1, bf16[1,270336]{1,0:T(2,128)(2,1)} %flat_ref.1), custom_call_target="tpu_custom_call" | custom-call | tf_op jit(solution)/shard_map/pallas_call | solution.py:575
  129.8 33.9 %shard_map.29 = bf16[1,270336]{1,0:T(2,128)(2,1)} custom-call(bf16[1,270336]{1,0:T(2,128)(2,1)} %shard_map.28.value_ref), custom_call_target="tpu_custom_call" | custom-call | tf_op jit(solution)/shard_map/pallas_call | solution.py:625

commit v8 on v7

--- a/solution.py
+++ b/solution.py
@@ -543,8 +543,7 @@
         after_rows = back[pl.ds(i * STEP + lead_rows + 1, STEP)]
         lane = lax.broadcasted_iota(jnp.int32, (STEP, LANES), 1)
         value = jnp.where(lane + lead_lanes < LANES, here, after_rows)
-        value = jnp.where(slots(i) < my_length, value, 0.0).reshape(1, STEP * LANES)
-        out_ref[:, pl.ds(pl.multiple_of(i * STEP * LANES, LANES), STEP * LANES)] = value.astype(jnp.bfloat16)
+        out_ref[pl.ds(pl.multiple_of(i * STEP, 8), STEP)] = jnp.where(slots(i) < my_length, value, 0.0)
         return 0
 
     lax.fori_loop(0, FLAT_ROWS // STEP, finish, 0)
@@ -563,10 +562,13 @@
             all_sent(ref, group)
 
 
-def hand_on_kernel(value_ref, out_ref, sem):
-    copy = pltpu.make_async_copy(value_ref, out_ref, sem)
-    copy.start()
-    copy.wait()
+def flatten_kernel(value_ref, out_ref):
+    def step(i, _):
+        value = value_ref[pl.ds(pl.multiple_of(i * STEP, 8), STEP)].reshape(1, STEP * LANES)
+        out_ref[:, pl.ds(pl.multiple_of(i * STEP * LANES, LANES), STEP * LANES)] = value.astype(jnp.bfloat16)
+        return 0
+
+    lax.fori_loop(0, FLAT_ROWS // STEP, step, 0)
 
 
 def newton_schulz(lengths, flat):
@@ -574,7 +576,7 @@
     vmem = pltpu.VMEM
     value = pl.pallas_call(
         core_kernel,
-        out_shape=jax.ShapeDtypeStruct((1, FLAT_ROWS * LANES), bf),
+        out_shape=jax.ShapeDtypeStruct((FLAT_ROWS, LANES), f32),
         in_specs=[pl.BlockSpec(memory_space=pltpu.SMEM), pl.BlockSpec(memory_space=pltpu.VMEM)],
         out_specs=pl.BlockSpec(memory_space=pltpu.VMEM),
         scratch_shapes=[
@@ -623,12 +625,11 @@
         ),
     )(lengths, flat)
     return pl.pallas_call(
-        hand_on_kernel,
+        flatten_kernel,
         out_shape=jax.ShapeDtypeStruct((1, FLAT_ROWS * LANES), bf),
-        in_specs=[pl.BlockSpec(memory_space=pl.ANY)],
-        out_specs=pl.BlockSpec(memory_space=pl.ANY),
-        scratch_shapes=[pltpu.SemaphoreType.DMA],
-        compiler_params=pltpu.CompilerParams(vmem_limit_bytes=60 * 1024 * 1024),
+        in_specs=[pl.BlockSpec(memory_space=pltpu.VMEM)],
+        out_specs=pl.BlockSpec(memory_space=pltpu.VMEM),
+        compiler_params=pltpu.CompilerParams(vmem_limit_bytes=56 * 1024 * 1024),
     )(value)
 
 

time: 164 us -> 132 us (0.80)
  Pallas kernels: 164 us -> 132 us
    pallas_call x2, Pallas kernels: 164 us -> 132 us  [the longest x1 129 us: newton_schulz(): pl.pallas_call(core_kernel, out_shape=jax.ShapeDtypeStruct((FLAT_ROWS, LA...]
where the time goes in v8:
time: 132 us
  Pallas kernels  132 us (100%)
    pallas_call x1, Pallas kernels, newton_schulz(): pl.pallas_call(core_kernel, out_shape=jax.ShapeDtypeStruct((FLAT_ROWS, LA...  129 us
    pallas_call x1, Pallas kernels, newton_schulz(): pl.pallas_call(flatten_kernel, out_shape=jax.ShapeDtypeStruct((1, FLAT_RO...  2.81 us

profile of v8, /device:TPU:1, one launch (start us, length us, event | category | flops | bytes accessed | tf_op | source)
XLA Modules:
  0.0 131.9 jit_solution(10580163309413671364)
XLA Ops:
  0.0 129.1 %shard_map.28.value_ref = f32[2112,128]{1,0:T(8,128)} custom-call(s32[16,16]{1,0:T(8,128)} %lengths_ref.1, bf16[1,270336]{1,0:T(2,128)(2,1)} %flat_ref.1), custom_call_target="tpu_custom_call" | custom-call | tf_op jit(solution)/shard_map/pallas_call | solution.py:577
  129.1 2.8 %shard_map.29 = bf16[1,270336]{1,0:T(2,128)(2,1)} custom-call(f32[2112,128]{1,0:T(8,128)} %shard_map.28.value_ref), custom_call_target="tpu_custom_call" | custom-call | tf_op jit(solution)/shard_map/pallas_call | solution.py:627

commit v9 on v8

--- a/solution.py
+++ b/solution.py
@@ -35,11 +35,13 @@
 STEP = 176
 PEERS = N_DP - 1
 BACK_GROUP = 5
+PARTS = SLAB // LANES
+OUT, X_R, X_S = 0, PARTS, 2 * PARTS
 (
-    OUT_0, OUT_1, OUT_EXTRA, BACK_0, BACK_1, BACK_EXTRA, X_R0, X_R1, X_S0, X_S1,
-    TO_SIB, RING_UP, RING_DOWN, G_UP, G_DOWN, G_SIB, Y_SUM, Y_GATHER, Z_A, Z_B, N_SENT,
-) = range(21)
-N_RECEIVED = 128
+    OUT_EXTRA, BACK_0, BACK_1, BACK_EXTRA, TO_SIB, RING_UP, RING_DOWN, G_UP, G_DOWN, G_SIB,
+    Y_SUM, Y_GATHER, Z_A, Z_B, N_SENT,
+) = range(3 * PARTS, 3 * PARTS + 15)
+N_RECEIVED = 112
 MESH = pl.DeviceIdType.MESH
 SCALE = 0.2 * math.sqrt(max(ROWS, COLS))
 
@@ -85,7 +87,7 @@
     def by_distance(i):
         return N_DP // 2 + (i + 1) // 2 * (1 - 2 * (i % 2))
 
-    counter = [10]
+    counter = [12]
 
     def message(src, dst, device, group, slot):
         return pltpu.make_async_remote_copy(
@@ -113,24 +115,27 @@
     def gather_start(axis, buf, group):
         p = place[axis]
         right, left = near[axis]
-        a = [send(buf.at[p, h], buf.at[p, h], right, group) for h in (top, bottom)]
-        b = [send(buf.at[p, h], buf.at[p, h], left, group) for h in (bottom, top)]
-        return a, b
-
-    def gather_pass(axis, buf, state, group):
+        tail = new_slot()
+        from_left = send(buf.at[p, top], buf.at[p, top], right, group)
+        from_right = send(buf.at[p, bottom], buf.at[p, bottom], left, group)
+        send(buf.at[p, bottom], buf.at[p, bottom], right, group, tail)
+        send(buf.at[p, top], buf.at[p, top], left, group, tail)
+        return buf, group, from_left, from_right, tail
+
+    def gather_pass(axis, state):
         p = place[axis]
         right, left = near[axis]
-        a, b = state
+        buf, group, from_left, from_right, tail = state
         before, after = (p + 3) % RING, (p + 1) % RING
-        a[0].wait_recv()
-        f = send(buf.at[before, top], buf.at[before, top], right, group)
-        b[0].wait_recv()
-        g = send(buf.at[after, bottom], buf.at[after, bottom], left, group)
-        return a[1], b[1], f, g
-
-    def gather_end(tail):
-        for copy in tail:
-            copy.wait_recv()
+        from_left.wait_recv()
+        send(buf.at[before, top], buf.at[before, top], right, group, tail)
+        from_right.wait_recv()
+        send(buf.at[after, bottom], buf.at[after, bottom], left, group, tail)
+
+    def gather_end(state):
+        all_received(state[0].at[pl.ds(0, 2), group_rows], state[4])
+
+    group_rows = pl.ds(0, GROUP_ROWS)
 
     group = y * RING + x
     my_start = jnp.int32(0)
@@ -162,11 +167,8 @@
 
     def out_copies(i):
         there, device = partner(i)
-        return (
-            message(extra.at[there], arrived_extra.at[i], device, OUT_EXTRA, 0),
-            message(canvas.at[0, there], arrived.at[0, i], device, OUT_0, 1),
-            message(canvas.at[1, there], arrived.at[1, i], device, OUT_1, 2),
-        )
+        copies = [message(canvas.at[j, there], arrived.at[j, i], device, OUT + j, j) for j in range(PARTS)]
+        return copies + [message(extra.at[there], arrived_extra.at[i], device, OUT_EXTRA, PARTS)]
 
     def place_part(o, _):
         there = (dp + o) % N_DP
@@ -178,7 +180,7 @@
         for j in range(4):
             here = staged[pl.ds(start + j, MAIN, stride=CHUNKS)]
             here2 = staged[pl.ds(start + j + MAIN * CHUNKS, 2, stride=CHUNKS)]
-            canvas[j // 2, there, :, pl.ds(j % 2 * LANES, LANES)] = jnp.where(lane >= lead_lanes, here, before).astype(jnp.bfloat16)
+            canvas[j, there] = jnp.where(lane >= lead_lanes, here, before).astype(jnp.bfloat16)
             extra_tmp[pl.ds(j * 2, 2)] = jnp.where(lane2 >= lead_lanes, here2, before2)
             before, before2 = here, here2
         extra[there] = extra_tmp[...].astype(jnp.bfloat16)
@@ -187,19 +189,15 @@
     lax.fori_loop(1, N_DP + 1, place_part, 0)
     pl.semaphore_wait(barrier, 4 + N_DP - 1)
 
-    def send_out(i, _):
-        for copy in out_copies(i)[:2]:
-            copy.start()
-        return 0
-
-    def send_out_more(i, _):
-        out_copies(i)[2].start()
-        return 0
-
-    lax.fori_loop(0, PEERS, send_out, 0)
-    lax.fori_loop(0, PEERS, send_out_more, 0)
-    for h in range(2):
-        arrived[h, PEERS] = canvas[h, dp]
+    for j in (PARTS, *range(PARTS)):
+
+        def send_out(i, _):
+            out_copies(i)[j].start()
+            return 0
+
+        lax.fori_loop(0, PEERS, send_out, 0)
+    for j in range(PARTS):
+        arrived[j, PEERS] = canvas[j, dp]
     arrived_extra[PEERS] = extra[dp]
 
     def targets(length, width, offset, shape, dim, slot_of):
@@ -219,29 +217,38 @@
     ke, row_e = targets(N_DP * EXTRA, EXTRA, MAIN, (1, N_DP * EXTRA), 1, arrival_slot)
     ke = ke % EXTRA
 
-    def land(h):
-        remote = pl.ds(0, PEERS)
-        if h == 0:
-            all_received(arrived_extra.at[remote], 0)
-        all_received(arrived.at[h, remote], 1 + h)
-        value = jnp.dot(pick, arrived[h].reshape(N_DP * MAIN, HALF_SLAB), preferred_element_type=jnp.float32)
+    remote = pl.ds(0, PEERS)
+
+    def land(j):
+        if j == 0:
+            all_received(arrived_extra.at[remote], PARTS)
+        all_received(arrived.at[j, remote], j)
+        value = jnp.dot(pick, arrived[j].reshape(N_DP * MAIN, LANES), preferred_element_type=jnp.float32)
+        row_j = jnp.where(ke // 2 == j, row_e - 2 * j, -1)
+        pick_j = (lax.broadcasted_iota(jnp.int32, (GROUP_ROWS, N_DP * EXTRA), 0) == row_j).astype(jnp.float32).astype(jnp.bfloat16)
         late = arrived_extra[...].reshape(N_DP * EXTRA, LANES)
-        parts = []
-        for j in (2 * h, 2 * h + 1):
-            row_j = jnp.where(ke // 2 == j, row_e - 2 * j, -1)
-            pick_j = (lax.broadcasted_iota(jnp.int32, (GROUP_ROWS, N_DP * EXTRA), 0) == row_j).astype(jnp.float32).astype(jnp.bfloat16)
-            parts.append(jnp.dot(pick_j, late, preferred_element_type=jnp.float32))
-        value = (value + jnp.concatenate(parts, axis=1)).astype(jnp.bfloat16)
-        x_ref[:, halves[h]] = value
-        xr[h, x, group_rows] = value
-        xs[h, y] = value
+        value = (value + jnp.dot(pick_j, late, preferred_element_type=jnp.float32)).astype(jnp.bfloat16)
+        x_ref[:, pl.ds(j * LANES, LANES)] = value
+        xr[j, x, group_rows] = value
+        xs[j, y] = value
+        return gather_start("col", xr.at[j], X_R + j), gather_start("row", xs.at[j], X_S + j)
+
+    def pass_part(states):
+        gather_pass("col", states[0])
+        gather_pass("row", states[1])
+
+    def end_part(states):
+        gather_end(states[0])
+        gather_end(states[1])
+
+    def xs_half(h):
+        return jnp.concatenate([xs[2 * h].reshape(BLOCK, LANES), xs[2 * h + 1].reshape(BLOCK, LANES)], axis=1)
 
     halves = (pl.ds(0, HALF_SLAB), pl.ds(HALF_SLAB, HALF_SLAB))
-    group_rows = pl.ds(0, GROUP_ROWS)
     pad = pl.ds(GROUP_ROWS, PANEL - GROUP_ROWS)
     for q in range(RING):
-        for h in range(2):
-            xr[h, q, pad] = jnp.zeros((PANEL - GROUP_ROWS, HALF_SLAB), jnp.bfloat16)
+        for j in range(PARTS):
+            xr[j, q, pad] = jnp.zeros((PANEL - GROUP_ROWS, LANES), jnp.bfloat16)
     for p in range(2):
         to_sib[p, pad] = jnp.zeros((PANEL - GROUP_ROWS, BLOCK), jnp.bfloat16)
         own_f32[p, pad] = jnp.zeros((PANEL - GROUP_ROWS, BLOCK), jnp.float32)
@@ -249,8 +256,9 @@
     def gram(core, h, store):
         def tile(i, _):
             rows = pl.ds(pl.multiple_of((i % 2) * HALF_ROWS, 16), HALF_ROWS)
+            q = 2 * core + i // 2
             value = lax.dot_general(
-                xr[h, 2 * core + i // 2, rows], xs[h].reshape(BLOCK, HALF_SLAB),
+                jnp.concatenate([xr[2 * h, q, rows], xr[2 * h + 1, q, rows]], axis=1), xs_half(h),
                 (((1,), (1,)), ((), ())), preferred_element_type=jnp.float32,
             )
             store(i // 2, rows, value)
@@ -270,20 +278,19 @@
     def add_sib(p, rows, value):
         to_sib[p, rows] = (sib_f32[p, rows] + value).astype(jnp.bfloat16)
 
-    land(0)
-    a0 = gather_start("col", xr.at[0], X_R0)
-    b0 = gather_start("row", xs.at[0], X_S0)
-    land(1)
-    a1 = gather_start("col", xr.at[1], X_R1)
-    b1 = gather_start("row", xs.at[1], X_S1)
-    a0 = gather_pass("col", xr.at[0], a0, X_R0)
-    b0 = gather_pass("row", xs.at[0], b0, X_S0)
-    a1 = gather_pass("col", xr.at[1], a1, X_R1)
-    b1 = gather_pass("row", xs.at[1], b1, X_S1)
-    gather_end(a0 + b0)
+    parts = [land(0), land(1)]
+    pass_part(parts[0])
+    parts.append(land(2))
+    pass_part(parts[1])
+    parts.append(land(3))
+    pass_part(parts[2])
+    end_part(parts[0])
+    end_part(parts[1])
     gram(1 - c, 0, keep_sib)
+    pass_part(parts[3])
     gram(c, 0, keep_own)
-    gather_end(a1 + b1)
+    end_part(parts[2])
+    end_part(parts[3])
     gram(1 - c, 1, add_sib)
 
     def shard_rows(s):
@@ -340,7 +347,7 @@
         all_received(g_full.at[pl.ds(2 * (1 - c), 2), rows], sib_slots[shift])
         left = g_full[:, rows, :].reshape(RING * SHARD, BLOCK)
         for h in range(2):
-            value = jnp.dot(left, xs[h].reshape(BLOCK, HALF_SLAB), preferred_element_type=f32)
+            value = jnp.dot(left, xs_half(h), preferred_element_type=f32)
             y_tmp[:, :, halves[h]] = value.reshape(RING, SHARD, HALF_SLAB)
         y_out[i] = y_tmp[...].astype(jnp.bfloat16)
         for o in (2, 1, 3):
@@ -379,32 +386,32 @@
         for shift in {3: (0,), 6: (-1, 1), 8: (-2, 2, -3, 3, 4)}.get(k, ()):
             add_up(shift)
 
-    def reduce_start(axis, buf, a_ref, b_ref, group):
-        p = place[axis]
+    def reduce_start(axis, buf, slots, group):
         right, left = near[axis]
-        far = (p + 2) % RING
-        return (send(buf.at[far, top], a_ref, right, group), send(buf.at[far, bottom], b_ref, left, group))
-
-    def reduce_near(axis, buf, c_ref, d_ref, group):
+        far = (place[axis] + 2) % RING
+        return (
+            send(buf.at[far, top], slots[0], right, group),
+            send(buf.at[far, bottom], slots[1], left, group),
+            new_slot(),
+        )
+
+    def reduce_near(axis, buf, slots, group, tail):
         p = place[axis]
         right, left = near[axis]
         after, before = (p + 1) % RING, (p + 3) % RING
-        return (
-            send(buf.at[after, bottom], c_ref.at[bottom], right, group),
-            send(buf.at[before, top], d_ref.at[top], left, group),
-        )
-
-    def reduce_pass(axis, buf, a_ref, b_ref, c_ref, d_ref, state, group):
+        send(buf.at[after, bottom], slots[2].at[bottom], right, group, tail)
+        send(buf.at[before, top], slots[3].at[top], left, group, tail)
+
+    def reduce_pass(axis, buf, slots, group, state):
         p = place[axis]
         right, left = near[axis]
         after, before = (p + 1) % RING, (p + 3) % RING
         state[0].wait_recv()
-        buf[after, top] = (buf[after, top].astype(f32) + a_ref[...].astype(f32)).astype(jnp.bfloat16)
-        c2 = send(buf.at[after, top], c_ref.at[top], right, group)
+        buf[after, top] = (buf[after, top].astype(f32) + slots[0][...].astype(f32)).astype(jnp.bfloat16)
+        send(buf.at[after, top], slots[2].at[top], right, group, state[2])
         state[1].wait_recv()
-        buf[before, bottom] = (buf[before, bottom].astype(f32) + b_ref[...].astype(f32)).astype(jnp.bfloat16)
-        d2 = send(buf.at[before, bottom], d_ref.at[bottom], left, group)
-        return (c2, d2)
+        buf[before, bottom] = (buf[before, bottom].astype(f32) + slots[1][...].astype(f32)).astype(jnp.bfloat16)
+        send(buf.at[before, bottom], slots[3].at[bottom], left, group, state[2])
 
     first, second = pl.ds(0, HALF_SLAB), pl.ds(HALF_SLAB, HALF_SLAB)
     slots_a, slots_b = [[r.at[i] for r in (got_a, got_b, got_c, got_d)] for i in range(2)]
@@ -415,11 +422,11 @@
 
     def open_a(buf, right, slots):
         buf[far] = times(far, right()).astype(jnp.bfloat16)
-        state = reduce_start("col", buf, *slots[:2], Z_A)
+        state = reduce_start("col", buf, slots, Z_A)
         buf[after] = times(after, right()).astype(jnp.bfloat16)
         buf[before] = times(before, right()).astype(jnp.bfloat16)
-        near_copies = reduce_near("col", buf, *slots[2:], Z_A)
-        return state, near_copies
+        reduce_near("col", buf, slots, Z_A, state[2])
+        return state
 
     def open_b(buf, right, slots):
         def columns(j, _):
@@ -432,14 +439,12 @@
 
         lax.fori_loop(0, BLOCK // LANES, columns, 0)
         buf[...] = z_b[...].astype(jnp.bfloat16).reshape(RING, GROUP_ROWS, HALF_SLAB)
-        state = reduce_start("row", buf, *slots[:2], Z_B)
-        return state, reduce_near("row", buf, *slots[2:], Z_B)
-
-    def pass_on(axis, buf, slots, opened):
-        return opened[1] + reduce_pass(axis, buf, *slots, opened[0], Z_A if axis == "col" else Z_B)
-
-    def close(tail, slots, total, cols):
-        gather_end(tail)
+        state = reduce_start("row", buf, slots, Z_B)
+        reduce_near("row", buf, slots, Z_B, state[2])
+        return state
+
+    def close(state, slots, total, cols):
+        all_received(xr.at[pl.ds(0, PARTS), 0, group_rows], state[2])
         total[:, cols] = total[:, cols] + slots[2][...].astype(f32) + slots[3][...].astype(f32)
 
     def own_b(total):
@@ -452,8 +457,8 @@
     ob = open_b(part.at[1], yb[...].reshape(RING * PANEL, HALF_SLAB), slots_b)
     z_f32[:, first] = times(x, ya[:, :GROUP_ROWS].reshape(BLOCK, HALF_SLAB))
     own_b(z_f32)
-    oa = pass_on("col", part.at[0], slots_a, oa)
-    ob = pass_on("row", part.at[1], slots_b, ob)
+    reduce_pass("col", part.at[0], slots_a, Z_A, oa)
+    reduce_pass("row", part.at[1], slots_b, Z_B, ob)
 
     _, row_of = targets(N_DP * MAIN, MAIN, 0, (N_DP * MAIN, 1), 0, lambda d: d)
     pick = (lax.broadcasted_iota(jnp.int32, (N_DP * MAIN, GROUP_ROWS), 1) == row_of).astype(f32).astype(jnp.bfloat16)
@@ -469,9 +474,9 @@
         there, device = partner(i)
         group = i // BACK_GROUP
         return (
-            message(outgoing.at[0, there], returned.at[0, i], device, BACK_0, 3 + group),
-            message(outgoing.at[1, there], returned.at[1, i], device, BACK_1, 6 + group),
-            message(outgoing_extra.at[there], returned_extra.at[i], device, BACK_EXTRA, 9),
+            message(outgoing.at[0, there], returned.at[0, i], device, BACK_0, 5 + group),
+            message(outgoing.at[1, there], returned.at[1, i], device, BACK_1, 8 + group),
+            message(outgoing_extra.at[there], returned_extra.at[i], device, BACK_EXTRA, 11),
         )
 
     def send_back(n):
@@ -533,9 +538,9 @@
         unpack(h, jnp.int32(PEERS))
     for h in range(2):
         for group in range(3):
-            all_received(returned.at[h, pl.ds(group * BACK_GROUP, BACK_GROUP)], 3 + 3 * h + group)
+            all_received(returned.at[h, pl.ds(group * BACK_GROUP, BACK_GROUP)], 5 + 3 * h + group)
             lax.fori_loop(group * BACK_GROUP, (group + 1) * BACK_GROUP, unpack_step(h), 0)
-    all_received(returned_extra.at[pl.ds(0, PEERS)], 9)
+    all_received(returned_extra.at[pl.ds(0, PEERS)], 11)
     lax.fori_loop(0, N_DP, unpack_late, 0)
 
     def finish(i, _):
@@ -548,12 +553,12 @@
 
     lax.fori_loop(0, FLAT_ROWS // STEP, finish, 0)
 
-    remote = pl.ds(0, PEERS)
-    halves_of_three = xs.at[0, pl.ds(0, RING - 1)]
     for ref, groups in (
-        (arrived.at[0, remote], (OUT_0, OUT_1, BACK_0, BACK_1)),
+        (arrived.at[0, remote], range(OUT, OUT + PARTS)),
+        (returned.at[0, remote], (BACK_0, BACK_1)),
         (arrived_extra.at[remote], (OUT_EXTRA, BACK_EXTRA)),
-        (halves_of_three, (X_R0, X_R1, X_S0, X_S1, Z_A, Z_B)),
+        (xs.at[0, pl.ds(0, RING - 1)], range(X_R, X_S + PARTS)),
+        (part.at[0, pl.ds(0, RING - 1)], (Z_A, Z_B)),
         (to_sib, (TO_SIB, G_SIB)),
         (ring_f, (RING_UP, RING_DOWN, G_UP, G_DOWN)),
         (y_in, (Y_SUM, Y_GATHER)),
@@ -568,7 +573,7 @@
         out_ref[:, pl.ds(pl.multiple_of(i * STEP * LANES, LANES), STEP * LANES)] = value.astype(jnp.bfloat16)
         return 0
 
-    lax.fori_loop(0, FLAT_ROWS // STEP, step, 0)
+    lax.fori_loop(0, value_ref.shape[0] // STEP, step, 0)
 
 
 def newton_schulz(lengths, flat):
@@ -581,15 +586,15 @@
         out_specs=pl.BlockSpec(memory_space=pltpu.VMEM),
         scratch_shapes=[
             vmem((LEAD + FLAT_ROWS + 88, LANES), f32),
-            vmem((2, N_DP, MAIN, HALF_SLAB), bf),
+            vmem((PARTS, N_DP, MAIN, LANES), bf),
             vmem((2, N_DP, MAIN, HALF_SLAB), bf),
             vmem((EXTRA, LANES), f32),
             vmem((N_DP, EXTRA, LANES), bf),
-            vmem((2, N_DP, MAIN, HALF_SLAB), bf),
+            vmem((PARTS, N_DP, MAIN, LANES), bf),
             vmem((N_DP, EXTRA, LANES), bf),
             vmem((GROUP_ROWS, SLAB), bf),
-            vmem((2, RING, PANEL, HALF_SLAB), bf),
-            vmem((2, RING, GROUP_ROWS, HALF_SLAB), bf),
+            vmem((PARTS, RING, PANEL, LANES), bf),
+            vmem((PARTS, RING, GROUP_ROWS, LANES), bf),
             vmem((2, PANEL, BLOCK), f32),
             vmem((2, PANEL, BLOCK), f32),
             vmem((2, PANEL, BLOCK), bf),
@@ -627,8 +632,9 @@
     return pl.pallas_call(
         flatten_kernel,
         out_shape=jax.ShapeDtypeStruct((1, FLAT_ROWS * LANES), bf),
-        in_specs=[pl.BlockSpec(memory_space=pltpu.VMEM)],
-        out_specs=pl.BlockSpec(memory_space=pltpu.VMEM),
+        grid=(4,),
+        in_specs=[pl.BlockSpec((FLAT_ROWS // 4, LANES), lambda i: (i, 0))],
+        out_specs=pl.BlockSpec((1, FLAT_ROWS // 4 * LANES), lambda i: (0, i)),
         compiler_params=pltpu.CompilerParams(vmem_limit_bytes=56 * 1024 * 1024),
     )(value)
 

time: 132 us -> 131 us (level)
    pallas_call x1, Pallas kernels: 129 us -> 127 us  [newton_schulz(): pl.pallas_call(core_kernel, out_shape=jax.ShapeDtypeStruct((FLAT_ROWS, LA...]
where the time goes in v9:
time: 131 us
  Pallas kernels  131 us (100%)
    pallas_call x1, Pallas kernels, newton_schulz(): pl.pallas_call(core_kernel, out_shape=jax.ShapeDtypeStruct((FLAT_ROWS, LA...  127 us
    pallas_call x1, Pallas kernels, newton_schulz(): pl.pallas_call(flatten_kernel, out_shape=jax.ShapeDtypeStruct((1, FLAT_RO...  3.64 us

profile of v9, /device:TPU:1, one launch (start us, length us, event | category | flops | bytes accessed | tf_op | source)
XLA Modules:
  0.0 130.8 jit_solution(2093784032161568395)
XLA Ops:
  0.0 127.2 %shard_map.28.value_ref = f32[2112,128]{1,0:T(8,128)} custom-call(s32[16,16]{1,0:T(8,128)} %lengths_ref.1, bf16[1,270336]{1,0:T(2,128)(2,1)} %flat_ref.1), custom_call_target="tpu_custom_call" | custom-call | tf_op jit(solution)/shard_map/pallas_call | solution.py:582
  127.2 3.6 %shard_map.29 = bf16[1,270336]{1,0:T(2,128)(2,1)} custom-call(f32[2112,128]{1,0:T(8,128)} %shard_map.28.value_ref), custom_call_target="tpu_custom_call" | custom-call | tf_op jit(solution)/shard_map/pallas_call | solution.py:632

commit v10 on v9

--- a/solution.py
+++ b/solution.py
@@ -39,8 +39,9 @@
 OUT, X_R, X_S = 0, PARTS, 2 * PARTS
 (
     OUT_EXTRA, BACK_0, BACK_1, BACK_EXTRA, TO_SIB, RING_UP, RING_DOWN, G_UP, G_DOWN, G_SIB,
-    Y_SUM, Y_GATHER, Z_A, Z_B, N_SENT,
-) = range(3 * PARTS, 3 * PARTS + 15)
+    Y_SUM, Y_GATHER, Z_A, Z_A_MORE, Z_B, N_SENT,
+) = range(3 * PARTS, 3 * PARTS + 16)
+LEFT = SLAB - LANES
 N_RECEIVED = 112
 MESH = pl.DeviceIdType.MESH
 SCALE = 0.2 * math.sqrt(max(ROWS, COLS))
@@ -340,6 +341,7 @@
 
     y_slots = [new_slot() for _ in range(N_Z)]
     y_left, y_right = new_slot(), new_slot()
+    far_slots = {shift: new_slot() for shift in (0, -1, 1, -2, 2)}
     order = (0, -1, 1, -2, 2, -3, 3, 4)
 
     def multiply(shift):
@@ -350,18 +352,41 @@
             value = jnp.dot(left, xs_half(h), preferred_element_type=f32)
             y_tmp[:, :, halves[h]] = value.reshape(RING, SHARD, HALF_SLAB)
         y_out[i] = y_tmp[...].astype(jnp.bfloat16)
-        for o in (2, 1, 3):
-            there = (x + o) % RING
-            send(y_out.at[i, there], y_in.at[i, o - 1], (dp, y, there), Y_SUM, y_slots[i])
         y_own[i] = y_tmp[x]
+        if shift not in far_slots:
+            for o in (2, 1, 3):
+                there = (x + o) % RING
+                send(y_out.at[i, there], y_in.at[i, o - 1], (dp, y, there), Y_SUM, y_slots[i])
+            return
+        right, left = near["col"]
+        far, after, before = (x + 2) % RING, (x + 1) % RING, (x + 3) % RING
+        low, high = halves
+        send(y_out.at[i, far, :, low], y_in.at[i, 2, :, low], right, Y_SUM, far_slots[shift])
+        send(y_out.at[i, far, :, high], y_in.at[i, 2, :, high], left, Y_SUM, far_slots[shift])
+        send(y_out.at[i, after, :, high], y_in.at[i, 0, :, high], right, Y_SUM, y_slots[i])
+        send(y_out.at[i, before, :, low], y_in.at[i, 1, :, low], left, Y_SUM, y_slots[i])
+
+    def pass_sums(shift):
+        i = order.index(shift)
+        right, left = near["col"]
+        after, before = (x + 1) % RING, (x + 3) % RING
+        low, high = halves
+        all_received(y_in.at[i, 2], far_slots[shift])
+        for there, cols, device, to in ((after, low, right, 0), (before, high, left, 1)):
+            total = y_out[i, there, :, cols].astype(f32) + y_in[i, 2, :, cols].astype(f32)
+            y_out[i, there, :, cols] = total.astype(jnp.bfloat16)
+            send(y_out.at[i, there, :, cols], y_in.at[i, to, :, cols], device, Y_SUM, y_slots[i])
 
     def add_up(shift):
         i, rows = order.index(shift), shard_rows(z + shift)
-        all_received(y_in.at[i], y_slots[i])
-        value = y_own[i] + y_in[i, 0].astype(f32) + y_in[i, 1].astype(f32) + y_in[i, 2].astype(f32)
+        terms = 2 if shift in far_slots else 3
+        all_received(y_in.at[i, pl.ds(0, terms)], y_slots[i])
+        value = y_own[i]
+        for t in range(terms):
+            value = value + y_in[i, t].astype(f32)
         y_f32[rows] = value
-        ya[y, rows] = value[:, :HALF_SLAB].astype(jnp.bfloat16)
-        yb[x, rows] = value[:, HALF_SLAB:].astype(jnp.bfloat16)
+        ya[y, rows] = value[:, :LEFT].astype(jnp.bfloat16)
+        yb[x, rows] = value[:, LEFT:].astype(jnp.bfloat16)
         for o in (2, 1, 3):
             send(ya.at[y, rows], ya.at[y, rows], (dp, (y + o) % RING, x), Y_GATHER, y_left)
             send(yb.at[x, rows], yb.at[x, rows], (dp, y, (x + o) % RING), Y_GATHER, y_right)
@@ -381,10 +406,14 @@
         relay(*up_part, dev_sib, G_SIB, sib_slots[4 if k == 8 else -back_by])
         if k >= 2:
             relay(*down_part, dev_sib, G_SIB, sib_slots[back_by])
+        for shift in {3: (0,), 5: (-1, 1), 7: (-2, 2)}.get(k, ()):
+            pass_sums(shift)
+        for shift in {5: (0,), 7: (-1, 1)}.get(k, ()):
+            add_up(shift)
         for shift in {1: (0,), 3: (-1, 1), 5: (-2, 2), 7: (-3, 3), 8: (4,)}.get(k, ()):
             multiply(shift)
-        for shift in {3: (0,), 6: (-1, 1), 8: (-2, 2, -3, 3, 4)}.get(k, ()):
-            add_up(shift)
+    for shift in (-2, 2, -3, 3, 4):
+        add_up(shift)
 
     def reduce_start(axis, buf, slots, group):
         right, left = near[axis]
@@ -414,18 +443,24 @@
         send(buf.at[before, bottom], slots[3].at[bottom], left, group, state[2])
 
     first, second = pl.ds(0, HALF_SLAB), pl.ds(HALF_SLAB, HALF_SLAB)
-    slots_a, slots_b = [[r.at[i] for r in (got_a, got_b, got_c, got_d)] for i in range(2)]
+    got = (got_a, got_b, got_c, got_d)
+    one_lane, other_lane = pl.ds(0, LANES), pl.ds(LANES, LANES)
+    slots_a = [r.at[0] for r in got]
+    slots_m = [r.at[1, :, one_lane] for r in got]
+    slots_b = [r.at[1, :, other_lane] for r in got]
+    part_a, part_m, part_b = part.at[0], part.at[1, :, :, one_lane], part.at[1, :, :, other_lane]
+    more, last = pl.ds(HALF_SLAB, LANES), pl.ds(LEFT, LANES)
     far, after, before = (x + 2) % RING, (x + 1) % RING, (x + 3) % RING
 
     def times(q, right):
         return jnp.dot(g_full[q, group_rows], right, preferred_element_type=f32)
 
-    def open_a(buf, right, slots):
+    def open_a(buf, right, slots, group):
         buf[far] = times(far, right()).astype(jnp.bfloat16)
-        state = reduce_start("col", buf, slots, Z_A)
+        state = reduce_start("col", buf, slots, group)
         buf[after] = times(after, right()).astype(jnp.bfloat16)
         buf[before] = times(before, right()).astype(jnp.bfloat16)
-        reduce_near("col", buf, slots, Z_A, state[2])
+        reduce_near("col", buf, slots, group, state[2])
         return state
 
     def open_b(buf, right, slots):
@@ -438,27 +473,33 @@
             return 0
 
         lax.fori_loop(0, BLOCK // LANES, columns, 0)
-        buf[...] = z_b[...].astype(jnp.bfloat16).reshape(RING, GROUP_ROWS, HALF_SLAB)
+        buf[...] = z_b[...].astype(jnp.bfloat16).reshape(RING, GROUP_ROWS, LANES)
         state = reduce_start("row", buf, slots, Z_B)
         reduce_near("row", buf, slots, Z_B, state[2])
         return state
 
     def close(state, slots, total, cols):
-        all_received(xr.at[pl.ds(0, PARTS), 0, group_rows], state[2])
+        all_received(xr.at[pl.ds(0, RING * slots[2].shape[-1] // HALF_SLAB), 0, group_rows], state[2])
         total[:, cols] = total[:, cols] + slots[2][...].astype(f32) + slots[3][...].astype(f32)
 
     def own_b(total):
-        total[:, second] = z_b[pl.ds(pl.multiple_of(y * GROUP_ROWS, 8), GROUP_ROWS)]
+        total[:, last] = z_b[pl.ds(pl.multiple_of(y * GROUP_ROWS, 8), GROUP_ROWS)]
 
     three = pl.ds(0, RING - 1)
     all_received(ya.at[three], y_left)
-    oa = open_a(part.at[0], lambda: ya[:, :GROUP_ROWS].reshape(BLOCK, HALF_SLAB), slots_a)
+    def y_part(cols):
+        return ya[:, group_rows, cols].reshape(BLOCK, -1)
+
+    oa = open_a(part_a, lambda: y_part(first), slots_a, Z_A)
+    om = open_a(part_m, lambda: y_part(more), slots_m, Z_A_MORE)
     all_received(yb.at[three], y_right)
-    ob = open_b(part.at[1], yb[...].reshape(RING * PANEL, HALF_SLAB), slots_b)
-    z_f32[:, first] = times(x, ya[:, :GROUP_ROWS].reshape(BLOCK, HALF_SLAB))
+    ob = open_b(part_b, yb[...].reshape(RING * PANEL, LANES), slots_b)
+    z_f32[:, first] = times(x, y_part(first))
+    reduce_pass("col", part_a, slots_a, Z_A, oa)
+    z_f32[:, more] = times(x, y_part(more))
     own_b(z_f32)
-    reduce_pass("col", part.at[0], slots_a, Z_A, oa)
-    reduce_pass("row", part.at[1], slots_b, Z_B, ob)
+    reduce_pass("col", part_m, slots_m, Z_A_MORE, om)
+    reduce_pass("row", part_b, slots_b, Z_B, ob)
 
     _, row_of = targets(N_DP * MAIN, MAIN, 0, (N_DP * MAIN, 1), 0, lambda d: d)
     pick = (lax.broadcasted_iota(jnp.int32, (N_DP * MAIN, GROUP_ROWS), 1) == row_of).astype(f32).astype(jnp.bfloat16)
@@ -505,7 +546,8 @@
     close(oa, slots_a, z_f32, first)
     leave(0, first)
     late = late_rows(0)
-    close(ob, slots_b, z_f32, second)
+    close(om, slots_m, z_f32, more)
+    close(ob, slots_b, z_f32, last)
     leave(1, second)
     outgoing_extra[...] = (late + late_rows(1)).astype(jnp.bfloat16).reshape(N_DP, EXTRA, LANES)
     send_back(2)
@@ -557,8 +599,8 @@
         (arrived.at[0, remote], range(OUT, OUT + PARTS)),
         (returned.at[0, remote], (BACK_0, BACK_1)),
         (arrived_extra.at[remote], (OUT_EXTRA, BACK_EXTRA)),
-        (xs.at[0, pl.ds(0, RING - 1)], range(X_R, X_S + PARTS)),
-        (part.at[0, pl.ds(0, RING - 1)], (Z_A, Z_B)),
+        (xs.at[0, pl.ds(0, RING - 1)], (*range(X_R, X_S + PARTS), Z_A_MORE, Z_B)),
+        (part.at[0, pl.ds(0, RING - 1)], (Z_A,)),
         (to_sib, (TO_SIB, G_SIB)),
         (ring_f, (RING_UP, RING_DOWN, G_UP, G_DOWN)),
         (y_in, (Y_SUM, Y_GATHER)),
@@ -609,13 +651,13 @@
             vmem((2, GROUP_ROWS, HALF_SLAB), bf),
             vmem((2, GROUP_ROWS, HALF_SLAB), bf),
             vmem((PANEL, SLAB), f32),
-            vmem((RING, PANEL, HALF_SLAB), bf),
-            vmem((RING, PANEL, HALF_SLAB), bf),
+            vmem((RING, PANEL, LEFT), bf),
+            vmem((RING, PANEL, LANES), bf),
             vmem((RING, SHARD, SLAB), f32),
             vmem((N_Z, RING, SHARD, SLAB), bf),
             vmem((N_Z, RING - 1, SHARD, SLAB), bf),
             vmem((N_Z, SHARD, SLAB), f32),
-            vmem((BLOCK, HALF_SLAB), f32),
+            vmem((BLOCK, LANES), f32),
             vmem((GROUP_ROWS, SLAB), f32),
             vmem((GROUP_ROWS, SLAB), bf),
             vmem((N_DP, EXTRA, LANES), bf),

time: 131 us -> 132 us (level)
    pallas_call x1, Pallas kernels: 127 us -> 129 us  [newton_schulz(): pl.pallas_call(core_kernel, out_shape=jax.ShapeDtypeStruct((FLAT_ROWS, LA...]
where the time goes in v10:
time: 132 us
  Pallas kernels  132 us (100%)
    pallas_call x1, Pallas kernels, newton_schulz(): pl.pallas_call(core_kernel, out_shape=jax.ShapeDtypeStruct((FLAT_ROWS, LA...  129 us
    pallas_call x1, Pallas kernels, newton_schulz(): pl.pallas_call(flatten_kernel, out_shape=jax.ShapeDtypeStruct((1, FLAT_RO...  3.64 us

profile of v10, /device:TPU:1, one launch (start us, length us, event | category | flops | bytes accessed | tf_op | source)
XLA Modules:
  0.0 132.2 jit_solution(3182514304862939073)
XLA Ops:
  0.0 128.5 %shard_map.28.value_ref = f32[2112,128]{1,0:T(8,128)} custom-call(s32[16,16]{1,0:T(8,128)} %lengths_ref.1, bf16[1,270336]{1,0:T(2,128)(2,1)} %flat_ref.1), custom_call_target="tpu_custom_call" | custom-call | tf_op jit(solution)/shard_map/pallas_call | solution.py:624
  128.5 3.6 %shard_map.29 = bf16[1,270336]{1,0:T(2,128)(2,1)} custom-call(f32[2112,128]{1,0:T(8,128)} %shard_map.28.value_ref), custom_call_target="tpu_custom_call" | custom-call | tf_op jit(solution)/shard_map/pallas_call | solution.py:674

commit v11 on v9

--- a/solution.py
+++ b/solution.py
@@ -34,6 +34,7 @@
 LEAD = 72
 STEP = 176
 PEERS = N_DP - 1
+WIDE = 768
 BACK_GROUP = 5
 PARTS = SLAB // LANES
 OUT, X_R, X_S = 0, PARTS, 2 * PARTS
@@ -41,7 +42,7 @@
     OUT_EXTRA, BACK_0, BACK_1, BACK_EXTRA, TO_SIB, RING_UP, RING_DOWN, G_UP, G_DOWN, G_SIB,
     Y_SUM, Y_GATHER, Z_A, Z_B, N_SENT,
 ) = range(3 * PARTS, 3 * PARTS + 15)
-N_RECEIVED = 112
+N_RECEIVED = 120
 MESH = pl.DeviceIdType.MESH
 SCALE = 0.2 * math.sqrt(max(ROWS, COLS))
 
@@ -72,10 +73,11 @@
         "col": ((dp, y, (x + 1) % RING), (dp, y, (x + 3) % RING)),
         "row": ((dp, (y + 1) % RING, x), (dp, (y + 3) % RING, x)),
     }
+    far = {"col": (dp, y, (x + 2) % RING), "row": (dp, (y + 2) % RING, x)}
     place = {"col": x, "row": y}
 
     barrier = pltpu.get_barrier_semaphore()
-    for peer in near["col"] + near["row"]:
+    for peer in (*near["col"], *near["row"], far["col"], far["row"]):
         pl.semaphore_signal(barrier, inc=1, device_id=peer, device_id_type=MESH)
 
     def greet(o, _):
@@ -116,6 +118,11 @@
         p = place[axis]
         right, left = near[axis]
         tail = new_slot()
+        if group in (X_R + PARTS - 1, X_S + PARTS - 1):
+            own = buf.at[p, group_rows]
+            for device in (far[axis], right, left):
+                send(own, own, device, group, tail)
+            return buf, tail
         from_left = send(buf.at[p, top], buf.at[p, top], right, group)
         from_right = send(buf.at[p, bottom], buf.at[p, bottom], left, group)
         send(buf.at[p, bottom], buf.at[p, bottom], right, group, tail)
@@ -133,7 +140,7 @@
         send(buf.at[after, bottom], buf.at[after, bottom], left, group, tail)
 
     def gather_end(state):
-        all_received(state[0].at[pl.ds(0, 2), group_rows], state[4])
+        all_received(state[0].at[pl.ds(0, 2 if len(state) > 2 else RING - 1), group_rows], state[-1])
 
     group_rows = pl.ds(0, GROUP_ROWS)
 
@@ -187,7 +194,7 @@
         return 0
 
     lax.fori_loop(1, N_DP + 1, place_part, 0)
-    pl.semaphore_wait(barrier, 4 + N_DP - 1)
+    pl.semaphore_wait(barrier, 6 + N_DP - 1)
 
     for j in (PARTS, *range(PARTS)):
 
@@ -287,7 +294,6 @@
     end_part(parts[0])
     end_part(parts[1])
     gram(1 - c, 0, keep_sib)
-    pass_part(parts[3])
     gram(c, 0, keep_own)
     end_part(parts[2])
     end_part(parts[3])
@@ -308,28 +314,33 @@
         sib_in.append(send(to_sib.at[panel, rows], from_sib.at[panel, rows], dev_sib, TO_SIB))
     gram(c, 1, add_own)
 
+    ring_cols = (pl.ds(0, WIDE), pl.ds(WIDE, BLOCK - WIDE))
     up_in, down_in = [], []
     for (upward, panel, distance), arrival in zip(plan, sib_in):
         rows = shard_rows(z + distance if upward else z - distance)
         arrival.wait_recv()
-        term = own_f32[panel, rows] + from_sib[panel, rows].astype(f32)
-        if distance == 0:
-            up, down = (6, 5) if panel == 0 else (5, 6)
-            up_in[up].wait_recv()
-            down_in[down].wait_recv()
-            term = term + ring_f[up].astype(f32) + ring_b[down].astype(f32)
-            g_full[2 * c + panel, rows] = term.astype(jnp.bfloat16)
-            continue
         arrivals, ring, device = (up_in, ring_f, dev_up) if upward else (down_in, ring_b, dev_down)
         k = len(arrivals)
-        if k < 2:
-            src = gh.at[2 * k + int(upward)]
-        else:
-            arrivals[k - 2].wait_recv()
-            src = ring.at[k - 2]
-            term = term + ring[k - 2].astype(f32)
-        src[...] = term.astype(jnp.bfloat16)
-        arrivals.append(send(src, ring.at[k], device, RING_UP if upward else RING_DOWN))
+        copies = []
+        for n, cols in enumerate(ring_cols):
+            term = own_f32[panel, rows, cols] + from_sib[panel, rows, cols].astype(f32)
+            if distance == 0:
+                up, down = (6, 5) if panel == 0 else (5, 6)
+                up_in[up][n].wait_recv()
+                down_in[down][n].wait_recv()
+                term = term + ring_f[up, :, cols].astype(f32) + ring_b[down, :, cols].astype(f32)
+                g_full[2 * c + panel, rows, cols] = term.astype(jnp.bfloat16)
+                continue
+            if k < 2:
+                src = gh.at[2 * k + int(upward), :, cols]
+            else:
+                arrivals[k - 2][n].wait_recv()
+                src = ring.at[k - 2, :, cols]
+                term = term + ring[k - 2, :, cols].astype(f32)
+            src[...] = term.astype(jnp.bfloat16)
+            copies.append(send(src, ring.at[k, :, cols], device, RING_UP if upward else RING_DOWN))
+        if distance:
+            arrivals.append(copies)
     mine = shard_rows(z)
 
     sib_slots = {shift: new_slot() for shift in (0, -1, 1, -2, 2, -3, 3, 4)}
@@ -383,15 +394,17 @@
             relay(*down_part, dev_sib, G_SIB, sib_slots[back_by])
         for shift in {1: (0,), 3: (-1, 1), 5: (-2, 2), 7: (-3, 3), 8: (4,)}.get(k, ()):
             multiply(shift)
-        for shift in {3: (0,), 6: (-1, 1), 8: (-2, 2, -3, 3, 4)}.get(k, ()):
+        for shift in {3: (0,), 6: (-1, 1), 7: (-2, 2)}.get(k, ()):
             add_up(shift)
+    for shift in (-3, 3, 4):
+        add_up(shift)
 
     def reduce_start(axis, buf, slots, group):
         right, left = near[axis]
-        far = (place[axis] + 2) % RING
+        farthest = (place[axis] + 2) % RING
         return (
-            send(buf.at[far, top], slots[0], right, group),
-            send(buf.at[far, bottom], slots[1], left, group),
+            send(buf.at[farthest, top], slots[0], right, group),
+            send(buf.at[farthest, bottom], slots[1], left, group),
             new_slot(),
         )
 
@@ -415,13 +428,13 @@
 
     first, second = pl.ds(0, HALF_SLAB), pl.ds(HALF_SLAB, HALF_SLAB)
     slots_a, slots_b = [[r.at[i] for r in (got_a, got_b, got_c, got_d)] for i in range(2)]
-    far, after, before = (x + 2) % RING, (x + 1) % RING, (x + 3) % RING
+    farthest, after, before = (x + 2) % RING, (x + 1) % RING, (x + 3) % RING
 
     def times(q, right):
         return jnp.dot(g_full[q, group_rows], right, preferred_element_type=f32)
 
     def open_a(buf, right, slots):
-        buf[far] = times(far, right()).astype(jnp.bfloat16)
+        buf[farthest] = times(farthest, right()).astype(jnp.bfloat16)
         state = reduce_start("col", buf, slots, Z_A)
         buf[after] = times(after, right()).astype(jnp.bfloat16)
         buf[before] = times(before, right()).astype(jnp.bfloat16)
@@ -632,9 +645,8 @@
     return pl.pallas_call(
         flatten_kernel,
         out_shape=jax.ShapeDtypeStruct((1, FLAT_ROWS * LANES), bf),
-        grid=(4,),
-        in_specs=[pl.BlockSpec((FLAT_ROWS // 4, LANES), lambda i: (i, 0))],
-        out_specs=pl.BlockSpec((1, FLAT_ROWS // 4 * LANES), lambda i: (0, i)),
+        in_specs=[pl.BlockSpec(memory_space=pltpu.VMEM)],
+        out_specs=pl.BlockSpec(memory_space=pltpu.VMEM),
         compiler_params=pltpu.CompilerParams(vmem_limit_bytes=56 * 1024 * 1024),
     )(value)
 

time: 131 us -> 132 us (level)
    pallas_call x1, Pallas kernels: 127 us -> 129 us  [newton_schulz(): pl.pallas_call(core_kernel, out_shape=jax.ShapeDtypeStruct((FLAT_ROWS, LA...]
where the time goes in v11:
time: 132 us
  Pallas kernels  131 us (99%)
    pallas_call x1, Pallas kernels, newton_schulz(): pl.pallas_call(core_kernel, out_shape=jax.ShapeDtypeStruct((FLAT_ROWS, LA...  129 us
    pallas_call x1, Pallas kernels, newton_schulz(): pl.pallas_call(flatten_kernel, out_shape=jax.ShapeDtypeStruct((1, FLAT_RO...  2.81 us

profile of v11, /device:TPU:1, one launch (start us, length us, event | category | flops | bytes accessed | tf_op | source)
XLA Modules:
  0.0 131.5 jit_solution(14999869782641409425)
XLA Ops:
  0.0 128.7 %shard_map.28.value_ref = f32[2112,128]{1,0:T(8,128)} custom-call(s32[16,16]{1,0:T(8,128)} %lengths_ref.1, bf16[1,270336]{1,0:T(2,128)(2,1)} %flat_ref.1), custom_call_target="tpu_custom_call" | custom-call | tf_op jit(solution)/shard_map/pallas_call | solution.py:595
  128.7 2.8 %shard_map.29 = bf16[1,270336]{1,0:T(2,128)(2,1)} custom-call(f32[2112,128]{1,0:T(8,128)} %shard_map.28.value_ref), custom_call_target="tpu_custom_call" | custom-call | tf_op jit(solution)/shard_map/pallas_call | solution.py:645

commit v12 on v11

--- a/solution.py
+++ b/solution.py
@@ -392,11 +392,11 @@
         relay(*up_part, dev_sib, G_SIB, sib_slots[4 if k == 8 else -back_by])
         if k >= 2:
             relay(*down_part, dev_sib, G_SIB, sib_slots[back_by])
+        for shift in {3: (0,), 6: (-1, 1)}.get(k, ()):
+            add_up(shift)
         for shift in {1: (0,), 3: (-1, 1), 5: (-2, 2), 7: (-3, 3), 8: (4,)}.get(k, ()):
             multiply(shift)
-        for shift in {3: (0,), 6: (-1, 1), 7: (-2, 2)}.get(k, ()):
-            add_up(shift)
-    for shift in (-3, 3, 4):
+    for shift in (-2, 2, -3, 3, 4):
         add_up(shift)
 
     def reduce_start(axis, buf, slots, group):

time: 132 us -> 129 us (0.977)
  Pallas kernels: 131 us -> 129 us
    pallas_call x1, Pallas kernels: 129 us -> 126 us  [newton_schulz(): pl.pallas_call(core_kernel, out_shape=jax.ShapeDtypeStruct((FLAT_ROWS, LA...]
where the time goes in v12:
time: 129 us
  Pallas kernels  129 us (100%)
    pallas_call x1, Pallas kernels, newton_schulz(): pl.pallas_call(core_kernel, out_shape=jax.ShapeDtypeStruct((FLAT_ROWS, LA...  126 us
    pallas_call x1, Pallas kernels, newton_schulz(): pl.pallas_call(flatten_kernel, out_shape=jax.ShapeDtypeStruct((1, FLAT_RO...  2.81 us

profile of v12, /device:TPU:1, one launch (start us, length us, event | category | flops | bytes accessed | tf_op | source)
XLA Modules:
  0.0 128.9 jit_solution(3294985129280838087)
XLA Ops:
  0.0 126.1 %shard_map.28.value_ref = f32[2112,128]{1,0:T(8,128)} custom-call(s32[16,16]{1,0:T(8,128)} %lengths_ref.1, bf16[1,270336]{1,0:T(2,128)(2,1)} %flat_ref.1), custom_call_target="tpu_custom_call" | custom-call | tf_op jit(solution)/shard_map/pallas_call | solution.py:595
  126.1 2.8 %shard_map.29 = bf16[1,270336]{1,0:T(2,128)(2,1)} custom-call(f32[2112,128]{1,0:T(8,128)} %shard_map.28.value_ref), custom_call_target="tpu_custom_call" | custom-call | tf_op jit(solution)/shard_map/pallas_call | solution.py:645
